TPU v7x, 256 devices: a whole 4x4x8 slice. The times are simulated.
256 devices in a mesh: gx: 32 (over x, y, core), gy: 8 (over z).
Axes of the slice: x: 4, y: 4, z: 8, core: 2. Of those that a mesh axis runs over, the one named last changes fastest.
Arguments:
- value: float32 [8, 2048, 8192], P(None, 'gx', 'gy'), may hold values from -6 to 6
- kernel_rows: float32 [511], replicated, may hold values from 0.0009784736 to 0.0029354207
- kernel_cols: float32 [511], replicated, may hold values from 0.0009784736 to 0.0029354207
- intensity: float32 [2], replicated, may hold values from 0.02 to 0.1
- diffusion: float32 [3], replicated, may hold values from 0.02 to 0.1
- drift: float32 [3], replicated, may hold values from -0.2 to 0.2
- cross: float32 [1], replicated, may hold values from -0.1 to 0.1
Outputs:
- updated: float32 [8, 2048, 8192], P(None, 'gx', 'gy')
- jump_rows: float32 [8, 2048, 8192], P(None, 'gx', 'gy')
- jump_cols: float32 [8, 2048, 8192], P(None, 'gx', 'gy')
All inputs are finite; a program needn't handle non-finite values.
Results may differ from a plain program's by a relative error of at most 0.00005.
Values sent between devices are 32-bit elements; how exact they have to be, the bound alone decides.
No kernel may reach another device: no remote copies, remote signals or barrier semaphores. Data moves between devices by JAX's collectives and lax.ppermute only.
A program may use at most 128 MiB of HBM per device.

v0:
```python
import jax
import jax.numpy as jnp
from jax import lax
from jax.sharding import PartitionSpec as P


def extended_2(block, sides, width):
    for axis, dim in sides:
        count = lax.axis_size(axis)
        forward = [(i, i + 1) for i in range(count - 1)]
        backward = [(target, source) for source, target in forward]
        low = lax.ppermute(
            lax.slice_in_dim(block, block.shape[dim] - width, None, axis=dim), axis, forward
        )
        high = lax.ppermute(lax.slice_in_dim(block, 0, width, axis=dim), axis, backward)
        block = jnp.concatenate([low, block, high], axis=dim)
    return block


def shifted(block, axis, distance):
    devices = range(lax.axis_size(axis))
    route = [(i - distance, i) for i in devices if i - distance in devices]
    return lax.ppermute(block, axis, route)


def toeplitz(weights, out_len):
    span = out_len + weights.shape[0] - 1
    extended = jnp.concatenate([weights, jnp.zeros((span - weights.shape[0] + 1,), weights.dtype)])
    flattened = jnp.tile(extended, out_len)[: out_len * span]
    return flattened.reshape(out_len, span)


def banded(padded, weights, radius, along):
    length = padded.shape[along] - 2 * radius
    block_len = min(512, length)
    block_count = length // block_len
    matrix = toeplitz(weights, block_len)
    pattern = "pac,ba->pbc" if along == 1 else "pra,ba->prb"

    def one_block(block_id):
        window = lax.dynamic_slice_in_dim(
            padded, block_id * block_len, block_len + 2 * radius, along
        )
        return jnp.einsum(pattern, window, matrix, precision=lax.Precision.HIGHEST)

    stacked = lax.map(one_block, jnp.arange(block_count, dtype=jnp.int32))
    if along == 1:
        return jnp.transpose(stacked, (1, 0, 2, 3)).reshape(
            stacked.shape[1], length, stacked.shape[3]
        )
    return jnp.transpose(stacked, (1, 2, 0, 3)).reshape(stacked.shape[1], stacked.shape[2], length)


def stencil(framed, diffusion, drift, cross):
    center = framed[1:-1, 1:-1, 1:-1]
    pairs = [
        (framed[1:-1, 2:, 1:-1], framed[1:-1, :-2, 1:-1]),
        (framed[1:-1, 1:-1, 2:], framed[1:-1, 1:-1, :-2]),
        (framed[2:, 1:-1, 1:-1], framed[:-2, 1:-1, 1:-1]),
    ]
    total = jnp.zeros_like(center)
    for axis_id in range(3):
        higher, lower = pairs[axis_id]
        total = total + diffusion[axis_id] * (higher - 2.0 * center + lower)
        total = total + drift[axis_id] * (higher - lower) * 0.5
    mixed = (
        framed[1:-1, 2:, 2:]
        - framed[1:-1, 2:, :-2]
        - framed[1:-1, :-2, 2:]
        + framed[1:-1, :-2, :-2]
    )
    return total + cross[0] * mixed * 0.25


def shards(value, kernel_rows, kernel_cols, intensity, diffusion, drift, cross):
    radius = (kernel_rows.shape[0] - 1) // 2
    plane_count, row_count, col_count = value.shape
    framed = extended_2(value, (("gx", 1), ("gy", 2)), 1)
    framed = jnp.pad(framed, ((1, 1), (0, 0), (0, 0)))
    tails = extended_2(value, (("gy", 2),), radius)
    jump_cols = banded(tails, kernel_cols, radius, 2) - jnp.sum(kernel_cols) * value
    reach_blocks = -(-radius // row_count)
    hop_count = min(reach_blocks, lax.axis_size("gx") - 1)
    above = []
    below = []
    offsets = list(range(1, hop_count + 1)) + [-step for step in range(1, hop_count + 1)]
    for offset in offsets:
        distance = abs(offset)
        if offset > 0:
            piece = value[:, max(0, distance * row_count - radius) :, :]
        else:
            piece = value[:, : min(row_count, radius - (distance - 1) * row_count), :]
        moved = shifted(piece, "gx", offset)
        if offset > 0:
            above.append(moved)
        else:
            below.append(moved)
    column = jnp.concatenate(above[::-1] + [value] + below, axis=1)
    row_sum = banded(column, kernel_rows, radius, 1)
    jump_rows = row_sum - jnp.sum(kernel_rows) * value
    updated = (
        value
        + stencil(framed, diffusion, drift, cross)
        + intensity[0] * jump_rows
        + intensity[1] * jump_cols
    )
    return (updated, jump_rows, jump_cols)


def solution(mesh):
    return jax.shard_map(
        shards,
        mesh=mesh,
        in_specs=(P(None, "gx", "gy"), P(), P(), P(), P(), P(), P()),
        out_specs=(P(None, "gx", "gy"), P(None, "gx", "gy"), P(None, "gx", "gy")),
        check_vma=False,
    )
```

profile of v0, /device:TPU:99, one launch (start us, length us, event | category | flops | bytes accessed | tf_op | source)
XLA Modules:
  0.0 406.7 jit_solution(4207265051686552483)
XLA Ops:
  0.6 2.6 collective-permute-start.8
  3.2 2.9 fusion.25
  6.1 1.2 copy.16
  7.3 0.0 copy-start
  7.4 5.0 %collective-permute-start.4 = (f32[8,63,1024]{2,0,1:T(8,128)S(1)}, f32[8,63,1024]{2,0,1:T(8,128)S(1)}, u32[]{:S(2)}, u32[]{:S(2)}) collective-permute-start(f32[8,63,1024]{2,0,1:T(8,128)S(1)} %copy.16), channel_id=1, source_target_pairs={{0,32},{8,40},{16,48},{24,56},{32,64},{40,72},{48,80},{56,88},{64,... | collective-permute-start | bytes 6193160 | tf_op jit(solution)/shard_map/ppermute | solution.py:23
  12.3 1.2 copy.17
  13.5 2.9 collective-permute-start.11
  16.4 0.1 fusion.26
  16.5 3.7 collective-permute-start.1
  20.1 3.2 collective-permute-start
  23.3 78.3 %collective-permute-done.1 = f32[8,1,1024]{2,1,0:T(1,128)S(1)} collective-permute-done((f32[8,1,1024]{2,1,0:T(1,128)S(1)}, f32[8,1,1024]{2,1,0:T(1,128)S(1)}, u32[]{:S(2)}, u32[]{:S(2)}) %collective-permute-start.1) | collective-permute-done | bytes 32800 | tf_op jit(solution)/shard_map/ppermute | solution.py:12
  101.6 29.4 %collective-permute-done = f32[8,1,1024]{2,1,0:T(1,128)S(1)} collective-permute-done((f32[8,1,1024]{2,1,0:T(1,128)S(1)}, f32[8,1,1024]{2,1,0:T(1,128)S(1)}, u32[]{:S(2)}, u32[]{:S(2)}) %collective-permute-start) | collective-permute-done | bytes 32800 | tf_op jit(solution)/shard_map/ppermute | solution.py:15
  131.1 0.3 pad_maximum_fusion.1
  131.4 0.3 copy-done.8
  131.7 0.2 fusion.23
  131.8 1.9 collective-permute-start.2
  133.7 4.8 %collective-permute-start.3 = (f32[8,66,1]{2,1,0:T(8,128)S(1)}, f32[8,66,1]{2,1,0:T(8,128)S(1)}, u32[]{:S(2)}, u32[]{:S(2)}) collective-permute-start(f32[8,66,1]{2,1,0:T(8,128)S(1)} %get-tuple-element.56), channel_id=1, source_target_pairs={{0,1},{1,2},{2,3},{3,4},{4,5},{5,6},{6,7},{8,9},{9,10},{10,11},{11... | collective-permute-start | bytes 6344 | tf_op jit(solution)/shard_map/ppermute | solution.py:12
  138.5 0.2 fusion.24
  138.7 2.0 collective-permute-done.2
  140.7 1.9 collective-permute-start.13
  142.6 0.0 collective-permute-done.3
  142.6 4.6 %collective-permute-start.12 = (f32[8,64,255]{2,1,0:T(8,128)S(1)}, f32[8,64,255]{2,1,0:T(8,128)S(1)}, u32[]{:S(2)}, u32[]{:S(2)}) collective-permute-start(f32[8,64,255]{2,1,0:T(8,128)S(1)} %get-tuple-element.60), channel_id=1, source_target_pairs={{0,1},{1,2},{2,3},{3,4},{4,5},{5,6},{6,7},{8,9},{9,10},{10,11},{11... | collective-permute-start | bytes 1566728 | tf_op jit(solution)/shard_map/ppermute | solution.py:12
  147.2 4.6 %collective-permute-done.13 = f32[8,64,255]{2,1,0:T(8,128)S(1)} collective-permute-done((f32[8,64,255]{2,1,0:T(8,128)S(1)}, f32[8,64,255]{2,1,0:T(8,128)S(1)}, u32[]{:S(2)}, u32[]{:S(2)}) %collective-permute-start.13) | collective-permute-done | bytes 522272 | tf_op jit(solution)/shard_map/ppermute | solution.py:15
  151.8 3.9 collective-permute-start.7
  155.7 0.0 collective-permute-done.12
  155.7 1.9 collective-permute-start.6
  157.6 0.0 collective-permute-done.4
  157.6 1.9 collective-permute-start.5
  159.6 0.0 collective-permute-done.11
  159.6 5.8 %collective-permute-start.10 = (f32[8,64,1024]{2,1,0:T(8,128)S(1)}, f32[8,64,1024]{2,1,0:T(8,128)}, u32[]{:S(2)}, u32[]{:S(2)}) collective-permute-start(f32[8,64,1024]{2,1,0:T(8,128)S(1)} %copy-done), channel_id=1, source_target_pairs={{24,0},{32,8},{40,16},{48,24},{56,32},{64,40},{72,48},{80,56},{88,... | collective-permute-start | bytes 6291464 | tf_op jit(solution)/shard_map/ppermute | solution.py:23
  165.4 0.0 collective-permute-done.8
  165.4 0.0 copy-done.7
  165.4 1.3 copy-done.2
  166.7 3.4 collective-permute-start.9
  170.1 0.6 reduce_sum.18
  170.7 0.6 reduce_sum.19
  171.3 0.6 concatenate.43
  172.6 0.2 tile.9
  172.8 0.2 reshape.24
  173.0 2.3 tile.20
  175.3 4.2 %tile.21 = f32[523776]{0:T(1024)} reshape(f32[512,1023]{1,0:T(8,128)} %tile.20) | data formatting | bytes 4190208 | tf_op jit(solution)/shard_map/tile | solution.py:29
  179.5 3.1 slice.142
  182.6 4.5 %reshape.21 = f32[512,1022]{1,0:T(8,128)} reshape(f32[523264]{0:T(1024)} %slice.142) | data formatting | bytes 4186112 | tf_op jit(solution)/shard_map/reshape | solution.py:30
  187.1 0.6 fusion.29
  187.7 0.7 fusion.27
  188.4 0.6 fusion.28
  189.0 4.4 %concatenate.39 = f32[8,66,1026]{2,1,0:T(8,128)} concatenate(f32[8,66,1]{2,1,0:T(8,128)S(1)} %collective-permute-done.3, f32[8,66,1024]{2,1,0:T(8,128)} %copy-done.1, f32[8,66,1]{2,1,0:T(8,128)S(1)} %collective-permute-done.2), dimensions={2} | concatenate | bytes 4333824 | tf_op jit(solution)/shard_map/concatenate | solution.py:16
  193.4 3.5 pad_maximum_fusion
  196.8 4.1 %concatenate.42 = f32[8,64,1534]{2,1,0:T(8,128)} concatenate(f32[8,64,255]{2,1,0:T(8,128)} %copy-done.7, f32[8,64,1024]{2,1,0:T(8,128)S(1)} %copy-done, f32[8,64,255]{2,1,0:T(8,128)S(1)} %collective-permute-done.13), dimensions={2} | concatenate | bytes 6283264 | tf_op jit(solution)/shard_map/concatenate | solution.py:16
  200.9 16.1 %while.2 = (s32[]{:T(128)}, f32[2,8,64,512]{3,2,1,0:T(8,128)}, s32[2]{0:T(128)S(1)}, f32[8,64,1534]{2,1,0:T(8,128)}, f32[512,1022]{1,0:T(8,128)}, /*index=5*/s32[]{:T(128)}, s32[1]{0:T(128)}, s32[]{:T(128)}, s32[]{:T(128)}) while((s32[]{:T(128)}, f32[2,8,64,512]{3,2,1,0:T(8,128)}, s32[2]{0:T(128)S(1)}, f32[8,64,1534]{2,1,0:T(8,128)}, ...), condition=%wide.region_2.3_spmd, body=%wide.region_1.2_spmd.sunk | while | flops 3214934016 | bytes 5243047 | solution.py:46
  200.9 0.6 dynamic_slice.21
  202.2 6.9 %fusion.37 = f32[2,8,64,512]{3,2,1,0:T(8,128)} fusion(f32[2,8,64,512]{3,2,1,0:T(8,128)} %get-tuple-element.115, s32[]{:T(128)S(6)} %copy.22, f32[512,1022]{1,0:T(8,128)} %get-tuple-element.127, f32[8,64,1534]{2,1,0:T(8,128)} %get-tuple-element.126, s32[]{:T(128)S(6)} %select_n.6), kind=kOutput, calls=%fused_computation.4.clone.1 | convolution fusion | flops 3214934016 | bytes 5242888 | tf_op jit(solution)/shard_map/while/body/eval_jaxpr/pra,ba->prb/dot_general | solution.py:44
  209.0 0.6 dynamic_slice.21
  210.3 6.8 %fusion.37 = f32[2,8,64,512]{3,2,1,0:T(8,128)} fusion(f32[2,8,64,512]{3,2,1,0:T(8,128)} %get-tuple-element.115, s32[]{:T(128)S(6)} %copy.22, f32[512,1022]{1,0:T(8,128)} %get-tuple-element.127, f32[8,64,1534]{2,1,0:T(8,128)} %get-tuple-element.126, s32[]{:T(128)S(6)} %select_n.6), kind=kOutput, calls=%fused_computation.4.clone.1 | convolution fusion | flops 3214934016 | bytes 5242888 | tf_op jit(solution)/shard_map/while/body/eval_jaxpr/pra,ba->prb/dot_general | solution.py:44
  217.1 3.3 copy.18
  220.4 2.5 copy.13
  222.9 2.5 copy.14
  225.4 0.0 collective-permute-done.7
  225.4 40.5 %collective-permute-done.6 = f32[8,64,1024]{2,1,0:T(8,128)} collective-permute-done((f32[8,64,1024]{2,1,0:T(8,128)S(1)}, f32[8,64,1024]{2,1,0:T(8,128)}, u32[]{:S(2)}, u32[]{:S(2)}) %collective-permute-start.6) | collective-permute-done | bytes 2097184 | tf_op jit(solution)/shard_map/ppermute | solution.py:23
  265.9 25.1 %collective-permute-done.5 = f32[8,64,1024]{2,1,0:T(8,128)} collective-permute-done((f32[8,64,1024]{2,1,0:T(8,128)S(1)}, f32[8,64,1024]{2,1,0:T(8,128)}, u32[]{:S(2)}, u32[]{:S(2)}) %collective-permute-start.5) | collective-permute-done | bytes 2097184 | tf_op jit(solution)/shard_map/ppermute | solution.py:23
  291.0 0.0 collective-permute-done.10
  291.0 3.0 collective-permute-done.9
  293.9 82.8 %concatenate.41 = f32[8,574,1024]{2,1,0:T(8,128)} concatenate(f32[8,63,1024]{2,1,0:T(8,128)} %copy.13, f32[8,64,1024]{2,1,0:T(8,128)} %collective-permute-done.5, f32[8,64,1024]{2,1,0:T(8,128)} %collective-permute-done.6, f32[8,64,1024]{2,1,0:T(8,128)} %collective-permute-done.7, f32[8,64,1024]{2,1,0:T(8,128)S(1)} %copy-done, f32[8,64,1024]{2,1,0:T(8,128)} %copy-done.2, ...), dimensions={1} | concatenate | bytes 37617664 | tf_op jit(solution)/shard_map/concatenate | solution.py:98
  376.8 29.8 %fusion.19 = (f32[8,64,1024]{2,1,0:T(8,128)}, f32[8,64,1024]{2,1,0:T(8,128)}, f32[8,64,1024]{2,1,0:T(8,128)}) fusion(f32[8,64,1024]{2,1,0:T(8,128)S(1)} %copy-done, f32[8,66,1025]{2,1,0:T(8,128)} %get-tuple-element.58, f32[8,66,1025]{2,1,0:T(8,128)} %get-tuple-element.57, f32[8,66,1026]{2,1,0:T(8,128)} %concatenate.39, f32[8,1,1024]{2,1,0:T(1,128)S(1)} %copy-done.9, ...), kind=kOutput, calls=%fused_computation.17 | convolution fusion | flops 3632791552 | bytes 44256940 | tf_op jit(solution)/shard_map/while/body/eval_jaxpr/pac,ba->pbc/dot_general | solution.py:44
  (30 shorter events, 0.1 us)
Async XLA Ops:
  0.6 164.7 %collective-permute-start.8 = (f32[8,64,1024]{2,1,0:T(8,128)}, f32[8,64,1024]{2,1,0:T(8,128)S(1)}, u32[]{:S(2)}, u32[]{:S(2)}) collective-permute-start(f32[8,64,1024]{2,1,0:T(8,128)} %param.9), channel_id=1, source_target_pairs={{8,0},{16,8},{24,16},{32,24},{40,32},{48,40},{56,48},{64,56},{72,6... | collective-permute-start | bytes 6291464 | tf_op jit(solution)/shard_map/ppermute | solution.py:23
  7.3 9.1 %copy-start = (f32[8,64,1024]{2,1,0:T(8,128)S(1)}, f32[8,64,1024]{2,1,0:T(8,128)}, u32[]{:S(2)}) copy-start(f32[8,64,1024]{2,1,0:T(8,128)} %param.9) | copy-start | bytes 6291460
  7.4 150.3 %collective-permute-start.4 = (f32[8,63,1024]{2,0,1:T(8,128)S(1)}, f32[8,63,1024]{2,0,1:T(8,128)S(1)}, u32[]{:S(2)}, u32[]{:S(2)}) collective-permute-start(f32[8,63,1024]{2,0,1:T(8,128)S(1)} %copy.16), channel_id=1, source_target_pairs={{0,32},{8,40},{16,48},{24,56},{32,64},{40,72},{48,80},{56,88},{64,... | collective-permute-start | bytes 6193160 | tf_op jit(solution)/shard_map/ppermute | solution.py:23
  13.5 146.0 %collective-permute-start.11 = (f32[8,63,1024]{2,0,1:T(8,128)S(1)}, f32[8,63,1024]{2,0,1:T(8,128)S(1)}, u32[]{:S(2)}, u32[]{:S(2)}) collective-permute-start(f32[8,63,1024]{2,0,1:T(8,128)S(1)} %copy.17), channel_id=1, source_target_pairs={{32,0},{40,8},{48,16},{56,24},{64,32},{72,40},{80,48},{88,56},{96,... | collective-permute-start | bytes 6193160 | tf_op jit(solution)/shard_map/ppermute | solution.py:23
  16.5 85.2 %collective-permute-start.1 = (f32[8,1,1024]{2,1,0:T(1,128)S(1)}, f32[8,1,1024]{2,1,0:T(1,128)S(1)}, u32[]{:S(2)}, u32[]{:S(2)}) collective-permute-start(f32[8,1,1024]{2,1,0:T(1,128)S(1)} %get-tuple-element.63), channel_id=1, source_target_pairs={{0,8},{8,16},{16,24},{24,32},{32,40},{40,48},{48,56},{56,64},{64,7... | collective-permute-start | bytes 98312 | tf_op jit(solution)/shard_map/ppermute | solution.py:12
  20.1 110.9 %collective-permute-start = (f32[8,1,1024]{2,1,0:T(1,128)S(1)}, f32[8,1,1024]{2,1,0:T(1,128)S(1)}, u32[]{:S(2)}, u32[]{:S(2)}) collective-permute-start(f32[8,1,1024]{2,1,0:T(1,128)S(1)} %get-tuple-element.64), channel_id=1, source_target_pairs={{8,0},{16,8},{24,16},{32,24},{40,32},{48,40},{56,48},{64,56},{72,6... | collective-permute-start | bytes 98312 | tf_op jit(solution)/shard_map/ppermute | solution.py:15
  131.1 0.6 copy-start.8
  131.7 33.7 %copy-start.1 = (f32[8,66,1024]{2,1,0:T(8,128)}, f32[8,66,1024]{2,1,0:T(8,128)S(1)}, u32[]{:S(2)}) copy-start(f32[8,66,1024]{2,1,0:T(8,128)S(1)} %pad_maximum_fusion.1) | copy-start | bytes 6488068
  131.7 38.4 %copy-start.10 = (f32[511]{0:T(512)S(1)}, f32[511]{0:T(512)}, u32[]{:S(2)}) copy-start(f32[511]{0:T(512)} %param.10) | copy-start | bytes 6136
  131.7 39.1 %copy-start.11 = (f32[511]{0:T(512)S(1)}, f32[511]{0:T(512)}, u32[]{:S(2)}) copy-start(f32[511]{0:T(512)} %param.11) | copy-start | bytes 6136
  131.8 8.9 %collective-permute-start.2 = (f32[8,66,1]{2,1,0:T(8,128)S(1)}, f32[8,66,1]{2,1,0:T(8,128)S(1)}, u32[]{:S(2)}, u32[]{:S(2)}) collective-permute-start(f32[8,66,1]{2,1,0:T(8,128)S(1)} %get-tuple-element.55), channel_id=1, source_target_pairs={{1,0},{2,1},{3,2},{4,3},{5,4},{6,5},{7,6},{9,8},{10,9},{11,10},{12... | collective-permute-start | bytes 6344 | tf_op jit(solution)/shard_map/ppermute | solution.py:15
  133.7 8.9 %collective-permute-start.3 = (f32[8,66,1]{2,1,0:T(8,128)S(1)}, f32[8,66,1]{2,1,0:T(8,128)S(1)}, u32[]{:S(2)}, u32[]{:S(2)}) collective-permute-start(f32[8,66,1]{2,1,0:T(8,128)S(1)} %get-tuple-element.56), channel_id=1, source_target_pairs={{0,1},{1,2},{2,3},{3,4},{4,5},{5,6},{6,7},{8,9},{9,10},{10,11},{11... | collective-permute-start | bytes 6344 | tf_op jit(solution)/shard_map/ppermute | solution.py:12
  140.7 11.1 %collective-permute-start.13 = (f32[8,64,255]{2,1,0:T(8,128)S(1)}, f32[8,64,255]{2,1,0:T(8,128)S(1)}, u32[]{:S(2)}, u32[]{:S(2)}) collective-permute-start(f32[8,64,255]{2,1,0:T(8,128)S(1)} %get-tuple-element.59), channel_id=1, source_target_pairs={{1,0},{2,1},{3,2},{4,3},{5,4},{6,5},{7,6},{9,8},{10,9},{11,10},{12... | collective-permute-start | bytes 1566728 | tf_op jit(solution)/shard_map/ppermute | solution.py:15
  142.6 13.1 %collective-permute-start.12 = (f32[8,64,255]{2,1,0:T(8,128)S(1)}, f32[8,64,255]{2,1,0:T(8,128)S(1)}, u32[]{:S(2)}, u32[]{:S(2)}) collective-permute-start(f32[8,64,255]{2,1,0:T(8,128)S(1)} %get-tuple-element.60), channel_id=1, source_target_pairs={{0,1},{1,2},{2,3},{3,4},{4,5},{5,6},{6,7},{8,9},{9,10},{10,11},{11... | collective-permute-start | bytes 1566728 | tf_op jit(solution)/shard_map/ppermute | solution.py:12
  151.8 73.6 %collective-permute-start.7 = (f32[8,64,1024]{2,1,0:T(8,128)S(1)}, f32[8,64,1024]{2,1,0:T(8,128)}, u32[]{:S(2)}, u32[]{:S(2)}) collective-permute-start(f32[8,64,1024]{2,1,0:T(8,128)S(1)} %copy-done), channel_id=1, source_target_pairs={{0,8},{8,16},{16,24},{24,32},{32,40},{40,48},{48,56},{56,64},{64,7... | collective-permute-start | bytes 6291464 | tf_op jit(solution)/shard_map/ppermute | solution.py:23
  155.7 9.7 %copy-start.7 = (f32[8,64,255]{2,1,0:T(8,128)}, f32[8,64,255]{2,1,0:T(8,128)S(1)}, u32[]{:S(2)}) copy-start(f32[8,64,255]{2,1,0:T(8,128)S(1)} %collective-permute-done.12) | copy-start | bytes 1566724
  155.7 110.2 %collective-permute-start.6 = (f32[8,64,1024]{2,1,0:T(8,128)S(1)}, f32[8,64,1024]{2,1,0:T(8,128)}, u32[]{:S(2)}, u32[]{:S(2)}) collective-permute-start(f32[8,64,1024]{2,1,0:T(8,128)S(1)} %copy-done), channel_id=1, source_target_pairs={{0,16},{8,24},{16,32},{24,40},{32,48},{40,56},{48,64},{56,72},{64,... | collective-permute-start | bytes 6291464 | tf_op jit(solution)/shard_map/ppermute | solution.py:23
  157.6 7.8 %copy-start.3 = (f32[8,63,1024]{2,0,1:T(8,128)}, f32[8,63,1024]{2,0,1:T(8,128)S(1)}, u32[]{:S(2)}) copy-start(f32[8,63,1024]{2,0,1:T(8,128)S(1)} %collective-permute-done.4) | copy-start | bytes 6193156
  157.6 133.3 %collective-permute-start.5 = (f32[8,64,1024]{2,1,0:T(8,128)S(1)}, f32[8,64,1024]{2,1,0:T(8,128)}, u32[]{:S(2)}, u32[]{:S(2)}) collective-permute-start(f32[8,64,1024]{2,1,0:T(8,128)S(1)} %copy-done), channel_id=1, source_target_pairs={{0,24},{8,32},{16,40},{24,48},{32,56},{40,64},{48,72},{56,80},{64,... | collective-permute-start | bytes 6291464 | tf_op jit(solution)/shard_map/ppermute | solution.py:23
  159.6 5.8 %copy-start.5 = (f32[8,63,1024]{2,0,1:T(8,128)}, f32[8,63,1024]{2,0,1:T(8,128)S(1)}, u32[]{:S(2)}) copy-start(f32[8,63,1024]{2,0,1:T(8,128)S(1)} %collective-permute-done.11) | copy-start | bytes 6193156
  159.6 131.4 %collective-permute-start.10 = (f32[8,64,1024]{2,1,0:T(8,128)S(1)}, f32[8,64,1024]{2,1,0:T(8,128)}, u32[]{:S(2)}, u32[]{:S(2)}) collective-permute-start(f32[8,64,1024]{2,1,0:T(8,128)S(1)} %copy-done), channel_id=1, source_target_pairs={{24,0},{32,8},{40,16},{48,24},{56,32},{64,40},{72,48},{80,56},{88,... | collective-permute-start | bytes 6291464 | tf_op jit(solution)/shard_map/ppermute | solution.py:23
  165.4 1.3 copy-start.2
  166.7 127.2 %collective-permute-start.9 = (f32[8,64,1024]{2,1,0:T(8,128)S(1)}, f32[8,64,1024]{2,1,0:T(8,128)}, u32[]{:S(2)}, u32[]{:S(2)}) collective-permute-start(f32[8,64,1024]{2,1,0:T(8,128)S(1)} %copy-done), channel_id=1, source_target_pairs={{16,0},{24,8},{32,16},{40,24},{48,32},{56,40},{64,48},{72,56},{80,... | collective-permute-start | bytes 6291464 | tf_op jit(solution)/shard_map/ppermute | solution.py:23
  182.6 4.5 %copy-start.14 = (f32[2]{0:T(128)S(1)}, f32[2]{0:T(128)}, u32[]{:S(2)}) copy-start(f32[2]{0:T(128)} %param.12) | copy-start | bytes 28
  182.6 5.1 %copy-start.12 = (f32[3]{0:T(128)S(1)}, f32[3]{0:T(128)}, u32[]{:S(2)}) copy-start(f32[3]{0:T(128)} %param.13) | copy-start | bytes 40
  182.6 5.8 %copy-start.13 = (f32[3]{0:T(128)S(1)}, f32[3]{0:T(128)}, u32[]{:S(2)}) copy-start(f32[3]{0:T(128)} %param.14) | copy-start | bytes 40
  188.9 4.4 %copy-start.9 = (f32[8,1,1024]{2,1,0:T(1,128)S(1)}, f32[8,1,1024]{2,1,0:T(1,128)}, u32[]{:S(2)}) copy-start(f32[8,1,1024]{2,1,0:T(1,128)} %copy-done.8) | copy-start | bytes 98308
  217.1 3.3 copy-start.4
  220.4 2.5 copy-start.6
where the time goes:
time: 410 us; the launch traced here: 407 us
  waiting for transfers between devices  183 us (45%)
  local copies, waits for them, and re-layouts  125 us (30%)
  starting transfers between devices  47.2 us (12%)
  matrix products  43.5 us (11%)
  other arithmetic  5.06 us (1%)
    concatenate x1, local copies, waits for them, and re-layouts, shards(): column = jnp.concatenate(above[::-1] + [value] + below, axis=1)  82.8 us
    ppermute x3, waiting for transfers between devices, extended_2(): lax.ppermute(lax.slice_in_dim(block, block.shape[dim] - width, None, axis...  78.3 us
    ppermute x8, waiting for transfers between devices, shifted(): return lax.ppermute(block, axis, route)  68.5 us
    dot_general x3, matrix products, one_block(): return jnp.einsum(pattern, window, matrix, precision=lax.Precision.HIGHEST)  43.5 us
    ppermute x3, waiting for transfers between devices, extended_2(): lax.ppermute(lax.slice_in_dim(block, 0, width, axis=dim), axis, backward)  36 us
    ppermute x8, starting transfers between devices, shifted(): return lax.ppermute(block, axis, route)  27.2 us
    ppermute x3, starting transfers between devices, extended_2(): lax.ppermute(lax.slice_in_dim(block, block.shape[dim] - width, None, axis...  13 us
    concatenate x2, local copies, waits for them, and re-layouts, extended_2(): block = jnp.concatenate([low, block, high], axis=dim)  8.48 us
  transfers between devices with their start and end apart: 14, of which 7 were waited for; matrix products, arithmetic and copies ran while one was open for 15% of the time, Pallas kernels for 0%

commit v1 on v0

v1 whole, which is shorter than its diff:
```python
import jax
import jax.numpy as jnp
from jax import lax
from jax.experimental import pallas as pl
from jax.experimental.pallas import tpu as pltpu
from jax.sharding import PartitionSpec as P

BLOCK = 256
WINDOW = 3 * BLOCK
VMEM_LIMIT = 48 * 1024 * 1024


def split(x):
    high = x.astype(jnp.bfloat16)
    return high, (x - high.astype(jnp.float32)).astype(jnp.bfloat16)


def band(weights_ref):
    wide = jnp.broadcast_to(weights_ref[...], (BLOCK, WINDOW))
    return split(pltpu.roll(wide, 1, 1, stride=1, stride_axis=0))


def product(a, b, contract):
    dims = (contract, ((), ()))
    return (
        lax.dot_general(a[0], b[0], dims, preferred_element_type=jnp.float32)
        + lax.dot_general(a[0], b[1], dims, preferred_element_type=jnp.float32)
        + lax.dot_general(a[1], b[0], dims, preferred_element_type=jnp.float32)
    )


def local_kernel(coef, value, low, high, above, below, weights, jump_ref, part_ref, wide_hi, wide_lo):
    planes, rows, cols = value.shape
    for source, start in ((low, 0), (value, BLOCK), (high, BLOCK + cols)):
        hi, lo = split(source[...].reshape(planes * rows, source.shape[2]))
        wide_hi[:, start : start + source.shape[2]] = hi
        wide_lo[:, start : start + source.shape[2]] = lo
    taps = band(weights)
    total = coef[0]
    for start in range(0, cols, BLOCK):
        window = pl.ds(start, WINDOW)
        sums = product((wide_hi[:, window], wide_lo[:, window]), taps, ((1,), (1,)))
        jump_ref[:, :, start : start + BLOCK] = (
            sums.reshape(planes, rows, BLOCK) - total * value[:, :, start : start + BLOCK]
        )
    intensity = coef[1]
    row_diff, row_drift = coef[2], coef[5] * 0.5
    col_diff, col_drift = coef[3], coef[6] * 0.5
    plane_diff, plane_drift = coef[4], coef[7] * 0.5
    mixed = coef[8] * 0.25
    lane = lax.broadcasted_iota(jnp.int32, (rows, cols), 1)
    line = lax.broadcasted_iota(jnp.int32, (rows, cols), 0)
    side = lane.shape[1] - 1

    def along(x, first, last):
        right = jnp.where(lane[: x.shape[0]] == side, last, pltpu.roll(x, side, 1))
        left = jnp.where(lane[: x.shape[0]] == 0, first, pltpu.roll(x, 1, 1))
        return right, left

    edges = []
    for edge in (above, below):
        middle = edge[:, 128 : 128 + cols]
        lanes8 = lax.broadcasted_iota(jnp.int32, middle.shape, 1)
        right = jnp.where(lanes8 == side, edge[:, 128 + cols : 129 + cols], pltpu.roll(middle, side, 1))
        left = jnp.where(lanes8 == 0, edge[:, 127:128], pltpu.roll(middle, 1, 1))
        edges.append((middle, right - left))
    above_term = (row_diff - row_drift) * edges[0][0] - mixed * edges[0][1]
    below_term = (row_diff + row_drift) * edges[1][0] + mixed * edges[1][1]
    for p in range(planes):
        x = value[p]
        right, left = along(x, low[p, :, BLOCK - 1 : BLOCK], high[p, :, 0:1])
        slope = right - left
        out = x + col_diff * (right - 2.0 * x + left) + col_drift * slope
        down = (row_diff + row_drift) * x + mixed * slope
        up = (row_diff - row_drift) * x - mixed * slope
        down = jnp.where(line == rows - 1, below_term[p : p + 1], pltpu.roll(down, rows - 1, 0))
        up = jnp.where(line == 0, above_term[p : p + 1], pltpu.roll(up, 1, 0))
        out = out + (down - 2.0 * row_diff * x + up)
        out = out - 2.0 * plane_diff * x
        if p + 1 < planes:
            out = out + (plane_diff + plane_drift) * value[p + 1]
        if p > 0:
            out = out + (plane_diff - plane_drift) * value[p - 1]
        part_ref[p] = out + intensity * jump_ref[p]


def local_part(coef, value, low, high, above, below, weights):
    planes, rows, cols = value.shape
    vmem = pl.BlockSpec(memory_space=pltpu.VMEM)
    shape = jax.ShapeDtypeStruct(value.shape, jnp.float32)
    wide = pltpu.VMEM((planes * rows, cols + 2 * BLOCK), jnp.bfloat16)
    return pl.pallas_call(
        local_kernel,
        out_shape=(shape, shape),
        in_specs=[pl.BlockSpec(memory_space=pltpu.SMEM)] + [vmem] * 6,
        out_specs=(vmem, vmem),
        scratch_shapes=[wide, wide],
        compiler_params=pltpu.CompilerParams(vmem_limit_bytes=VMEM_LIMIT),
        cost_estimate=pl.CostEstimate(
            flops=6 * planes * rows * cols * WINDOW, bytes_accessed=16 * planes * rows * cols, transcendentals=0
        ),
        name="columns_and_stencil",
    )(coef, value, low, high, above, below, weights)


def rows_kernel(coef, column, weights, out_ref, tall_hi, tall_lo):
    rows, cols = column.shape
    zeros = jnp.zeros((BLOCK, cols), jnp.bfloat16)
    for tall in (tall_hi, tall_lo):
        tall[:BLOCK] = zeros
        tall[BLOCK + rows :] = zeros
    hi, lo = split(column[...])
    tall_hi[BLOCK : BLOCK + rows] = hi
    tall_lo[BLOCK : BLOCK + rows] = lo
    taps = band(weights)
    for start in range(0, rows, BLOCK):
        window = pl.ds(start, WINDOW)
        sums = product(taps, (tall_hi[window], tall_lo[window]), ((1,), (0,)))
        out_ref[start : start + BLOCK] = sums - coef[0] * column[start : start + BLOCK]


def rows_part(coef, column, weights):
    rows, cols = column.shape
    vmem = pl.BlockSpec(memory_space=pltpu.VMEM)
    tall = pltpu.VMEM((rows + 2 * BLOCK, cols), jnp.bfloat16)
    return pl.pallas_call(
        rows_kernel,
        out_shape=jax.ShapeDtypeStruct(column.shape, jnp.float32),
        in_specs=[pl.BlockSpec(memory_space=pltpu.SMEM), vmem, vmem],
        out_specs=vmem,
        scratch_shapes=[tall, tall],
        compiler_params=pltpu.CompilerParams(vmem_limit_bytes=VMEM_LIMIT),
        cost_estimate=pl.CostEstimate(
            flops=6 * rows * cols * WINDOW, bytes_accessed=8 * rows * cols, transcendentals=0
        ),
        name="rows",
    )(coef, column, weights)


def neighbours(low_side, high_side, axis):
    count = lax.axis_size(axis)
    forward = [(i, i + 1) for i in range(count - 1)]
    backward = [(i + 1, i) for i in range(count - 1)]
    return lax.ppermute(high_side, axis, forward), lax.ppermute(low_side, axis, backward)


def shards(value, kernel_rows, kernel_cols, intensity, diffusion, drift, cross):
    planes, rows, cols = value.shape
    devices = lax.axis_size("gx")
    groups = devices // planes
    width = cols // groups
    wide_rows = jnp.pad(kernel_rows, (0, WINDOW - kernel_rows.shape[0]))[None]
    wide_cols = jnp.pad(kernel_cols, (0, WINDOW - kernel_cols.shape[0]))[None]
    coef = jnp.concatenate([jnp.sum(kernel_cols)[None], intensity[1:2], diffusion, drift, cross])
    row_coef = jnp.sum(kernel_rows)[None]

    pieces = value.reshape(planes, rows, groups, width).transpose(0, 2, 1, 3)
    pieces = pieces.reshape(devices, rows, width)
    column = lax.all_to_all(pieces, "gx", 0, 0, tiled=True).reshape(devices * rows, width)

    low, high = neighbours(value[:, :, :BLOCK], value[:, :, cols - BLOCK :], "gy")

    def line(i):
        return jnp.concatenate([low[:, i, BLOCK - 128 :], value[:, i], high[:, i, :128]], axis=1)

    above, below = neighbours(line(0), line(rows - 1), "gx")
    jump_cols, part = local_part(coef, value, low, high, above, below, wide_cols)

    jump = rows_part(row_coef, column, wide_rows).reshape(devices, rows, width)
    back = lax.all_to_all(jump, "gx", 0, 0, tiled=True)
    jump_rows = back.reshape(planes, groups, rows, width).transpose(0, 2, 1, 3)
    jump_rows = jump_rows.reshape(planes, rows, cols)
    return part + intensity[0] * jump_rows, jump_rows, jump_cols


def solution(mesh):
    return jax.shard_map(
        shards,
        mesh=mesh,
        in_specs=(P(None, "gx", "gy"), P(), P(), P(), P(), P(), P()),
        out_specs=(P(None, "gx", "gy"), P(None, "gx", "gy"), P(None, "gx", "gy")),
        check_vma=False,
    )
```

time: 410 us -> 107 us (0.26)
  the two profiles are of different devices: /device:TPU:99 before, /device:TPU:102 now
where the time goes in v1:
time: 107 us; the launch traced here: 106 us
  waiting for transfers between devices  40.5 us (38%)
  starting transfers between devices  30 us (28%)
  local copies, waits for them, and re-layouts  19.8 us (19%)
  Pallas kernels  9.27 us (9%)
  other arithmetic  5.34 us (5%)
  between operations  1.52 us (1%)
    all_to_all x1, waiting for transfers between devices, shards(): lax.all_to_all(pieces, 'gx', 0, 0, tiled=True)  25.7 us
    ppermute x2, waiting for transfers between devices, neighbours(): lax.ppermute(high_side, axis, forward)  9.45 us
    ppermute x2, starting transfers between devices, neighbours(): lax.ppermute(low_side, axis, backward)  7.85 us
    all_to_all x1, starting transfers between devices, shards(): lax.all_to_all(pieces, 'gx', 0, 0, tiled=True)  7.74 us
    all_to_all x1, starting transfers between devices, shards(): back = lax.all_to_all(jump, 'gx', 0, 0, tiled=True)  7.44 us
    ppermute x2, starting transfers between devices, neighbours(): lax.ppermute(high_side, axis, forward)  6.96 us
    pallas_call x1, Pallas kernels, local_part(): pl.pallas_call(local_kernel, out_shape=(shape, shape), in_specs=[pl.Block...  5.94 us
    ppermute x2, waiting for transfers between devices, neighbours(): lax.ppermute(low_side, axis, backward)  5.33 us
  transfers between devices with their start and end apart: 6, of which 3 were waited for; matrix products, arithmetic and copies ran while one was open for 5% of the time, Pallas kernels for 6%

profile of v1, /device:TPU:102, one launch (start us, length us, event | category | flops | bytes accessed | tf_op | source)
XLA Modules:
  0.0 106.4 jit_solution(1182516306090464425)
XLA Ops:
  0.6 1.8 %fusion = (f32[8,64,256]{2,1,0:T(8,128)S(1)}, f32[8,64,256]{2,1,0:T(8,128)S(1)}, f32[8,64,256]{2,1,0:T(8,128)S(1)}, f32[8,64,256]{2,1,0:T(8,128)S(1)}) fusion(f32[8,64,1024]{2,1,0:T(8,128)} %value.1), kind=kLoop, calls=%fused_computation.11 | loop fusion | bytes 4194304 | tf_op jit(solution)/shard_map/slice.1
  2.4 0.3 copy.33
  2.7 0.3 copy.30
  3.0 0.3 copy.29
  3.3 0.3 copy.34
  3.6 0.1 pad_maximum_fusion
  3.8 2.0 %copy.27 = f32[8,256,256]{2,1,0:T(8,128)} copy(f32[8,256,256]{2,0,1:T(8,128)S(1)} %pad_maximum_fusion) | data formatting | bytes 4194304 | tf_op jit(solution)/shard_map/concatenate
  5.8 0.0 copy-start.6
  5.8 7.7 %all-to-all-start = ((f32[32,64,256]{2,1,0:T(8,128)}), f32[32,64,256]{2,1,0:T(8,128)S(1)}, u32[]{:S(2)}, u32[]{:S(2)}) async-start(f32[32,64,256]{2,1,0:T(8,128)} %bitcast.26), calls=%async_computation | async-start | bytes 4194304 | tf_op jit(solution)/shard_map/all_to_all | solution.py:159
  13.5 0.0 copy-done.6
  13.5 0.6 reduce_sum.19
  14.1 25.7 %all-to-all-done = f32[32,64,256]{2,1,0:T(8,128)S(1)} async-done(((f32[32,64,256]{2,1,0:T(8,128)}), f32[32,64,256]{2,1,0:T(8,128)S(1)}, u32[]{:S(2)}, u32[]{:S(2)}) %all-to-all-start) | async-done | bytes 2097184 | tf_op jit(solution)/shard_map/all_to_all | solution.py:159
  39.8 3.3 %rows.1 = f32[2048,256]{1,0:T(8,128)S(1)} custom-call(f32[1]{0:T(128)} %bitcast.8.coef, f32[2048,256]{1,0:T(8,128)S(1)} %bitcast.25, f32[1,768]{1,0:T(1,128)S(1)} %broadcast_in_dim.15.weights), custom_call_target="tpu_custom_call" | custom-call | flops 2415919104 | bytes 4194304 | tf_op jit(solution)/shard_map/rows/pallas_call | solution.py:126
  43.2 0.0 copy-start.3
  43.2 1.3 %copy-done.3 = f32[2048,256]{1,0:T(8,128)} copy-done((f32[2048,256]{1,0:T(8,128)}, f32[2048,256]{1,0:T(8,128)S(1)}, u32[]{:S(2)}) %copy-start.3) | copy-done | bytes 2097176
  44.5 0.0 copy-start
  44.5 0.0 copy-start.8
  44.5 0.0 copy-start.7
  44.5 0.0 copy-start.9
  44.5 0.0 copy-start.10
  44.5 7.4 %all-to-all-start.1 = ((f32[32,64,256]{2,1,0:T(8,128)}), f32[32,64,256]{2,1,0:T(8,128)}, u32[]{:S(2)}, u32[]{:S(2)}) async-start(f32[32,64,256]{2,1,0:T(8,128)} %bitcast.24), calls=%async_computation.1 | async-start | bytes 4194304 | tf_op jit(solution)/shard_map/all_to_all | solution.py:170
  52.0 5.0 %collective-permute-start = (f32[8,64,256]{2,0,1:T(8,128)S(1)}, f32[8,64,256]{2,0,1:T(8,128)S(1)}, u32[]{:S(2)}, u32[]{:S(2)}) collective-permute-start(f32[8,64,256]{2,0,1:T(8,128)S(1)} %copy.29), channel_id=1, source_target_pairs={{0,1},{1,2},{2,3},{3,4},{4,5},{5,6},{6,7},{8,9},{9,10},{10,11},{11... | collective-permute-start | bytes 1572872 | tf_op jit(solution)/shard_map/ppermute | solution.py:144
  57.0 1.9 %collective-permute-start.1 = (f32[8,64,256]{2,0,1:T(8,128)S(1)}, f32[8,64,256]{2,0,1:T(8,128)S(1)}, u32[]{:S(2)}, u32[]{:S(2)}) collective-permute-start(f32[8,64,256]{2,0,1:T(8,128)S(1)} %copy.30), channel_id=1, source_target_pairs={{1,0},{2,1},{3,2},{4,3},{5,4},{6,5},{7,6},{9,8},{10,9},{11,10},{12... | collective-permute-start | bytes 1572872 | tf_op jit(solution)/shard_map/ppermute | solution.py:144
  58.9 0.0 copy-done
  58.9 0.1 fusion.1
  59.0 9.4 %collective-permute-done = f32[8,64,256]{2,0,1:T(8,128)S(1)} collective-permute-done((f32[8,64,256]{2,0,1:T(8,128)S(1)}, f32[8,64,256]{2,0,1:T(8,128)S(1)}, u32[]{:S(2)}, u32[]{:S(2)}) %collective-permute-start) | collective-permute-done | bytes 524320 | tf_op jit(solution)/shard_map/ppermute | solution.py:144
  68.5 0.0 copy-start.4
  68.5 5.3 %collective-permute-done.1 = f32[8,64,256]{2,0,1:T(8,128)S(1)} collective-permute-done((f32[8,64,256]{2,0,1:T(8,128)S(1)}, f32[8,64,256]{2,0,1:T(8,128)S(1)}, u32[]{:S(2)}, u32[]{:S(2)}) %collective-permute-start.1) | collective-permute-done | bytes 524320 | tf_op jit(solution)/shard_map/ppermute | solution.py:144
  73.8 0.0 copy-start.5
  73.8 1.9 %collective-permute-start.2 = (f32[8,1280]{1,0:T(8,128)S(1)}, f32[8,1280]{1,0:T(8,128)S(1)}, u32[]{:S(2)}, u32[]{:S(2)}) collective-permute-start(f32[8,1280]{1,0:T(8,128)S(1)} %pad_maximum_fusion.1), channel_id=1, source_target_pairs={{0,8},{8,16},{16,24},{24,32},{32,40},{40,48},{48,56},{56,64},{64,7... | collective-permute-start | bytes 122888 | tf_op jit(solution)/shard_map/ppermute | solution.py:144
  75.7 0.0 copy-done.4
  75.8 0.0 copy-done.5
  75.8 5.9 %collective-permute-start.3 = (f32[8,1280]{1,0:T(8,128)S(1)}, f32[8,1280]{1,0:T(8,128)S(1)}, u32[]{:S(2)}, u32[]{:S(2)}) collective-permute-start(f32[8,1280]{1,0:T(8,128)S(1)} %pad_maximum_fusion.2), channel_id=1, source_target_pairs={{8,0},{16,8},{24,16},{32,24},{40,32},{48,40},{56,48},{64,56},{72,6... | collective-permute-start | bytes 122888 | tf_op jit(solution)/shard_map/ppermute | solution.py:144
  81.7 0.0 copy-done.8
  81.7 0.7 fusion.2
  82.4 0.0 copy-done.7
  82.4 0.6 reduce_sum.18
  83.6 0.0 copy-done.9
  83.7 0.0 copy-done.10
  83.7 1.3 %concatenate.12.coef = f32[9]{0:T(128)S(1)} concatenate(f32[1]{0:T(128)} %bitcast, f32[1]{0:T(128)} %get-tuple-element.18, f32[3]{0:T(128)S(1)} %copy-done.9, f32[3]{0:T(128)S(1)} %copy-done.10, f32[1]{0:T(128)S(6)} %copy.41), dimensions={0} | concatenate | bytes 72 | tf_op jit(solution)/shard_map/concatenate | solution.py:154
  85.0 1.2 %copy.23.low = f32[8,64,256]{2,1,0:T(8,128)S(1)} copy(f32[8,64,256]{2,0,1:T(8,128)} %copy-done.4) | data formatting | bytes 1048576 | tf_op jit(solution)/shard_map/ppermute | solution.py:144
  86.2 1.2 %copy.24.high = f32[8,64,256]{2,1,0:T(8,128)S(1)} copy(f32[8,64,256]{2,0,1:T(8,128)} %copy-done.5) | data formatting | bytes 1048576 | tf_op jit(solution)/shard_map/ppermute | solution.py:144
  87.4 0.0 collective-permute-done.2.above
  87.4 0.0 collective-permute-done.3.below
  87.4 5.9 %columns_and_stencil.1 = (f32[8,64,1024]{2,1,0:T(8,128)}, f32[8,64,1024]{2,1,0:T(8,128)S(1)}) custom-call(f32[9]{0:T(128)S(1)} %concatenate.12.coef, f32[8,64,1024]{2,1,0:T(8,128)S(1)} %copy-done, f32[8,64,256]{2,1,0:T(8,128)S(1)} %copy.23.low, f32[8,64,256]{2,1,0:T(8,128)S(1)} %copy.24.high, f32[8,1280]{1,0:T(8,128)S(1)} %collective-permute-done.2.above, ...), custom_call_target="tpu_custom_call" | custom-call | flops 2415919104 | bytes 8388608 | tf_op jit(solution)/shard_map/columns_and_stencil/pallas_call | solution.py:92
  93.4 0.0 copy-start.1
  93.4 1.3 %copy-done.1 = f32[8,64,1024]{2,1,0:T(8,128)} copy-done((f32[8,64,1024]{2,1,0:T(8,128)}, f32[8,64,1024]{2,1,0:T(8,128)S(1)}, u32[]{:S(2)}) %copy-start.1) | copy-done | bytes 2097176
  94.7 0.0 all-to-all-done.1
  94.7 4.3 %copy.38 = f32[8,4,64,256]{3,1,2,0:T(4,128)} copy(f32[8,4,64,256]{3,2,1,0:T(8,128)} %bitcast.12) | data formatting | bytes 4194304 | tf_op jit(solution)/shard_map/reshape | solution.py:171
  99.0 0.0 copy-start.2
  99.0 3.4 %reshape.26 = f32[8,64,1024]{2,1,0:T(8,128)} reshape(f32[8,64,4,256]{3,2,1,0:T(4,128)} %bitcast.27) | data formatting | bytes 4194304 | tf_op jit(solution)/shard_map/reshape | solution.py:172
  102.4 0.0 copy-done.2
  102.4 4.0 %multiply_add_fusion = f32[8,64,1024]{2,1,0:T(8,128)} fusion(f32[8,64,1024]{2,1,0:T(8,128)S(1)} %copy-done.2, f32[8,64,1024]{2,1,0:T(8,128)} %reshape.26, f32[]{:T(128)} %bitcast.7), kind=kLoop, calls=%fused_computation.2 | loop fusion | flops 1048576 | bytes 6291460 | tf_op jit(solution)/shard_map/add | solution.py:173
  (10 shorter events, 0.0 us)
Async XLA Ops:
  5.8 7.8 %copy-start.6 = (f32[511]{0:T(512)S(1)}, f32[511]{0:T(512)}, u32[]{:S(2)}) copy-start(f32[511]{0:T(512)} %param.8) | copy-start | bytes 6136
  5.8 34.1 %all-to-all-start = ((f32[32,64,256]{2,1,0:T(8,128)}), f32[32,64,256]{2,1,0:T(8,128)S(1)}, u32[]{:S(2)}, u32[]{:S(2)}) async-start(f32[32,64,256]{2,1,0:T(8,128)} %bitcast.26), calls=%async_computation | async-start | bytes 4194304 | tf_op jit(solution)/shard_map/all_to_all | solution.py:159
  43.2 1.3 %copy-start.3 = (f32[2048,256]{1,0:T(8,128)}, f32[2048,256]{1,0:T(8,128)S(1)}, u32[]{:S(2)}) copy-start(f32[2048,256]{1,0:T(8,128)S(1)} %rows.1) | copy-start | bytes 6291460
  44.5 14.4 %copy-start = (f32[8,64,1024]{2,1,0:T(8,128)S(1)}, f32[8,64,1024]{2,1,0:T(8,128)}, u32[]{:S(2)}) copy-start(f32[8,64,1024]{2,1,0:T(8,128)} %value.1) | copy-start | bytes 6291460
  44.5 37.2 %copy-start.8 = (f32[2]{0:T(128)S(1)}, f32[2]{0:T(128)}, u32[]{:S(2)}) copy-start(f32[2]{0:T(128)} %param.10) | copy-start | bytes 28
  44.5 37.9 %copy-start.7 = (f32[511]{0:T(512)S(1)}, f32[511]{0:T(512)}, u32[]{:S(2)}) copy-start(f32[511]{0:T(512)} %param.9) | copy-start | bytes 6136
  44.5 39.2 %copy-start.9 = (f32[3]{0:T(128)S(1)}, f32[3]{0:T(128)}, u32[]{:S(2)}) copy-start(f32[3]{0:T(128)} %param.11) | copy-start | bytes 40
  44.5 39.2 %copy-start.10 = (f32[3]{0:T(128)S(1)}, f32[3]{0:T(128)}, u32[]{:S(2)}) copy-start(f32[3]{0:T(128)} %param.12) | copy-start | bytes 40
  44.5 50.2 %all-to-all-start.1 = ((f32[32,64,256]{2,1,0:T(8,128)}), f32[32,64,256]{2,1,0:T(8,128)}, u32[]{:S(2)}, u32[]{:S(2)}) async-start(f32[32,64,256]{2,1,0:T(8,128)} %bitcast.24), calls=%async_computation.1 | async-start | bytes 4194304 | tf_op jit(solution)/shard_map/all_to_all | solution.py:170
  52.0 16.5 %collective-permute-start = (f32[8,64,256]{2,0,1:T(8,128)S(1)}, f32[8,64,256]{2,0,1:T(8,128)S(1)}, u32[]{:S(2)}, u32[]{:S(2)}) collective-permute-start(f32[8,64,256]{2,0,1:T(8,128)S(1)} %copy.29), channel_id=1, source_target_pairs={{0,1},{1,2},{2,3},{3,4},{4,5},{5,6},{6,7},{8,9},{9,10},{10,11},{11... | collective-permute-start | bytes 1572872 | tf_op jit(solution)/shard_map/ppermute | solution.py:144
  57.0 16.8 %collective-permute-start.1 = (f32[8,64,256]{2,0,1:T(8,128)S(1)}, f32[8,64,256]{2,0,1:T(8,128)S(1)}, u32[]{:S(2)}, u32[]{:S(2)}) collective-permute-start(f32[8,64,256]{2,0,1:T(8,128)S(1)} %copy.30), channel_id=1, source_target_pairs={{1,0},{2,1},{3,2},{4,3},{5,4},{6,5},{7,6},{9,8},{10,9},{11,10},{12... | collective-permute-start | bytes 1572872 | tf_op jit(solution)/shard_map/ppermute | solution.py:144
  68.5 7.3 %copy-start.4 = (f32[8,64,256]{2,0,1:T(8,128)}, f32[8,64,256]{2,0,1:T(8,128)S(1)}, u32[]{:S(2)}) copy-start(f32[8,64,256]{2,0,1:T(8,128)S(1)} %collective-permute-done) | copy-start | bytes 1572868
  73.8 2.0 %copy-start.5 = (f32[8,64,256]{2,0,1:T(8,128)}, f32[8,64,256]{2,0,1:T(8,128)S(1)}, u32[]{:S(2)}) copy-start(f32[8,64,256]{2,0,1:T(8,128)S(1)} %collective-permute-done.1) | copy-start | bytes 1572868
  73.8 13.6 %collective-permute-start.2 = (f32[8,1280]{1,0:T(8,128)S(1)}, f32[8,1280]{1,0:T(8,128)S(1)}, u32[]{:S(2)}, u32[]{:S(2)}) collective-permute-start(f32[8,1280]{1,0:T(8,128)S(1)} %pad_maximum_fusion.1), channel_id=1, source_target_pairs={{0,8},{8,16},{16,24},{24,32},{32,40},{40,48},{48,56},{56,64},{64,7... | collective-permute-start | bytes 122888 | tf_op jit(solution)/shard_map/ppermute | solution.py:144
  75.8 11.7 %collective-permute-start.3 = (f32[8,1280]{1,0:T(8,128)S(1)}, f32[8,1280]{1,0:T(8,128)S(1)}, u32[]{:S(2)}, u32[]{:S(2)}) collective-permute-start(f32[8,1280]{1,0:T(8,128)S(1)} %pad_maximum_fusion.2), channel_id=1, source_target_pairs={{8,0},{16,8},{24,16},{32,24},{40,32},{48,40},{56,48},{64,56},{72,6... | collective-permute-start | bytes 122888 | tf_op jit(solution)/shard_map/ppermute | solution.py:144
  93.4 1.3 %copy-start.1 = (f32[8,64,1024]{2,1,0:T(8,128)}, f32[8,64,1024]{2,1,0:T(8,128)S(1)}, u32[]{:S(2)}) copy-start(f32[8,64,1024]{2,1,0:T(8,128)S(1)} %get-tuple-element.5) | copy-start | bytes 6291460
  99.0 3.4 %copy-start.2 = (f32[8,64,1024]{2,1,0:T(8,128)S(1)}, f32[8,64,1024]{2,1,0:T(8,128)}, u32[]{:S(2)}) copy-start(f32[8,64,1024]{2,1,0:T(8,128)} %copy-done.1) | copy-start | bytes 6291460

commit v2 on v1

v2 whole, which is shorter than its diff:
```python
import jax
import jax.numpy as jnp
from jax import lax
from jax.experimental import pallas as pl
from jax.experimental.pallas import tpu as pltpu
from jax.sharding import PartitionSpec as P

BLOCK = 256
WINDOW = 3 * BLOCK
HALF = BLOCK // 2
EDGE = 128
RING = 4
CORES = 2
VMEM = pl.BlockSpec(memory_space=pltpu.VMEM)
SMEM = pl.BlockSpec(memory_space=pltpu.SMEM)


def params(mib):
    return pltpu.CompilerParams(vmem_limit_bytes=mib * 1024 * 1024)


def f32(*shape):
    return jax.ShapeDtypeStruct(shape, jnp.float32)


def split(x):
    high = x.astype(jnp.bfloat16)
    return high, (x - high.astype(jnp.float32)).astype(jnp.bfloat16)


def band(weights, wide):
    wide[...] = jnp.zeros_like(wide)
    wide[:, : weights.shape[1]] = weights[...]
    spread = jnp.broadcast_to(wide[...], (BLOCK, WINDOW))
    return split(pltpu.roll(spread, 1, 1, stride=1, stride_axis=0)), jnp.sum(wide[...], axis=1, keepdims=True)


def product(a, b, contract):
    dims = (contract, ((), ()))
    return (
        lax.dot_general(a[0], b[0], dims, preferred_element_type=jnp.float32)
        + lax.dot_general(a[0], b[1], dims, preferred_element_type=jnp.float32)
        + lax.dot_general(a[1], b[0], dims, preferred_element_type=jnp.float32)
    )


def ring(y, step):
    return lax.rem(y + (step + RING), RING)


def part_of(index, size):
    return pl.ds(pl.multiple_of(index * size, size), size)


def within_kernel(value, weights, out, taps_hi, taps_lo, total_ref, wide_hi, wide_lo, wide):
    planes, rows, cols = value.shape
    taps, total = band(weights, wide)
    taps_hi[...], taps_lo[...] = taps
    total_ref[...] = jnp.broadcast_to(total, total_ref.shape)
    wide_hi[...], wide_lo[...] = split(value[...].reshape(planes * rows, cols))
    for start in range(0, cols, BLOCK):
        first, last = max(0, start - BLOCK), min(cols, start + 2 * BLOCK)
        used = slice(first - start + BLOCK, last - start + BLOCK)
        sums = product(
            (wide_hi[:, first:last], wide_lo[:, first:last]), tuple(t[:, used] for t in taps), ((1,), (1,))
        )
        out[:, :, start : start + BLOCK] = (
            sums.reshape(planes, rows, BLOCK) - total[None] * value[:, :, start : start + BLOCK]
        )


def within_part(value, weights):
    planes, rows, cols = value.shape
    scratch = pltpu.VMEM((planes * rows, cols), jnp.bfloat16)
    taps = jax.ShapeDtypeStruct((BLOCK, WINDOW), jnp.bfloat16)
    return pl.pallas_call(
        within_kernel, out_shape=(f32(*value.shape), taps, taps, f32(8, EDGE)), in_specs=[VMEM] * 2,
        out_specs=[VMEM] * 4,
        scratch_shapes=[scratch, scratch, pltpu.VMEM((1, WINDOW), jnp.float32)], compiler_params=params(9), name="own_columns",
    )(value, weights)


def local_kernel(
    intensity, diffusion, drift, cross, value, low, high, above, below, within, taps_hi, taps_lo, jump_ref, part_ref
):
    planes, rows, cols = value.shape
    jump_ref[...] = within[...]
    for source, start, used in ((low, 0, slice(0, BLOCK)), (high, cols - BLOCK, slice(2 * BLOCK, WINDOW))):
        side = split(source[:, :rows].reshape(planes * rows, BLOCK))
        sums = product(side, (taps_hi[:, used], taps_lo[:, used]), ((1,), (1,)))
        jump_ref[:, :, start : start + BLOCK] += sums.reshape(planes, rows, BLOCK)
    row_diff, row_drift = diffusion[0], drift[0] * 0.5
    col_diff, col_drift = diffusion[1], drift[1] * 0.5
    plane_diff, plane_drift = diffusion[2], drift[2] * 0.5
    mixed = cross[0] * 0.25
    side = cols - 1

    def along(x, first, last):
        lane = lax.broadcasted_iota(jnp.int32, x.shape, 1)
        right = jnp.where(lane == side, last, pltpu.roll(x, side, 1))
        left = jnp.where(lane == 0, first, pltpu.roll(x, 1, 1))
        return right, left

    line = lax.broadcasted_iota(jnp.int32, (rows, cols), 0)
    for p in range(planes):
        edges = []
        for edge, row in ((above, rows), (below, rows + 1)):
            middle = edge[p : p + 1]
            right, left = along(middle, low[p, row : row + 1, BLOCK - 1 :], high[p, row : row + 1, :1])
            edges.append((middle, right - left))
        above_term = (row_diff - row_drift) * edges[0][0] - mixed * edges[0][1]
        below_term = (row_diff + row_drift) * edges[1][0] + mixed * edges[1][1]
        x = value[p]
        right, left = along(x, low[p, :rows, BLOCK - 1 :], high[p, :rows, :1])
        slope = right - left
        out = x + col_diff * (right - 2.0 * x + left) + col_drift * slope
        down = (row_diff + row_drift) * x + mixed * slope
        up = (row_diff - row_drift) * x - mixed * slope
        down = jnp.where(line == rows - 1, below_term, pltpu.roll(down, rows - 1, 0))
        up = jnp.where(line == 0, above_term, pltpu.roll(up, 1, 0))
        out = out + (down - 2.0 * row_diff * x + up)
        out = out - 2.0 * plane_diff * x
        if p + 1 < planes:
            out = out + (plane_diff + plane_drift) * value[p + 1]
        if p > 0:
            out = out + (plane_diff - plane_drift) * value[p - 1]
        part_ref[p] = out + intensity[1] * jump_ref[p]


def local_part(intensity, diffusion, drift, cross, value, low, high, above, below, within, taps):
    planes, rows, cols = value.shape
    return pl.pallas_call(
        local_kernel, out_shape=(f32(*value.shape),) * 2, in_specs=[SMEM] * 4 + [VMEM] * 8, out_specs=(VMEM, VMEM),
        compiler_params=params(6),
        name="side_columns_and_stencil",
    )(intensity, diffusion, drift, cross, value, low, high, above, below, within, *taps)


def tails_kernel(place, value, other, edge, high_side, low_side, above, below):
    planes, rows, cols = value.shape
    for core in range(CORES):

        @pl.when(place[2] == core)
        def _():
            for p in range(planes):
                line = slice(p, p + 1)
                above[line] = other[p, rows - 1 :, :] if core else edge[line]
                below[line] = edge[line] if core else other[p, :1, :]

    for out, start in ((high_side, cols - BLOCK), (low_side, 0)):
        columns = slice(start, start + BLOCK)
        out[:, :rows] = value[:, :, columns]
        for p in range(planes):
            out[p, rows : rows + 1] = above[p : p + 1, columns]
            out[p, rows + 1 : rows + 2] = below[p : p + 1, columns]
            out[p, rows + 2 :] = jnp.zeros((out.shape[1] - rows - 2, BLOCK), jnp.float32)


def tails_part(place, value, other, edge):
    planes, rows, cols = value.shape
    side = f32(planes, rows + 8, BLOCK)
    return pl.pallas_call(
        tails_kernel, out_shape=[side, side, f32(planes, cols), f32(planes, cols)], in_specs=[SMEM] + [VMEM] * 3,
        out_specs=[VMEM] * 4, compiler_params=params(4),
        name="tails",
    )(place, value, other, edge)


def taps_kernel(weights, high_ref, low_ref, total_ref, wide):
    (high_ref[...], low_ref[...]), total = band(weights, wide)
    total_ref[...] = jnp.broadcast_to(total, total_ref.shape)


def taps_part(weights):
    shape = jax.ShapeDtypeStruct((BLOCK, WINDOW), jnp.bfloat16)
    return pl.pallas_call(
        taps_kernel, out_shape=(shape, shape, f32(8, EDGE)), in_specs=[VMEM], out_specs=(VMEM,) * 3,
        scratch_shapes=[pltpu.VMEM((1, WINDOW), jnp.float32)], compiler_params=params(8), name="row_taps",
    )(weights)


def load_kernel(place, value, held, line, done):
    copy = pltpu.make_async_copy(value, held, done)
    copy.start()
    copy.wait()
    planes, rows, _ = value.shape
    for core, row in ((0, 0), (1, rows - 1)):

        @pl.when(place[2] == core)
        def _():
            for p in range(planes):
                line[p : p + 1] = held[p, row : row + 1, :]


def load_part(place, value):
    planes, _, cols = value.shape
    return pl.pallas_call(
        load_kernel, out_shape=[f32(*value.shape), f32(planes, cols)],
        in_specs=[SMEM, pl.BlockSpec(memory_space=pl.ANY)], out_specs=[VMEM] * 2,
        scratch_shapes=[pltpu.SemaphoreType.DMA], compiler_params=params(4), name="load",
    )(place, value)


def pieces_kernel(steps, place, value, other, *refs):
    outs, done = refs[:-1], refs[-1]
    y, core = place[1], place[2]
    rows = value.shape[1]
    copies = []
    for i, (k, out) in enumerate(zip(steps, outs)):
        plane = CORES * ring(y, k) + core
        for j, (source, at) in enumerate(((value, core), (other, 1 - core))):
            copies.append(pltpu.make_async_copy(source.at[plane], out.at[part_of(at, rows)], done.at[i, j]))
    for copy in copies:
        copy.start()
    for copy in copies:
        copy.wait()


def pieces_part(steps, place, value, other):
    _, rows, cols = value.shape
    anywhere = pl.BlockSpec(memory_space=pl.ANY)
    return pl.pallas_call(
        lambda *refs: pieces_kernel(steps, *refs),
        out_shape=[f32(CORES * rows, cols)] * len(steps), in_specs=[SMEM, anywhere, anywhere],
        out_specs=[VMEM] * len(steps), scratch_shapes=[pltpu.SemaphoreType.DMA((len(steps), 2))],
        compiler_params=params(4), name="pieces",
    )(place, value, other)


def tap_tile(taps, at, size):
    return tuple(t[:, at : at + size] for t in taps)


def near_kernel(place, p0, p1, p3, taps_hi, taps_lo, total, out, hold):
    y = place[1]
    taps = (taps_hi, taps_lo)
    size = p0.shape[0]
    for k, piece in ((0, p0), (1, p1), (3, p3)):
        hold[part_of(ring(y, -k), size)] = piece[...]
    hold[part_of(ring(y, -2), size)] = jnp.zeros_like(p0)
    first, second = split(hold[:BLOCK]), split(hold[BLOCK:])
    dims = ((1,), (0,))
    scale = total[0:1, 0:1]
    out[:BLOCK] = (
        product(tap_tile(taps, BLOCK, BLOCK), first, dims)
        + product(tap_tile(taps, 2 * BLOCK, BLOCK), second, dims)
        - scale * hold[:BLOCK]
    )
    out[BLOCK:] = (
        product(tap_tile(taps, 0, BLOCK), first, dims)
        + product(tap_tile(taps, BLOCK, BLOCK), second, dims)
        - scale * hold[BLOCK:]
    )


def near_part(place, p0, p1, p3, taps):
    size, cols = p0.shape
    return pl.pallas_call(
        near_kernel, out_shape=f32(RING * size, cols), in_specs=[SMEM] + [VMEM] * 6, out_specs=VMEM,
        scratch_shapes=[pltpu.VMEM((RING * size, cols), jnp.float32)], compiler_params=params(9), name="near_rows",
    )(place, p0, p1, p3, *taps)


def middle_kernel(place, near, p2, x0, x1, x3, taps_hi, taps_lo, total, out, opposite, hold):
    y = place[1]
    taps = (taps_hi, taps_lo)
    size = p2.shape[0]
    at = ring(y, -2)
    dims = ((1,), (0,))
    for k, piece in ((0, x0), (1, x1), (3, x3)):
        hold[part_of(ring(y, -k), size)] = piece[...]
    hold[part_of(at, size)] = jnp.zeros_like(p2)
    rows2 = split(p2[...])
    below, above = split(hold[:BLOCK]), split(hold[BLOCK:])
    for i, far, tile in ((0, above, 0), (1, below, 2 * BLOCK)):
        column = part_of(at + 2 - 2 * i, HALF)
        mine = tuple(t[:, column] for t in taps)
        out[i * BLOCK : (i + 1) * BLOCK] = (
            near[i * BLOCK : (i + 1) * BLOCK]
            + product(mine, rows2, dims)
            + product(tap_tile(taps, tile, BLOCK), far, dims)
        )
    mid = out[part_of(at, size)] - total[0:1, 0:1] * p2[...]
    out[part_of(at, size)] = mid
    opposite[...] = mid


def middle_part(place, near, p2, x0, x1, x3, taps):
    rows, cols = near.shape
    size = rows // RING
    return pl.pallas_call(
        middle_kernel, out_shape=(f32(rows, cols), f32(size, cols)), in_specs=[SMEM] + [VMEM] * 8,
        out_specs=(VMEM, VMEM), scratch_shapes=[pltpu.VMEM((rows, cols), jnp.float32)],
        compiler_params=params(9),
        name="middle_rows",
    )(place, near, p2, x0, x1, x3, *taps)


def last_kernel(place, middle, x2, taps_hi, taps_lo, b0, b1, b3, hold):
    y = place[1]
    taps = (taps_hi, taps_lo)
    size = x2.shape[0]
    at = ring(y, -2)
    dims = ((1,), (0,))
    hold[...] = middle[...]
    far = split(x2[...])

    @pl.when(at >= RING // 2)
    def _():
        column = part_of(at - RING // 2, HALF)
        hold[:BLOCK] += product(tuple(t[:, column] for t in taps), far, dims)

    @pl.when(at < RING // 2)
    def _():
        column = part_of(at + RING, HALF)
        hold[BLOCK:] += product(tuple(t[:, column] for t in taps), far, dims)

    for k, out in ((0, b0), (1, b1), (3, b3)):
        out[...] = hold[part_of(ring(y, -k), size)]


def last_part(place, middle, x2, taps):
    rows, cols = middle.shape
    return pl.pallas_call(
        last_kernel, out_shape=[f32(rows // RING, cols)] * 3, in_specs=[SMEM] + [VMEM] * 4, out_specs=[VMEM] * 3,
        scratch_shapes=[pltpu.VMEM((rows, cols), jnp.float32)], compiler_params=params(9), name="last_rows",
    )(place, middle, x2, *taps[:2])


def swap_kernel(place, da, db, out):
    rows = out.shape[1]
    for k, source in enumerate((da, db)):
        out[k] = source[part_of(1 - place[2], rows)]


def swap_part(place, da, db):
    rows, cols = da.shape
    return pl.pallas_call(
        swap_kernel, out_shape=f32(2, rows // CORES, cols), in_specs=[SMEM] + [VMEM] * 2, out_specs=VMEM,
        compiler_params=params(8), name="swap",
    )(place, da, db)


def finish_kernel(steps, place, intensity, da, db, other, part, *refs):
    updated, jump, new_updated, new_jump, done = refs[-5:]
    y, core = place[1], place[2]
    rows = other.shape[1]
    copies = []
    for i, (step, source) in enumerate(zip(steps, (da, db))):
        for j in range(CORES):
            at = CORES * i + j
            plane = CORES * ring(y, step) + (1 - core if j else core)
            block = other[i] if j else source[part_of(core, rows)]
            new_jump[at] = block
            new_updated[at] = part[plane] + intensity[0] * block
            for k, (new, out) in enumerate(((new_jump, jump), (new_updated, updated))):
                copy = pltpu.make_async_copy(new.at[at], out.at[plane], done.at[at, k])
                copy.start()
                copies.append(copy)
    for copy in copies:
        copy.wait()


def finish_part(steps, place, intensity, da, db, other, part, results):
    planes, rows, cols = part.shape
    anywhere = pl.BlockSpec(memory_space=pl.ANY)
    scratch = pltpu.VMEM((2 * CORES, rows, cols), jnp.float32)
    return pl.pallas_call(
        lambda *refs: finish_kernel(steps, *refs),
        out_shape=[f32(*part.shape)] * 2, in_specs=[SMEM, SMEM] + [VMEM] * 4 + [anywhere] * len(results),
        out_specs=[anywhere] * 2, scratch_shapes=[scratch, scratch, pltpu.SemaphoreType.DMA((2 * CORES, 2))],
        input_output_aliases={6: 0, 7: 1} if results else {},
        compiler_params=params(8), name="finish",
    )(place, intensity, da, db, other, part, *results)


def neighbours(low_side, high_side, axis):
    count = lax.axis_size(axis)
    forward = [(i, i + 1) for i in range(count - 1)]
    backward = [(i + 1, i) for i in range(count - 1)]
    return lax.ppermute(high_side, axis, forward), lax.ppermute(low_side, axis, backward)


def send(block, move):
    route = []
    for i in range(RING * RING * CORES):
        x, y, core = move(i // (RING * CORES), i // CORES % RING, i % CORES)
        if 0 <= x < RING:
            route.append((i, (x * RING + y % RING) * CORES + core))
    return lax.ppermute(block, "gx", route)


def to_ring(block, step):
    return send(block, lambda x, y, core: (x, y + step, core))


def to_other_core(block):
    return send(block, lambda x, y, core: (x, y, 1 - core))


def across_chips(line):
    ends = lax.axis_size("gx") - 1
    route = [(i, i + 1 if i % CORES else i - 1) for i in range(1, ends)]
    return lax.ppermute(line, "gx", route)


def to_group(block, k):
    return send(block, lambda x, y, core: (x + 1 if (y - k) % RING >= RING // 2 else x - 1, y, core))


def after(x, *others):
    return lax.optimization_barrier((x, *others))[0]


def shards(value, kernel_rows, kernel_cols, intensity, diffusion, drift, cross):
    planes, rows, cols = value.shape
    me = lax.axis_index("gx")
    chip = lax.div(me, CORES)
    place = jnp.stack([lax.div(chip, RING), lax.rem(chip, RING), lax.rem(me, CORES)])

    other = to_other_core(value)
    value, line = load_part(place, value)
    edge = across_chips(line)

    s1, s3, p0 = pieces_part((1, 3, 0), place, value, other)
    p1, p3, x0 = to_ring(s1, 1), to_ring(s3, 3), to_group(p0, 0)
    (s2,) = pieces_part((2,), after(place, p0, edge), value, other)
    within, col_hi, col_lo, _ = within_part(value, after(kernel_cols[None], s2))
    taps = taps_part(after(kernel_rows[None], within))
    p2 = to_ring(after(s2, p1, p3, taps[2]), 2)
    x1, x3 = to_group(after(p1, x0), 1), to_group(after(p3, x0), 3)
    high_side, low_side, above, below = tails_part(after(place, p0), value, other, edge)
    low, high = neighbours(low_side, high_side, "gy")
    near = near_part(after(place, low, high), p0, p1, p3, taps)
    x2 = to_group(p2, 2)
    middle, b2 = middle_part(place, near, p2, x0, x1, x3, taps)
    d2 = to_ring(b2, -2)
    jump_cols, part = local_part(
        after(intensity, b2), diffusion, drift, cross, value, low, high, above, below, within, (col_hi, col_lo)
    )
    b0, b1, b3 = last_part(after(place, part), middle, x2, taps)
    d1, d3 = to_ring(b1, -1), to_ring(b3, -3)
    swapped = to_other_core(swap_part(place, b0, d2))
    results = finish_part((0, 2), place, intensity, b0, d2, swapped, part, ())
    swapped = to_other_core(swap_part(place, d1, d3))
    updated, jump_rows = finish_part((1, 3), place, intensity, d1, d3, swapped, part, results)
    return updated, jump_rows, jump_cols


def solution(mesh):
    return jax.shard_map(
        shards,
        mesh=mesh,
        in_specs=(P(None, "gx", "gy"), P(), P(), P(), P(), P(), P()),
        out_specs=(P(None, "gx", "gy"), P(None, "gx", "gy"), P(None, "gx", "gy")),
        check_vma=False,
    )
```

time: 107 us -> 89.5 us (0.84)
  the two profiles are of different devices: /device:TPU:102 before, /device:TPU:99 now
where the time goes in v2:
time: 89.5 us; the launch traced here: 89.2 us
  starting transfers between devices  33.9 us (38%)
  waiting for transfers between devices  29.8 us (33%)
  Pallas kernels  22.1 us (25%)
  between operations  1.72 us (2%)
  local copies, waits for them, and re-layouts  1.62 us (2%)
    ppermute x13, starting transfers between devices, send(): return lax.ppermute(block, 'gx', route)  24.5 us
    ppermute x13, waiting for transfers between devices, send(): return lax.ppermute(block, 'gx', route)  14.5 us
    ppermute x1, waiting for transfers between devices, across_chips(): return lax.ppermute(line, 'gx', route)  7.92 us
    ppermute x1, waiting for transfers between devices, neighbours(): lax.ppermute(low_side, axis, backward)  5.56 us
    pallas_call x1, Pallas kernels, local_part(): pl.pallas_call(local_kernel, out_shape=(f32(*value.shape),) * 2, in_specs...  4.89 us
    ppermute x1, starting transfers between devices, neighbours(): lax.ppermute(high_side, axis, forward)  4.76 us
    pallas_call x2, Pallas kernels, finish_part(): pl.pallas_call(lambda *refs: finish_kernel(steps, *refs), out_shape=[f32(...  3.91 us
    pallas_call x1, Pallas kernels, middle_part(): pl.pallas_call(middle_kernel, out_shape=(f32(rows, cols), f32(size, cols)...  2.73 us
  transfers between devices with their start and end apart: 16, of which 7 were waited for; matrix products, arithmetic and copies ran while one was open for 0% of the time, Pallas kernels for 22%

profile of v2, /device:TPU:99, one launch (start us, length us, event | category | flops | bytes accessed | tf_op | source)
XLA Modules:
  0.0 89.2 jit_solution(3595141348941084861)
XLA Ops:
  0.6 0.8 collective-permute-start
  1.4 0.1 pad_add_fusion.place.refs_0_
  1.5 0.0 copy-start
  1.5 1.6 %copy-done = f32[8,64,1024]{2,1,0:T(8,128)S(1)} copy-done((f32[8,64,1024]{2,1,0:T(8,128)S(1)}, f32[8,64,1024]{2,1,0:T(8,128)}, u32[]{:S(2)}) %copy-start) | copy-done | bytes 2097176
  3.1 0.7 load.1
  3.8 1.6 %collective-permute-done.refs_2_.other = f32[8,64,1024]{2,1,0:T(8,128)S(1)} collective-permute-done((f32[8,64,1024]{2,1,0:T(8,128)}, f32[8,64,1024]{2,1,0:T(8,128)S(1)}, u32[]{:S(2)}, u32[]{:S(2)}) %collective-permute-start) | collective-permute-done | bytes 2097184 | tf_op jit(solution)/shard_map/ppermute | solution.py:390
  5.4 0.7 pieces.2
  6.1 1.4 %collective-permute-start.4 = (f32[128,1024]{1,0:T(8,128)S(1)}, f32[128,1024]{1,0:T(8,128)S(1)}, u32[]{:S(2)}, u32[]{:S(2)}) collective-permute-start(f32[128,1024]{1,0:T(8,128)S(1)} %get-tuple-element.46), channel_id=1, source_target_pairs={{0,16},{8,24},{16,32},{24,40},{32,48},{40,56},{48,0},{56,8},{64,80... | collective-permute-start | bytes 1572872 | tf_op jit(solution)/shard_map/ppermute | solution.py:390
  7.5 1.5 %collective-permute-start.5 = (f32[128,1024]{1,0:T(8,128)S(1)}, f32[128,1024]{1,0:T(8,128)S(1)}, u32[]{:S(2)}, u32[]{:S(2)}) collective-permute-start(f32[128,1024]{1,0:T(8,128)S(1)} %get-tuple-element.47), channel_id=1, source_target_pairs={{0,48},{8,56},{16,0},{24,8},{32,16},{40,24},{48,32},{56,40},{64,11... | collective-permute-start | bytes 1572872 | tf_op jit(solution)/shard_map/ppermute | solution.py:390
  9.0 2.7 %collective-permute-start.1 = (f32[8,1024]{1,0:T(8,128)S(1)}, f32[8,1024]{1,0:T(8,128)S(1)}, u32[]{:S(2)}, u32[]{:S(2)}) collective-permute-start(f32[8,1024]{1,0:T(8,128)S(1)} %get-tuple-element.42), channel_id=1, source_target_pairs={{8,16},{16,8},{24,32},{32,24},{40,48},{48,40},{56,64},{64,56},{72,... | collective-permute-start | bytes 98312 | tf_op jit(solution)/shard_map/ppermute | solution.py:404
  11.7 0.0 copy-start.2
  11.7 2.2 %collective-permute-start.7 = (f32[128,1024]{1,0:T(8,128)S(1)}, f32[128,1024]{1,0:T(8,128)S(1)}, u32[]{:S(2)}, u32[]{:S(2)}) collective-permute-start(f32[128,1024]{1,0:T(8,128)S(1)} %get-tuple-element.40.p0), channel_id=1, source_target_pairs={{32,96},{40,104},{48,112},{56,120},{64,0},{72,8},{80,16},{88,24},{... | collective-permute-start | bytes 1572872 | tf_op jit(solution)/shard_map/ppermute | solution.py:390
  13.9 7.9 %collective-permute-done.1.edge = f32[8,1024]{1,0:T(8,128)S(1)} collective-permute-done((f32[8,1024]{1,0:T(8,128)S(1)}, f32[8,1024]{1,0:T(8,128)S(1)}, u32[]{:S(2)}, u32[]{:S(2)}) %collective-permute-start.1) | collective-permute-done | bytes 32800 | tf_op jit(solution)/shard_map/ppermute | solution.py:404
  21.8 0.6 pieces.3
  22.4 0.0 copy-start.3
  22.4 0.0 copy-done.2
  22.4 2.4 %own_columns.1 = (f32[8,64,1024]{2,1,0:T(8,128)S(1)}, bf16[256,768]{1,0:T(8,128)(2,1)S(1)}, bf16[256,768]{1,0:T(8,128)(2,1)S(1)}, f32[8,128]{1,0:T(8,128)}) custom-call(f32[8,64,1024]{2,1,0:T(8,128)S(1)} %get-tuple-element.39.refs_1_.value, f32[1,511]{1,0:T(1,128)S(1)} %bitcast.5), custom_call_target="tpu_custom_call" | custom-call | tf_op jit(solution)/shard_map/own_columns/pallas_call | solution.py:76
  24.9 0.0 copy-done.3
  24.9 0.2 row_taps.1
  25.1 0.0 collective-permute-done.4.p1
  25.1 0.0 collective-permute-done.5.p3
  25.1 2.7 %collective-permute-start.6 = (f32[128,1024]{1,0:T(8,128)S(1)}, f32[128,1024]{1,0:T(8,128)S(1)}, u32[]{:S(2)}, u32[]{:S(2)}) collective-permute-start(f32[128,1024]{1,0:T(8,128)S(1)} %pieces.3), channel_id=1, source_target_pairs={{0,32},{8,40},{16,48},{24,56},{32,0},{40,8},{48,16},{56,24},{64,96... | collective-permute-start | bytes 1572872 | tf_op jit(solution)/shard_map/ppermute | solution.py:390
  27.8 0.7 tails.1
  28.5 4.8 %collective-permute-start.2 = (f32[8,72,256]{2,1,0:T(8,128)S(1)}, f32[8,72,256]{2,1,0:T(8,128)S(1)}, u32[]{:S(2)}, u32[]{:S(2)}) collective-permute-start(f32[8,72,256]{2,1,0:T(8,128)S(1)} %get-tuple-element.43), channel_id=1, source_target_pairs={{0,1},{1,2},{2,3},{3,4},{4,5},{5,6},{6,7},{8,9},{9,10},{10,11},{11... | collective-permute-start | bytes 1769480 | tf_op jit(solution)/shard_map/ppermute | solution.py:381
  33.2 1.9 %collective-permute-start.3 = (f32[8,72,256]{2,1,0:T(8,128)S(1)}, f32[8,72,256]{2,1,0:T(8,128)S(1)}, u32[]{:S(2)}, u32[]{:S(2)}) collective-permute-start(f32[8,72,256]{2,1,0:T(8,128)S(1)} %get-tuple-element.44), channel_id=1, source_target_pairs={{1,0},{2,1},{3,2},{4,3},{5,4},{6,5},{7,6},{9,8},{10,9},{11,10},{12... | collective-permute-start | bytes 1769480 | tf_op jit(solution)/shard_map/ppermute | solution.py:381
  35.2 0.0 collective-permute-done.7.x0
  35.2 3.1 %collective-permute-start.8 = (f32[128,1024]{1,0:T(8,128)S(1)}, f32[128,1024]{1,0:T(8,128)S(1)}, u32[]{:S(2)}, u32[]{:S(2)}) collective-permute-start(f32[128,1024]{1,0:T(8,128)S(1)} %collective-permute-done.4.p1), channel_id=1, source_target_pairs={{0,64},{8,72},{48,112},{56,120},{64,128},{72,136},{80,16},{88,24},... | collective-permute-start | bytes 1572872 | tf_op jit(solution)/shard_map/ppermute | solution.py:390
  38.3 2.2 %collective-permute-start.9 = (f32[128,1024]{1,0:T(8,128)S(1)}, f32[128,1024]{1,0:T(8,128)S(1)}, u32[]{:S(2)}, u32[]{:S(2)}) collective-permute-start(f32[128,1024]{1,0:T(8,128)S(1)} %collective-permute-done.5.p3), channel_id=1, source_target_pairs={{16,80},{24,88},{32,96},{40,104},{64,0},{72,8},{80,144},{88,152},{... | collective-permute-start | bytes 1572872 | tf_op jit(solution)/shard_map/ppermute | solution.py:390
  40.5 0.0 collective-permute-done.6.p2
  40.5 3.1 %collective-permute-start.10 = (f32[128,1024]{1,0:T(8,128)S(1)}, f32[128,1024]{1,0:T(8,128)S(1)}, u32[]{:S(2)}, u32[]{:S(2)}) collective-permute-start(f32[128,1024]{1,0:T(8,128)S(1)} %collective-permute-done.6.p2), channel_id=1, source_target_pairs={{0,64},{8,72},{16,80},{24,88},{64,128},{72,136},{80,144},{88,152},... | collective-permute-start | bytes 1572872 | tf_op jit(solution)/shard_map/ppermute | solution.py:390
  44.3 1.8 %collective-permute-done.2.low = f32[8,72,256]{2,1,0:T(8,128)S(1)} collective-permute-done((f32[8,72,256]{2,1,0:T(8,128)S(1)}, f32[8,72,256]{2,1,0:T(8,128)S(1)}, u32[]{:S(2)}, u32[]{:S(2)}) %collective-permute-start.2) | collective-permute-done | bytes 589856 | tf_op jit(solution)/shard_map/ppermute | solution.py:381
  46.0 5.6 %collective-permute-done.3.high = f32[8,72,256]{2,1,0:T(8,128)S(1)} collective-permute-done((f32[8,72,256]{2,1,0:T(8,128)S(1)}, f32[8,72,256]{2,1,0:T(8,128)S(1)}, u32[]{:S(2)}, u32[]{:S(2)}) %collective-permute-start.3) | collective-permute-done | bytes 589856 | tf_op jit(solution)/shard_map/ppermute | solution.py:381
  51.6 2.7 %near_rows.1.near = f32[512,1024]{1,0:T(8,128)S(1)} custom-call(s32[3]{0:T(128)S(1)} %pad_add_fusion.place.refs_0_, f32[128,1024]{1,0:T(8,128)S(1)} %get-tuple-element.40.p0, f32[128,1024]{1,0:T(8,128)S(1)} %collective-permute-done.4.p1, f32[128,1024]{1,0:T(8,128)S(1)} %collective-permute-done.5.p3, bf16[256,768]{1,0:T(8,128)(2,1)S(1)} %get-tuple-element.52.taps_hi, ...), custom_call_target="tpu_custom_call" | custom-call | tf_op jit(solution)/shard_map/near_rows/pallas_call | solution.py:258
  54.3 0.0 copy-start.1
  54.3 0.0 copy-start.4
  54.3 0.0 copy-start.5
  54.3 0.0 collective-permute-done.8.x1
  54.3 0.0 collective-permute-done.9.x3
  54.3 2.7 %middle_rows.1 = (f32[512,1024]{1,0:T(8,128)S(1)}, f32[128,1024]{1,0:T(8,128)S(1)}) custom-call(s32[3]{0:T(128)S(1)} %pad_add_fusion.place.refs_0_, f32[512,1024]{1,0:T(8,128)S(1)} %near_rows.1.near, f32[128,1024]{1,0:T(8,128)S(1)} %collective-permute-done.6.p2, f32[128,1024]{1,0:T(8,128)S(1)} %collective-permute-done.7.x0, ...), custom_call_target="tpu_custom_call" | custom-call | tf_op jit(solution)/shard_map/middle_rows/pallas_call | solution.py:291
  57.1 0.3 collective-permute-start.14
  57.3 0.0 copy-done.1
  57.3 0.0 copy-done.4
  57.4 0.0 copy-done.5
  57.4 4.9 %side_columns_and_stencil.1 = (f32[8,64,1024]{2,1,0:T(8,128)}, f32[8,64,1024]{2,1,0:T(8,128)S(1)}) custom-call(f32[2]{0:T(128)S(1)} %copy-done.1, f32[3]{0:T(128)S(1)} %copy-done.4, f32[3]{0:T(128)S(1)} %copy-done.5, f32[1]{0:T(128)S(6)} %copy.14.cross, f32[8,64,1024]{2,1,0:T(8,128)S(1)} %get-tuple-element.39.refs_1_.value, ...), custom_call_target="tpu_custom_call" | custom-call | tf_op jit(solution)/shard_map/side_columns_and_stencil/pallas_call | solution.py:132
  62.2 0.0 collective-permute-done.10.x2
  62.3 1.4 %last_rows.1 = (f32[128,1024]{1,0:T(8,128)S(1)}, f32[128,1024]{1,0:T(8,128)S(1)}, f32[128,1024]{1,0:T(8,128)S(1)}) custom-call(s32[3]{0:T(128)S(1)} %pad_add_fusion.place.refs_0_, f32[512,1024]{1,0:T(8,128)S(1)} %get-tuple-element.66.middle, f32[128,1024]{1,0:T(8,128)S(1)} %collective-permute-done.10.x2, bf16[256,768]{1,0:T(8,128)(2,1)S(1)} %get-tuple-element.52.taps_hi, ...), custom_call_target="tpu_custom_call" | custom-call | tf_op jit(solution)/shard_map/last_rows/pallas_call | solution.py:324
  63.7 4.2 %collective-permute-start.11 = (f32[128,1024]{1,0:T(8,128)S(1)}, f32[128,1024]{1,0:T(8,128)S(1)}, u32[]{:S(2)}, u32[]{:S(2)}) collective-permute-start(f32[128,1024]{1,0:T(8,128)S(1)} %get-tuple-element.67), channel_id=1, source_target_pairs={{0,48},{8,56},{16,0},{24,8},{32,16},{40,24},{48,32},{56,40},{64,11... | collective-permute-start | bytes 1572872 | tf_op jit(solution)/shard_map/ppermute | solution.py:390
  67.9 0.0 collective-permute-start.12
  67.9 4.0 %collective-permute-done.14.db.refs_3_ = f32[128,1024]{1,0:T(8,128)S(1)} collective-permute-done((f32[128,1024]{1,0:T(8,128)S(1)}, f32[128,1024]{1,0:T(8,128)S(1)}, u32[]{:S(2)}, u32[]{:S(2)}) %collective-permute-start.14) | collective-permute-done | bytes 524320 | tf_op jit(solution)/shard_map/ppermute | solution.py:390
  71.9 0.6 swap.3
  72.5 2.1 %collective-permute-start.15 = (f32[2,64,1024]{2,1,0:T(8,128)S(1)}, f32[2,64,1024]{2,1,0:T(8,128)S(1)}, u32[]{:S(2)}, u32[]{:S(2)}) collective-permute-start(f32[2,64,1024]{2,1,0:T(8,128)S(1)} %swap.3), channel_id=1, source_target_pairs={{0,8},{8,0},{16,24},{24,16},{32,40},{40,32},{48,56},{56,48},{64,72... | collective-permute-start | bytes 1572872 | tf_op jit(solution)/shard_map/ppermute | solution.py:390
  74.7 7.1 %collective-permute-done.11.da.refs_2_ = f32[128,1024]{1,0:T(8,128)S(1)} collective-permute-done((f32[128,1024]{1,0:T(8,128)S(1)}, f32[128,1024]{1,0:T(8,128)S(1)}, u32[]{:S(2)}, u32[]{:S(2)}) %collective-permute-start.11) | collective-permute-done | bytes 524320 | tf_op jit(solution)/shard_map/ppermute | solution.py:390
  81.8 1.7 %collective-permute-done.12.db.refs_3_ = f32[128,1024]{1,0:T(8,128)S(1)} collective-permute-done((f32[128,1024]{1,0:T(8,128)S(1)}, f32[128,1024]{1,0:T(8,128)S(1)}, u32[]{:S(2)}, u32[]{:S(2)}) %collective-permute-start.12) | collective-permute-done | bytes 524320 | tf_op jit(solution)/shard_map/ppermute | solution.py:390
  83.5 0.6 swap.2
  84.1 1.0 %collective-permute-start.13 = (f32[2,64,1024]{2,1,0:T(8,128)S(1)}, f32[2,64,1024]{2,1,0:T(8,128)S(1)}, u32[]{:S(2)}, u32[]{:S(2)}) collective-permute-start(f32[2,64,1024]{2,1,0:T(8,128)S(1)} %swap.2), channel_id=1, source_target_pairs={{0,8},{8,0},{16,24},{24,16},{32,40},{40,32},{48,56},{56,48},{64,72... | collective-permute-start | bytes 1572872 | tf_op jit(solution)/shard_map/ppermute | solution.py:390
  85.1 0.0 collective-permute-done.15.refs_4_
  85.1 1.9 %finish.2 = (f32[8,64,1024]{2,1,0:T(8,128)}, f32[8,64,1024]{2,1,0:T(8,128)}) custom-call(s32[3]{0:T(128)S(1)} %pad_add_fusion.place.refs_0_, f32[2]{0:T(128)S(1)} %copy-done.1, f32[128,1024]{1,0:T(8,128)S(1)} %get-tuple-element.69.da.refs_2_, f32[128,1024]{1,0:T(8,128)S(1)} %collective-permute-done.14.db.refs_3_, ...), custom_call_target="tpu_custom_call" | custom-call | tf_op jit(solution)/shard_map/finish/pallas_call | solution.py:368
  87.0 0.0 collective-permute-done.13.refs_4_
  87.0 2.0 %finish.3 = (f32[8,64,1024]{2,1,0:T(8,128)}, f32[8,64,1024]{2,1,0:T(8,128)}) custom-call(s32[3]{0:T(128)S(1)} %pad_add_fusion.place.refs_0_, f32[2]{0:T(128)S(1)} %copy-done.1, f32[128,1024]{1,0:T(8,128)S(1)} %collective-permute-done.11.da.refs_2_, f32[128,1024]{1,0:T(8,128)S(1)} %collective-permute-done.12.db.refs_3_, ...), custom_call_target="tpu_custom_call", output_to_operand_aliasing={{0}: (6, {}), {1}: (7, {})} | custom-call | tf_op jit(solution)/shard_map/finish/pallas_call | solution.py:368
Async XLA Ops:
  0.6 4.8 %collective-permute-start = (f32[8,64,1024]{2,1,0:T(8,128)}, f32[8,64,1024]{2,1,0:T(8,128)S(1)}, u32[]{:S(2)}, u32[]{:S(2)}) collective-permute-start(f32[8,64,1024]{2,1,0:T(8,128)} %value.1), channel_id=1, source_target_pairs={{0,8},{8,0},{16,24},{24,16},{32,40},{40,32},{48,56},{56,48},{64,72... | collective-permute-start | bytes 6291464 | tf_op jit(solution)/shard_map/ppermute | solution.py:390
  1.5 1.6 %copy-start = (f32[8,64,1024]{2,1,0:T(8,128)S(1)}, f32[8,64,1024]{2,1,0:T(8,128)}, u32[]{:S(2)}) copy-start(f32[8,64,1024]{2,1,0:T(8,128)} %value.1) | copy-start | bytes 6291460
  6.1 18.9 %collective-permute-start.4 = (f32[128,1024]{1,0:T(8,128)S(1)}, f32[128,1024]{1,0:T(8,128)S(1)}, u32[]{:S(2)}, u32[]{:S(2)}) collective-permute-start(f32[128,1024]{1,0:T(8,128)S(1)} %get-tuple-element.46), channel_id=1, source_target_pairs={{0,16},{8,24},{16,32},{24,40},{32,48},{40,56},{48,0},{56,8},{64,80... | collective-permute-start | bytes 1572872 | tf_op jit(solution)/shard_map/ppermute | solution.py:390
  7.5 17.6 %collective-permute-start.5 = (f32[128,1024]{1,0:T(8,128)S(1)}, f32[128,1024]{1,0:T(8,128)S(1)}, u32[]{:S(2)}, u32[]{:S(2)}) collective-permute-start(f32[128,1024]{1,0:T(8,128)S(1)} %get-tuple-element.47), channel_id=1, source_target_pairs={{0,48},{8,56},{16,0},{24,8},{32,16},{40,24},{48,32},{56,40},{64,11... | collective-permute-start | bytes 1572872 | tf_op jit(solution)/shard_map/ppermute | solution.py:390
  9.0 12.8 %collective-permute-start.1 = (f32[8,1024]{1,0:T(8,128)S(1)}, f32[8,1024]{1,0:T(8,128)S(1)}, u32[]{:S(2)}, u32[]{:S(2)}) collective-permute-start(f32[8,1024]{1,0:T(8,128)S(1)} %get-tuple-element.42), channel_id=1, source_target_pairs={{8,16},{16,8},{24,32},{32,24},{40,48},{48,40},{56,64},{64,56},{72,... | collective-permute-start | bytes 98312 | tf_op jit(solution)/shard_map/ppermute | solution.py:404
  11.7 10.7 %copy-start.2 = (f32[511]{0:T(512)S(1)}, f32[511]{0:T(512)}, u32[]{:S(2)}) copy-start(f32[511]{0:T(512)} %param.9) | copy-start | bytes 6136
  11.7 23.5 %collective-permute-start.7 = (f32[128,1024]{1,0:T(8,128)S(1)}, f32[128,1024]{1,0:T(8,128)S(1)}, u32[]{:S(2)}, u32[]{:S(2)}) collective-permute-start(f32[128,1024]{1,0:T(8,128)S(1)} %get-tuple-element.40.p0), channel_id=1, source_target_pairs={{32,96},{40,104},{48,112},{56,120},{64,0},{72,8},{80,16},{88,24},{... | collective-permute-start | bytes 1572872 | tf_op jit(solution)/shard_map/ppermute | solution.py:390
  22.4 2.5 %copy-start.3 = (f32[511]{0:T(512)S(1)}, f32[511]{0:T(512)}, u32[]{:S(2)}) copy-start(f32[511]{0:T(512)} %param.8) | copy-start | bytes 6136
  25.1 15.4 %collective-permute-start.6 = (f32[128,1024]{1,0:T(8,128)S(1)}, f32[128,1024]{1,0:T(8,128)S(1)}, u32[]{:S(2)}, u32[]{:S(2)}) collective-permute-start(f32[128,1024]{1,0:T(8,128)S(1)} %pieces.3), channel_id=1, source_target_pairs={{0,32},{8,40},{16,48},{24,56},{32,0},{40,8},{48,16},{56,24},{64,96... | collective-permute-start | bytes 1572872 | tf_op jit(solution)/shard_map/ppermute | solution.py:390
  28.5 17.6 %collective-permute-start.2 = (f32[8,72,256]{2,1,0:T(8,128)S(1)}, f32[8,72,256]{2,1,0:T(8,128)S(1)}, u32[]{:S(2)}, u32[]{:S(2)}) collective-permute-start(f32[8,72,256]{2,1,0:T(8,128)S(1)} %get-tuple-element.43), channel_id=1, source_target_pairs={{0,1},{1,2},{2,3},{3,4},{4,5},{5,6},{6,7},{8,9},{9,10},{10,11},{11... | collective-permute-start | bytes 1769480 | tf_op jit(solution)/shard_map/ppermute | solution.py:381
  33.2 18.4 %collective-permute-start.3 = (f32[8,72,256]{2,1,0:T(8,128)S(1)}, f32[8,72,256]{2,1,0:T(8,128)S(1)}, u32[]{:S(2)}, u32[]{:S(2)}) collective-permute-start(f32[8,72,256]{2,1,0:T(8,128)S(1)} %get-tuple-element.44), channel_id=1, source_target_pairs={{1,0},{2,1},{3,2},{4,3},{5,4},{6,5},{7,6},{9,8},{10,9},{11,10},{12... | collective-permute-start | bytes 1769480 | tf_op jit(solution)/shard_map/ppermute | solution.py:381
  35.2 19.1 %collective-permute-start.8 = (f32[128,1024]{1,0:T(8,128)S(1)}, f32[128,1024]{1,0:T(8,128)S(1)}, u32[]{:S(2)}, u32[]{:S(2)}) collective-permute-start(f32[128,1024]{1,0:T(8,128)S(1)} %collective-permute-done.4.p1), channel_id=1, source_target_pairs={{0,64},{8,72},{48,112},{56,120},{64,128},{72,136},{80,16},{88,24},... | collective-permute-start | bytes 1572872 | tf_op jit(solution)/shard_map/ppermute | solution.py:390
  38.3 16.0 %collective-permute-start.9 = (f32[128,1024]{1,0:T(8,128)S(1)}, f32[128,1024]{1,0:T(8,128)S(1)}, u32[]{:S(2)}, u32[]{:S(2)}) collective-permute-start(f32[128,1024]{1,0:T(8,128)S(1)} %collective-permute-done.5.p3), channel_id=1, source_target_pairs={{16,80},{24,88},{32,96},{40,104},{64,0},{72,8},{80,144},{88,152},{... | collective-permute-start | bytes 1572872 | tf_op jit(solution)/shard_map/ppermute | solution.py:390
  40.5 21.7 %collective-permute-start.10 = (f32[128,1024]{1,0:T(8,128)S(1)}, f32[128,1024]{1,0:T(8,128)S(1)}, u32[]{:S(2)}, u32[]{:S(2)}) collective-permute-start(f32[128,1024]{1,0:T(8,128)S(1)} %collective-permute-done.6.p2), channel_id=1, source_target_pairs={{0,64},{8,72},{16,80},{24,88},{64,128},{72,136},{80,144},{88,152},... | collective-permute-start | bytes 1572872 | tf_op jit(solution)/shard_map/ppermute | solution.py:390
  54.3 3.1 %copy-start.1 = (f32[2]{0:T(128)S(1)}, f32[2]{0:T(128)}, u32[]{:S(2)}) copy-start(f32[2]{0:T(128)} %refs_1_.3) | copy-start | bytes 28
  54.3 3.1 %copy-start.4 = (f32[3]{0:T(128)S(1)}, f32[3]{0:T(128)}, u32[]{:S(2)}) copy-start(f32[3]{0:T(128)} %diffusion.1) | copy-start | bytes 40
  54.3 3.1 %copy-start.5 = (f32[3]{0:T(128)S(1)}, f32[3]{0:T(128)}, u32[]{:S(2)}) copy-start(f32[3]{0:T(128)} %drift.1) | copy-start | bytes 40
  57.1 14.9 %collective-permute-start.14 = (f32[128,1024]{1,0:T(8,128)S(1)}, f32[128,1024]{1,0:T(8,128)S(1)}, u32[]{:S(2)}, u32[]{:S(2)}) collective-permute-start(f32[128,1024]{1,0:T(8,128)S(1)} %get-tuple-element.58), channel_id=1, source_target_pairs={{0,32},{8,40},{16,48},{24,56},{32,0},{40,8},{48,16},{56,24},{64,96... | collective-permute-start | bytes 1572872 | tf_op jit(solution)/shard_map/ppermute | solution.py:390
  63.7 18.1 %collective-permute-start.11 = (f32[128,1024]{1,0:T(8,128)S(1)}, f32[128,1024]{1,0:T(8,128)S(1)}, u32[]{:S(2)}, u32[]{:S(2)}) collective-permute-start(f32[128,1024]{1,0:T(8,128)S(1)} %get-tuple-element.67), channel_id=1, source_target_pairs={{0,48},{8,56},{16,0},{24,8},{32,16},{40,24},{48,32},{56,40},{64,11... | collective-permute-start | bytes 1572872 | tf_op jit(solution)/shard_map/ppermute | solution.py:390
  67.9 15.6 %collective-permute-start.12 = (f32[128,1024]{1,0:T(8,128)S(1)}, f32[128,1024]{1,0:T(8,128)S(1)}, u32[]{:S(2)}, u32[]{:S(2)}) collective-permute-start(f32[128,1024]{1,0:T(8,128)S(1)} %get-tuple-element.68), channel_id=1, source_target_pairs={{0,16},{8,24},{16,32},{24,40},{32,48},{40,56},{48,0},{56,8},{64,80... | collective-permute-start | bytes 1572872 | tf_op jit(solution)/shard_map/ppermute | solution.py:390
  72.5 12.6 %collective-permute-start.15 = (f32[2,64,1024]{2,1,0:T(8,128)S(1)}, f32[2,64,1024]{2,1,0:T(8,128)S(1)}, u32[]{:S(2)}, u32[]{:S(2)}) collective-permute-start(f32[2,64,1024]{2,1,0:T(8,128)S(1)} %swap.3), channel_id=1, source_target_pairs={{0,8},{8,0},{16,24},{24,16},{32,40},{40,32},{48,56},{56,48},{64,72... | collective-permute-start | bytes 1572872 | tf_op jit(solution)/shard_map/ppermute | solution.py:390
  84.1 2.9 %collective-permute-start.13 = (f32[2,64,1024]{2,1,0:T(8,128)S(1)}, f32[2,64,1024]{2,1,0:T(8,128)S(1)}, u32[]{:S(2)}, u32[]{:S(2)}) collective-permute-start(f32[2,64,1024]{2,1,0:T(8,128)S(1)} %swap.2), channel_id=1, source_target_pairs={{0,8},{8,0},{16,24},{24,16},{32,40},{40,32},{48,56},{56,48},{64,72... | collective-permute-start | bytes 1572872 | tf_op jit(solution)/shard_map/ppermute | solution.py:390

commit v3 on v2

--- a/solution.py
+++ b/solution.py
@@ -81,7 +81,8 @@
 
 
 def local_kernel(
-    intensity, diffusion, drift, cross, value, low, high, above, below, within, taps_hi, taps_lo, jump_ref, part_ref
+    place, intensity, diffusion, drift, cross, value, low, high, beside, edge, within, taps_hi, taps_lo,
+    jump_ref, part_ref, frame,
 ):
     planes, rows, cols = value.shape
     jump_ref[...] = within[...]
@@ -101,15 +102,19 @@
         left = jnp.where(lane == 0, first, pltpu.roll(x, 1, 1))
         return right, left
 
+    core = place[2]
+    frame[core] = edge[...]
+    frame[1 - core] = beside[...]
+    edges = []
+    for i in range(2):
+        middle = frame[i, :, EDGE : EDGE + cols]
+        right, left = along(middle, frame[i, :, EDGE - 1 : EDGE], frame[i, :, EDGE + cols : EDGE + cols + 1])
+        edges.append((middle, right - left))
+    above_terms = (row_diff - row_drift) * edges[0][0] - mixed * edges[0][1]
+    below_terms = (row_diff + row_drift) * edges[1][0] + mixed * edges[1][1]
     line = lax.broadcasted_iota(jnp.int32, (rows, cols), 0)
     for p in range(planes):
-        edges = []
-        for edge, row in ((above, rows), (below, rows + 1)):
-            middle = edge[p : p + 1]
-            right, left = along(middle, low[p, row : row + 1, BLOCK - 1 :], high[p, row : row + 1, :1])
-            edges.append((middle, right - left))
-        above_term = (row_diff - row_drift) * edges[0][0] - mixed * edges[0][1]
-        below_term = (row_diff + row_drift) * edges[1][0] + mixed * edges[1][1]
+        above_term, below_term = above_terms[p : p + 1], below_terms[p : p + 1]
         x = value[p]
         right, left = along(x, low[p, :rows, BLOCK - 1 :], high[p, :rows, :1])
         slope = right - left
@@ -127,43 +132,34 @@
         part_ref[p] = out + intensity[1] * jump_ref[p]
 
 
-def local_part(intensity, diffusion, drift, cross, value, low, high, above, below, within, taps):
-    planes, rows, cols = value.shape
-    return pl.pallas_call(
-        local_kernel, out_shape=(f32(*value.shape),) * 2, in_specs=[SMEM] * 4 + [VMEM] * 8, out_specs=(VMEM, VMEM),
-        compiler_params=params(6),
-        name="side_columns_and_stencil",
-    )(intensity, diffusion, drift, cross, value, low, high, above, below, within, *taps)
-
-
-def tails_kernel(place, value, other, edge, high_side, low_side, above, below):
+def local_part(place, intensity, diffusion, drift, cross, value, low, high, beside, edge, within, taps):
+    planes, rows, cols = value.shape
+    return pl.pallas_call(
+        local_kernel, out_shape=(f32(*value.shape),) * 2, in_specs=[SMEM] * 5 + [VMEM] * 8, out_specs=(VMEM, VMEM),
+        scratch_shapes=[pltpu.VMEM((2, planes, cols + 2 * EDGE), jnp.float32)],
+        compiler_params=params(6), name="side_columns_and_stencil",
+    )(place, intensity, diffusion, drift, cross, value, low, high, beside, edge, within, *taps)
+
+
+def lines_kernel(place, value, low, high, outer, inner):
     planes, rows, cols = value.shape
     for core in range(CORES):
 
         @pl.when(place[2] == core)
         def _():
-            for p in range(planes):
-                line = slice(p, p + 1)
-                above[line] = other[p, rows - 1 :, :] if core else edge[line]
-                below[line] = edge[line] if core else other[p, :1, :]
-
-    for out, start in ((high_side, cols - BLOCK), (low_side, 0)):
-        columns = slice(start, start + BLOCK)
-        out[:, :rows] = value[:, :, columns]
-        for p in range(planes):
-            out[p, rows : rows + 1] = above[p : p + 1, columns]
-            out[p, rows + 1 : rows + 2] = below[p : p + 1, columns]
-            out[p, rows + 2 :] = jnp.zeros((out.shape[1] - rows - 2, BLOCK), jnp.float32)
-
-
-def tails_part(place, value, other, edge):
-    planes, rows, cols = value.shape
-    side = f32(planes, rows + 8, BLOCK)
-    return pl.pallas_call(
-        tails_kernel, out_shape=[side, side, f32(planes, cols), f32(planes, cols)], in_specs=[SMEM] + [VMEM] * 3,
-        out_specs=[VMEM] * 4, compiler_params=params(4),
-        name="tails",
-    )(place, value, other, edge)
+            for out, row in ((outer, (rows - 1) * core), (inner, (rows - 1) * (1 - core))):
+                for p in range(planes):
+                    out[p : p + 1, :EDGE] = low[p, row : row + 1, BLOCK - EDGE :]
+                    out[p : p + 1, EDGE : EDGE + cols] = value[p, row : row + 1, :]
+                    out[p : p + 1, EDGE + cols :] = high[p, row : row + 1, :EDGE]
+
+
+def lines_part(place, value, low, high):
+    planes, _, cols = value.shape
+    return pl.pallas_call(
+        lines_kernel, out_shape=[f32(planes, cols + 2 * EDGE)] * 2, in_specs=[SMEM] + [VMEM] * 3,
+        out_specs=[VMEM] * 2, compiler_params=params(4), name="lines",
+    )(place, value, low, high)
 
 
 def taps_kernel(weights, high_ref, low_ref, total_ref, wide):
@@ -179,26 +175,21 @@
     )(weights)
 
 
-def load_kernel(place, value, held, line, done):
+def load_kernel(value, held, high_side, low_side, done):
     copy = pltpu.make_async_copy(value, held, done)
     copy.start()
     copy.wait()
-    planes, rows, _ = value.shape
-    for core, row in ((0, 0), (1, rows - 1)):
-
-        @pl.when(place[2] == core)
-        def _():
-            for p in range(planes):
-                line[p : p + 1] = held[p, row : row + 1, :]
-
-
-def load_part(place, value):
-    planes, _, cols = value.shape
-    return pl.pallas_call(
-        load_kernel, out_shape=[f32(*value.shape), f32(planes, cols)],
-        in_specs=[SMEM, pl.BlockSpec(memory_space=pl.ANY)], out_specs=[VMEM] * 2,
-        scratch_shapes=[pltpu.SemaphoreType.DMA], compiler_params=params(4), name="load",
-    )(place, value)
+    cols = value.shape[2]
+    high_side[...] = held[:, :, cols - BLOCK :]
+    low_side[...] = held[:, :, :BLOCK]
+
+
+def load_part(value):
+    side = f32(*value.shape[:2], BLOCK)
+    return pl.pallas_call(
+        load_kernel, out_shape=[f32(*value.shape), side, side], in_specs=[pl.BlockSpec(memory_space=pl.ANY)],
+        out_specs=[VMEM] * 3, scratch_shapes=[pltpu.SemaphoreType.DMA], compiler_params=params(4), name="load",
+    )(value)
 
 
 def pieces_kernel(steps, place, value, other, *refs):
@@ -261,98 +252,85 @@
     )(place, p0, p1, p3, *taps)
 
 
-def middle_kernel(place, near, p2, x0, x1, x3, taps_hi, taps_lo, total, out, opposite, hold):
-    y = place[1]
+def gather_halo(y, pieces, hold):
+    for k, piece in pieces:
+        hold[part_of(ring(y, -k), piece.shape[0])] = piece[...]
+
+
+def opposite_kernel(place, near, p2, x0, x1, x3, taps_hi, taps_lo, total, same, other, hold):
+    y, core = place[1], place[2]
+    size, rows = p2.shape[0], same.shape[0]
+    at = ring(y, -2)
+    gather_halo(y, ((0, x0), (1, x1), (3, x3)), hold)
+    hold[part_of(at, size)] = jnp.zeros_like(p2)
+    pair, half = lax.div(at, 2), lax.rem(at, 2)
+    lines = part_of(half, HALF)
+    near_taps = tuple(t[lines, part_of(2 + half, HALF)] for t in (taps_hi, taps_lo))
+    far_taps = tuple(t[lines, part_of(2 * pair, BLOCK)] for t in (taps_hi, taps_lo))
+    dims = ((1,), (0,))
+    out = (
+        near[part_of(at, size)]
+        + product(near_taps, split(p2[...]), dims)
+        + product(far_taps, split(hold[part_of(1 - pair, BLOCK)]), dims)
+        - total[0:1, 0:1] * p2[...]
+    )
+    hold[:size] = out
+    same[...] = hold[part_of(core, rows)]
+    other[...] = hold[part_of(1 - core, rows)]
+
+
+def opposite_part(place, near, p2, x0, x1, x3, taps):
+    rows, cols = near.shape
+    return pl.pallas_call(
+        opposite_kernel, out_shape=[f32(rows // RING // CORES, cols)] * 2, in_specs=[SMEM] + [VMEM] * 8,
+        out_specs=[VMEM] * 2, scratch_shapes=[pltpu.VMEM((rows, cols), jnp.float32)], compiler_params=params(9),
+        name="opposite_rows",
+    )(place, near, p2, x0, x1, x3, *taps)
+
+
+def others_kernel(
+    place, near, p2, x0, x1, x2, x3, taps_hi, taps_lo, same0, other0, same1, other1, same3, other3, hold, total
+):
+    y, core = place[1], place[2]
     taps = (taps_hi, taps_lo)
-    size = p2.shape[0]
+    size, rows = p2.shape[0], same0.shape[0]
     at = ring(y, -2)
     dims = ((1,), (0,))
-    for k, piece in ((0, x0), (1, x1), (3, x3)):
-        hold[part_of(ring(y, -k), size)] = piece[...]
-    hold[part_of(at, size)] = jnp.zeros_like(p2)
+    gather_halo(y, ((0, x0), (1, x1), (2, x2), (3, x3)), hold)
     rows2 = split(p2[...])
     below, above = split(hold[:BLOCK]), split(hold[BLOCK:])
     for i, far, tile in ((0, above, 0), (1, below, 2 * BLOCK)):
         column = part_of(at + 2 - 2 * i, HALF)
-        mine = tuple(t[:, column] for t in taps)
-        out[i * BLOCK : (i + 1) * BLOCK] = (
+        total[i * BLOCK : (i + 1) * BLOCK] = (
             near[i * BLOCK : (i + 1) * BLOCK]
-            + product(mine, rows2, dims)
+            + product(tuple(t[:, column] for t in taps), rows2, dims)
             + product(tap_tile(taps, tile, BLOCK), far, dims)
         )
-    mid = out[part_of(at, size)] - total[0:1, 0:1] * p2[...]
-    out[part_of(at, size)] = mid
-    opposite[...] = mid
-
-
-def middle_part(place, near, p2, x0, x1, x3, taps):
+    for k, same, other in ((0, same0, other0), (1, same1, other1), (3, same3, other3)):
+        first = CORES * ring(y, -k)
+        same[...] = total[part_of(first + core, rows)]
+        other[...] = total[part_of(first + 1 - core, rows)]
+
+
+def others_part(place, near, p2, x0, x1, x2, x3, taps):
     rows, cols = near.shape
-    size = rows // RING
-    return pl.pallas_call(
-        middle_kernel, out_shape=(f32(rows, cols), f32(size, cols)), in_specs=[SMEM] + [VMEM] * 8,
-        out_specs=(VMEM, VMEM), scratch_shapes=[pltpu.VMEM((rows, cols), jnp.float32)],
-        compiler_params=params(9),
-        name="middle_rows",
-    )(place, near, p2, x0, x1, x3, *taps)
-
-
-def last_kernel(place, middle, x2, taps_hi, taps_lo, b0, b1, b3, hold):
-    y = place[1]
-    taps = (taps_hi, taps_lo)
-    size = x2.shape[0]
-    at = ring(y, -2)
-    dims = ((1,), (0,))
-    hold[...] = middle[...]
-    far = split(x2[...])
-
-    @pl.when(at >= RING // 2)
-    def _():
-        column = part_of(at - RING // 2, HALF)
-        hold[:BLOCK] += product(tuple(t[:, column] for t in taps), far, dims)
-
-    @pl.when(at < RING // 2)
-    def _():
-        column = part_of(at + RING, HALF)
-        hold[BLOCK:] += product(tuple(t[:, column] for t in taps), far, dims)
-
-    for k, out in ((0, b0), (1, b1), (3, b3)):
-        out[...] = hold[part_of(ring(y, -k), size)]
-
-
-def last_part(place, middle, x2, taps):
-    rows, cols = middle.shape
-    return pl.pallas_call(
-        last_kernel, out_shape=[f32(rows // RING, cols)] * 3, in_specs=[SMEM] + [VMEM] * 4, out_specs=[VMEM] * 3,
-        scratch_shapes=[pltpu.VMEM((rows, cols), jnp.float32)], compiler_params=params(9), name="last_rows",
-    )(place, middle, x2, *taps[:2])
-
-
-def swap_kernel(place, da, db, out):
-    rows = out.shape[1]
-    for k, source in enumerate((da, db)):
-        out[k] = source[part_of(1 - place[2], rows)]
-
-
-def swap_part(place, da, db):
-    rows, cols = da.shape
-    return pl.pallas_call(
-        swap_kernel, out_shape=f32(2, rows // CORES, cols), in_specs=[SMEM] + [VMEM] * 2, out_specs=VMEM,
-        compiler_params=params(8), name="swap",
-    )(place, da, db)
-
-
-def finish_kernel(steps, place, intensity, da, db, other, part, *refs):
+    scratch = pltpu.VMEM((rows, cols), jnp.float32)
+    return pl.pallas_call(
+        others_kernel, out_shape=[f32(rows // RING // CORES, cols)] * 6, in_specs=[SMEM] + [VMEM] * 8,
+        out_specs=[VMEM] * 6, scratch_shapes=[scratch, scratch], compiler_params=params(10), name="other_rows",
+    )(place, near, p2, x0, x1, x2, x3, *taps[:2])
+
+
+def finish_kernel(steps, place, intensity, same1, other1, same2, other2, part, *refs):
     updated, jump, new_updated, new_jump, done = refs[-5:]
     y, core = place[1], place[2]
-    rows = other.shape[1]
     copies = []
-    for i, (step, source) in enumerate(zip(steps, (da, db))):
-        for j in range(CORES):
+    for i, (step, blocks) in enumerate(zip(steps, ((same1, other1), (same2, other2)))):
+        for j, block in enumerate(blocks):
             at = CORES * i + j
             plane = CORES * ring(y, step) + (1 - core if j else core)
-            block = other[i] if j else source[part_of(core, rows)]
-            new_jump[at] = block
-            new_updated[at] = part[plane] + intensity[0] * block
+            new_jump[at] = block[...]
+            new_updated[at] = part[plane] + intensity[0] * block[...]
             for k, (new, out) in enumerate(((new_jump, jump), (new_updated, updated))):
                 copy = pltpu.make_async_copy(new.at[at], out.at[plane], done.at[at, k])
                 copy.start()
@@ -361,17 +339,17 @@
         copy.wait()
 
 
-def finish_part(steps, place, intensity, da, db, other, part, results):
+def finish_part(steps, place, intensity, blocks, part, results):
     planes, rows, cols = part.shape
     anywhere = pl.BlockSpec(memory_space=pl.ANY)
     scratch = pltpu.VMEM((2 * CORES, rows, cols), jnp.float32)
     return pl.pallas_call(
         lambda *refs: finish_kernel(steps, *refs),
-        out_shape=[f32(*part.shape)] * 2, in_specs=[SMEM, SMEM] + [VMEM] * 4 + [anywhere] * len(results),
+        out_shape=[f32(*part.shape)] * 2, in_specs=[SMEM, SMEM] + [VMEM] * 5 + [anywhere] * len(results),
         out_specs=[anywhere] * 2, scratch_shapes=[scratch, scratch, pltpu.SemaphoreType.DMA((2 * CORES, 2))],
-        input_output_aliases={6: 0, 7: 1} if results else {},
+        input_output_aliases={7: 0, 8: 1} if results else {},
         compiler_params=params(8), name="finish",
-    )(place, intensity, da, db, other, part, *results)
+    )(place, intensity, *blocks, part, *results)
 
 
 def neighbours(low_side, high_side, axis):
@@ -390,8 +368,8 @@
     return lax.ppermute(block, "gx", route)
 
 
-def to_ring(block, step):
-    return send(block, lambda x, y, core: (x, y + step, core))
+def to_ring(block, step, flip=False):
+    return send(block, lambda x, y, core: (x, y + step, 1 - core if flip else core))
 
 
 def to_other_core(block):
@@ -419,31 +397,30 @@
     place = jnp.stack([lax.div(chip, RING), lax.rem(chip, RING), lax.rem(me, CORES)])
 
     other = to_other_core(value)
-    value, line = load_part(place, value)
-    edge = across_chips(line)
-
-    s1, s3, p0 = pieces_part((1, 3, 0), place, value, other)
+    value, high_side, low_side = load_part(value)
+
+    s1, s3, p0, s2 = pieces_part((1, 3, 0, 2), place, value, other)
     p1, p3, x0 = to_ring(s1, 1), to_ring(s3, 3), to_group(p0, 0)
-    (s2,) = pieces_part((2,), after(place, p0, edge), value, other)
+    low, high = neighbours(after(low_side, p0), after(high_side, p0), "gy")
     within, col_hi, col_lo, _ = within_part(value, after(kernel_cols[None], s2))
     taps = taps_part(after(kernel_rows[None], within))
     p2 = to_ring(after(s2, p1, p3, taps[2]), 2)
-    x1, x3 = to_group(after(p1, x0), 1), to_group(after(p3, x0), 3)
-    high_side, low_side, above, below = tails_part(after(place, p0), value, other, edge)
-    low, high = neighbours(low_side, high_side, "gy")
-    near = near_part(after(place, low, high), p0, p1, p3, taps)
-    x2 = to_group(p2, 2)
-    middle, b2 = middle_part(place, near, p2, x0, x1, x3, taps)
-    d2 = to_ring(b2, -2)
+    x1, x3 = to_group(after(p1, low, high), 1), to_group(after(p3, x0), 3)
+    outer, inner = lines_part(after(place, p1), value, low, high)
+    edge, beside = across_chips(outer), to_other_core(inner)
+    near = near_part(after(place, outer), p0, p1, p3, taps)
+    x2 = to_group(after(p2, near), 2)
+    b2, o2 = opposite_part(place, near, p2, x0, x1, x3, taps)
+    d2, o2 = to_ring(b2, -2), to_ring(o2, -2, True)
+    b0, o0, b1, o1, b3, o3 = others_part(place, near, p2, x0, x1, x2, x3, taps)
+    d1, d3 = to_ring(b1, -1), to_ring(b3, -3)
+    o1, o3 = to_ring(o1, -1, True), to_ring(o3, -3, True)
+    o0 = to_other_core(o0)
     jump_cols, part = local_part(
-        after(intensity, b2), diffusion, drift, cross, value, low, high, above, below, within, (col_hi, col_lo)
-    )
-    b0, b1, b3 = last_part(after(place, part), middle, x2, taps)
-    d1, d3 = to_ring(b1, -1), to_ring(b3, -3)
-    swapped = to_other_core(swap_part(place, b0, d2))
-    results = finish_part((0, 2), place, intensity, b0, d2, swapped, part, ())
-    swapped = to_other_core(swap_part(place, d1, d3))
-    updated, jump_rows = finish_part((1, 3), place, intensity, d1, d3, swapped, part, results)
+        place, after(intensity, b0), diffusion, drift, cross, value, low, high, beside, edge, within, (col_hi, col_lo)
+    )
+    results = finish_part((0, 2), place, intensity, (b0, o0, d2, o2), part, ())
+    updated, jump_rows = finish_part((1, 3), place, intensity, (d1, o1, d3, o3), part, results)
     return updated, jump_rows, jump_cols
 
 

time: 89.5 us -> 83 us (0.927)
  waiting for transfers between devices: 29.8 us -> 18.9 us
  starting transfers between devices: 33.9 us -> 40 us
  Pallas kernels: 22.1 us -> 20.5 us
    ppermute x1, waiting for transfers between devices: 7.92 us -> 2.71 us  [across_chips(): return lax.ppermute(line, 'gx', route)]
    ppermute x1, waiting for transfers between devices: 5.56 us -> 2.09 us  [neighbours(): lax.ppermute(low_side, axis, backward)]
    ppermute x1, starting transfers between devices: 2.65 us -> 5.84 us  [across_chips(): return lax.ppermute(line, 'gx', route)]
    ppermute x13 -> x16, starting transfers between devices: 24.5 us -> 27.5 us  [send(): return lax.ppermute(block, 'gx', route)]
    pallas_call x6 -> x4, Pallas kernels: 6.7 us -> 4.92 us  [the longest x1 2.8 us: others_part(): pl.pallas_call(others_kernel, out_shape=[f32(rows // RING // CORES, cols)...]
    ppermute x13 -> x16, waiting for transfers between devices: 14.5 us -> 13.2 us  [send(): return lax.ppermute(block, 'gx', route)]
    ppermute x1, waiting for transfers between devices: 1.78 us -> 0.86 us  [neighbours(): lax.ppermute(high_side, axis, forward)]
    pallas_call x2 -> x1, Pallas kernels: 1.34 us -> 1.85 us  [pieces_part(): pl.pallas_call(lambda *refs: pieces_kernel(steps, *refs), out_shape=[f32(...]
  transfers between devices with their start and end apart: 16 -> 19, of which waited for: 7 -> 10; matrix products, arithmetic and copies ran while one was open for 0% -> 0% of each run, Pallas kernels for 22% -> 20%
where the time goes in v3:
time: 83 us; the launch traced here: 82.7 us
  starting transfers between devices  40 us (48%)
  Pallas kernels  20.5 us (25%)
  waiting for transfers between devices  18.9 us (23%)
  between operations  1.67 us (2%)
  local copies, waits for them, and re-layouts  1.61 us (2%)
    ppermute x16, starting transfers between devices, send(): return lax.ppermute(block, 'gx', route)  27.5 us
    ppermute x16, waiting for transfers between devices, send(): return lax.ppermute(block, 'gx', route)  13.2 us
    ppermute x1, starting transfers between devices, across_chips(): return lax.ppermute(line, 'gx', route)  5.84 us
    ppermute x1, starting transfers between devices, neighbours(): lax.ppermute(high_side, axis, forward)  4.76 us
    pallas_call x1, Pallas kernels, local_part(): pl.pallas_call(local_kernel, out_shape=(f32(*value.shape),) * 2, in_specs...  4.61 us
    pallas_call x2, Pallas kernels, finish_part(): pl.pallas_call(lambda *refs: finish_kernel(steps, *refs), out_shape=[f32(...  3.87 us
    pallas_call x1, Pallas kernels, others_part(): pl.pallas_call(others_kernel, out_shape=[f32(rows // RING // CORES, cols)...  2.8 us
    ppermute x1, waiting for transfers between devices, across_chips(): return lax.ppermute(line, 'gx', route)  2.71 us
  transfers between devices with their start and end apart: 19, of which 10 were waited for; matrix products, arithmetic and copies ran while one was open for 0% of the time, Pallas kernels for 20%

profile of v3, /device:TPU:99, one launch (start us, length us, event | category | flops | bytes accessed | tf_op | source)
XLA Modules:
  0.0 82.7 jit_solution(7348630303287627075)
XLA Ops:
  0.6 0.8 collective-permute-start
  1.4 0.0 copy-start
  1.4 1.6 %copy-done = f32[8,64,1024]{2,1,0:T(8,128)S(1)} copy-done((f32[8,64,1024]{2,1,0:T(8,128)S(1)}, f32[8,64,1024]{2,1,0:T(8,128)}, u32[]{:S(2)}) %copy-start) | copy-done | bytes 2097176
  3.0 0.2 load.1
  3.2 0.1 pad_add_fusion.refs_0_.place
  3.3 2.2 %collective-permute-done.refs_2_ = f32[8,64,1024]{2,1,0:T(8,128)} collective-permute-done((f32[8,64,1024]{2,1,0:T(8,128)}, f32[8,64,1024]{2,1,0:T(8,128)}, u32[]{:S(2)}, u32[]{:S(2)}) %collective-permute-start) | collective-permute-done | bytes 2097184 | tf_op jit(solution)/shard_map/ppermute | solution.py:368
  5.5 0.0 copy-start.2
  5.5 1.8 %pieces.1 = (f32[128,1024]{1,0:T(8,128)S(1)}, f32[128,1024]{1,0:T(8,128)S(1)}, f32[128,1024]{1,0:T(8,128)S(1)}, f32[128,1024]{1,0:T(8,128)S(1)}) custom-call(s32[3]{0:T(128)S(1)} %pad_add_fusion.refs_0_.place, f32[8,64,1024]{2,1,0:T(8,128)S(1)} %get-tuple-element.43.refs_1_.value, f32[8,64,1024]{2,1,0:T(8,128)} %collective-permute-done.refs_2_), custom_call_target="tpu_custom_call" | custom-call | tf_op jit(solution)/shard_map/pieces/pallas_call | solution.py:213
  7.4 0.0 copy-start.3
  7.4 1.4 %collective-permute-start.1 = (f32[128,1024]{1,0:T(8,128)S(1)}, f32[128,1024]{1,0:T(8,128)S(1)}, u32[]{:S(2)}, u32[]{:S(2)}) collective-permute-start(f32[128,1024]{1,0:T(8,128)S(1)} %get-tuple-element.44), channel_id=1, source_target_pairs={{0,16},{8,24},{16,32},{24,40},{32,48},{40,56},{48,0},{56,8},{64,80... | collective-permute-start | bytes 1572872 | tf_op jit(solution)/shard_map/ppermute | solution.py:368
  8.8 1.5 %collective-permute-start.4 = (f32[128,1024]{1,0:T(8,128)S(1)}, f32[128,1024]{1,0:T(8,128)S(1)}, u32[]{:S(2)}, u32[]{:S(2)}) collective-permute-start(f32[128,1024]{1,0:T(8,128)S(1)} %get-tuple-element.53), channel_id=1, source_target_pairs={{0,48},{8,56},{16,0},{24,8},{32,16},{40,24},{48,32},{56,40},{64,11... | collective-permute-start | bytes 1572872 | tf_op jit(solution)/shard_map/ppermute | solution.py:368
  10.3 1.9 %collective-permute-start.3 = (f32[8,64,256]{2,1,0:T(8,128)S(1)}, f32[8,64,256]{2,1,0:T(8,128)S(1)}, u32[]{:S(2)}, u32[]{:S(2)}) collective-permute-start(f32[8,64,256]{2,1,0:T(8,128)S(1)} %get-tuple-element.50), channel_id=1, source_target_pairs={{1,0},{2,1},{3,2},{4,3},{5,4},{6,5},{7,6},{9,8},{10,9},{11,10},{12... | collective-permute-start | bytes 1572872 | tf_op jit(solution)/shard_map/ppermute | solution.py:359
  12.2 4.8 %collective-permute-start.2 = (f32[8,64,256]{2,1,0:T(8,128)S(1)}, f32[8,64,256]{2,1,0:T(8,128)S(1)}, u32[]{:S(2)}, u32[]{:S(2)}) collective-permute-start(f32[8,64,256]{2,1,0:T(8,128)S(1)} %get-tuple-element.48), channel_id=1, source_target_pairs={{0,1},{1,2},{2,3},{3,4},{4,5},{5,6},{6,7},{8,9},{9,10},{10,11},{11... | collective-permute-start | bytes 1572872 | tf_op jit(solution)/shard_map/ppermute | solution.py:359
  17.0 2.2 %collective-permute-start.6 = (f32[128,1024]{1,0:T(8,128)S(1)}, f32[128,1024]{1,0:T(8,128)S(1)}, u32[]{:S(2)}, u32[]{:S(2)}) collective-permute-start(f32[128,1024]{1,0:T(8,128)S(1)} %get-tuple-element.47.p0), channel_id=1, source_target_pairs={{32,96},{40,104},{48,112},{56,120},{64,0},{72,8},{80,16},{88,24},{... | collective-permute-start | bytes 1572872 | tf_op jit(solution)/shard_map/ppermute | solution.py:368
  19.1 0.0 copy-done.2
  19.2 2.4 %own_columns.1 = (f32[8,64,1024]{2,1,0:T(8,128)S(1)}, bf16[256,768]{1,0:T(8,128)(2,1)S(1)}, bf16[256,768]{1,0:T(8,128)(2,1)S(1)}, f32[8,128]{1,0:T(8,128)}) custom-call(f32[8,64,1024]{2,1,0:T(8,128)S(1)} %get-tuple-element.43.refs_1_.value, f32[1,511]{1,0:T(1,128)S(1)} %bitcast.5), custom_call_target="tpu_custom_call" | custom-call | tf_op jit(solution)/shard_map/own_columns/pallas_call | solution.py:76
  21.5 0.0 copy-done.3
  21.5 0.2 row_taps.1
  21.7 0.2 collective-permute-done.1.p1
  21.9 0.0 collective-permute-done.4.p3
  21.9 2.4 %collective-permute-start.5 = (f32[128,1024]{1,0:T(8,128)S(1)}, f32[128,1024]{1,0:T(8,128)S(1)}, u32[]{:S(2)}, u32[]{:S(2)}) collective-permute-start(f32[128,1024]{1,0:T(8,128)S(1)} %get-tuple-element.61), channel_id=1, source_target_pairs={{0,32},{8,40},{16,48},{24,56},{32,0},{40,8},{48,16},{56,24},{64,96... | collective-permute-start | bytes 1572872 | tf_op jit(solution)/shard_map/ppermute | solution.py:368
  24.4 2.1 %collective-permute-done.3.high = f32[8,64,256]{2,1,0:T(8,128)S(1)} collective-permute-done((f32[8,64,256]{2,1,0:T(8,128)S(1)}, f32[8,64,256]{2,1,0:T(8,128)S(1)}, u32[]{:S(2)}, u32[]{:S(2)}) %collective-permute-start.3) | collective-permute-done | bytes 524320 | tf_op jit(solution)/shard_map/ppermute | solution.py:359
  26.4 0.9 %collective-permute-done.2.low = f32[8,64,256]{2,1,0:T(8,128)S(1)} collective-permute-done((f32[8,64,256]{2,1,0:T(8,128)S(1)}, f32[8,64,256]{2,1,0:T(8,128)S(1)}, u32[]{:S(2)}, u32[]{:S(2)}) %collective-permute-start.2) | collective-permute-done | bytes 524320 | tf_op jit(solution)/shard_map/ppermute | solution.py:359
  27.3 3.1 %collective-permute-start.7 = (f32[128,1024]{1,0:T(8,128)S(1)}, f32[128,1024]{1,0:T(8,128)S(1)}, u32[]{:S(2)}, u32[]{:S(2)}) collective-permute-start(f32[128,1024]{1,0:T(8,128)S(1)} %collective-permute-done.1.p1), channel_id=1, source_target_pairs={{0,64},{8,72},{48,112},{56,120},{64,128},{72,136},{80,16},{88,24},... | collective-permute-start | bytes 1572872 | tf_op jit(solution)/shard_map/ppermute | solution.py:368
  30.4 0.7 collective-permute-done.6.x0
  31.1 2.2 %collective-permute-start.9 = (f32[128,1024]{1,0:T(8,128)S(1)}, f32[128,1024]{1,0:T(8,128)S(1)}, u32[]{:S(2)}, u32[]{:S(2)}) collective-permute-start(f32[128,1024]{1,0:T(8,128)S(1)} %collective-permute-done.4.p3), channel_id=1, source_target_pairs={{16,80},{24,88},{32,96},{40,104},{64,0},{72,8},{80,144},{88,152},{... | collective-permute-start | bytes 1572872 | tf_op jit(solution)/shard_map/ppermute | solution.py:368
  33.3 0.6 lines.1
  33.9 2.7 %near_rows.1.near = f32[512,1024]{1,0:T(8,128)S(1)} custom-call(s32[3]{0:T(128)S(1)} %pad_add_fusion.refs_0_.place, f32[128,1024]{1,0:T(8,128)S(1)} %get-tuple-element.47.p0, f32[128,1024]{1,0:T(8,128)S(1)} %collective-permute-done.1.p1, f32[128,1024]{1,0:T(8,128)S(1)} %collective-permute-done.4.p3, bf16[256,768]{1,0:T(8,128)(2,1)S(1)} %get-tuple-element.58.taps_hi, ...), custom_call_target="tpu_custom_call" | custom-call | tf_op jit(solution)/shard_map/near_rows/pallas_call | solution.py:249
  36.5 0.0 collective-permute-done.5.p2
  36.6 3.1 %collective-permute-start.8 = (f32[128,1024]{1,0:T(8,128)S(1)}, f32[128,1024]{1,0:T(8,128)S(1)}, u32[]{:S(2)}, u32[]{:S(2)}) collective-permute-start(f32[128,1024]{1,0:T(8,128)S(1)} %collective-permute-done.5.p2), channel_id=1, source_target_pairs={{0,64},{8,72},{16,80},{24,88},{64,128},{72,136},{80,144},{88,152},... | collective-permute-start | bytes 1572872 | tf_op jit(solution)/shard_map/ppermute | solution.py:368
  39.7 1.1 %collective-permute-done.7.x1 = f32[128,1024]{1,0:T(8,128)S(1)} collective-permute-done((f32[128,1024]{1,0:T(8,128)S(1)}, f32[128,1024]{1,0:T(8,128)S(1)}, u32[]{:S(2)}, u32[]{:S(2)}) %collective-permute-start.7) | collective-permute-done | bytes 524320 | tf_op jit(solution)/shard_map/ppermute | solution.py:368
  40.8 3.5 %collective-permute-done.9.x3 = f32[128,1024]{1,0:T(8,128)S(1)} collective-permute-done((f32[128,1024]{1,0:T(8,128)S(1)}, f32[128,1024]{1,0:T(8,128)S(1)}, u32[]{:S(2)}, u32[]{:S(2)}) %collective-permute-start.9) | collective-permute-done | bytes 524320 | tf_op jit(solution)/shard_map/ppermute | solution.py:368
  44.3 1.3 %opposite_rows.1 = (f32[64,1024]{1,0:T(8,128)S(1)}, f32[64,1024]{1,0:T(8,128)S(1)}) custom-call(s32[3]{0:T(128)S(1)} %pad_add_fusion.refs_0_.place, f32[512,1024]{1,0:T(8,128)S(1)} %near_rows.1.near, f32[128,1024]{1,0:T(8,128)S(1)} %collective-permute-done.5.p2, f32[128,1024]{1,0:T(8,128)S(1)} %collective-permute-done.6.x0, ...), custom_call_target="tpu_custom_call" | custom-call | tf_op jit(solution)/shard_map/opposite_rows/pallas_call | solution.py:284
  45.7 1.4 %collective-permute-start.17 = (f32[64,1024]{1,0:T(8,128)S(1)}, f32[64,1024]{1,0:T(8,128)S(1)}, u32[]{:S(2)}, u32[]{:S(2)}) collective-permute-start(f32[64,1024]{1,0:T(8,128)S(1)} %get-tuple-element.76), channel_id=1, source_target_pairs={{0,32},{8,40},{16,48},{24,56},{32,0},{40,8},{48,16},{56,24},{64,96... | collective-permute-start | bytes 786440 | tf_op jit(solution)/shard_map/ppermute | solution.py:368
  47.0 4.9 %collective-permute-start.18 = (f32[64,1024]{1,0:T(8,128)S(1)}, f32[64,1024]{1,0:T(8,128)S(1)}, u32[]{:S(2)}, u32[]{:S(2)}) collective-permute-start(f32[64,1024]{1,0:T(8,128)S(1)} %get-tuple-element.77), channel_id=1, source_target_pairs={{0,40},{8,32},{16,56},{24,48},{32,8},{40,0},{48,24},{56,16},{64,10... | collective-permute-start | bytes 786440 | tf_op jit(solution)/shard_map/ppermute | solution.py:368
  51.9 0.0 copy-start.1
  51.9 0.0 copy-start.4
  51.9 0.0 copy-start.5
  51.9 0.0 collective-permute-start.14
  51.9 5.8 %collective-permute-start.15 = (f32[8,1280]{1,0:T(8,128)S(1)}, f32[8,1280]{1,0:T(8,128)S(1)}, u32[]{:S(2)}, u32[]{:S(2)}) collective-permute-start(f32[8,1280]{1,0:T(8,128)S(1)} %get-tuple-element.51), channel_id=1, source_target_pairs={{8,16},{16,8},{24,32},{32,24},{40,48},{48,40},{56,64},{64,56},{72,... | collective-permute-start | bytes 122888 | tf_op jit(solution)/shard_map/ppermute | solution.py:382
  57.7 0.0 collective-permute-done.8.x2
  57.8 2.8 %other_rows.1 = (f32[64,1024]{1,0:T(8,128)S(1)}, f32[64,1024]{1,0:T(8,128)S(1)}, f32[64,1024]{1,0:T(8,128)S(1)}, f32[64,1024]{1,0:T(8,128)S(1)}, f32[64,1024]{1,0:T(8,128)S(1)}, /*index=5*/f32[64,1024]{1,0:T(8,128)S(1)}) custom-call(s32[3]{0:T(128)S(1)} %pad_add_fusion.refs_0_.place, f32[512,1024]{1,0:T(8,128)S(1)} %near_rows.1.near, ...), custom_call_target="tpu_custom_call" | custom-call | tf_op jit(solution)/shard_map/other_rows/pallas_call | solution.py:318
  60.6 1.3 %collective-permute-start.16 = (f32[64,1024]{1,0:T(8,128)S(1)}, f32[64,1024]{1,0:T(8,128)S(1)}, u32[]{:S(2)}, u32[]{:S(2)}) collective-permute-start(f32[64,1024]{1,0:T(8,128)S(1)} %get-tuple-element.75), channel_id=1, source_target_pairs={{0,8},{8,0},{16,24},{24,16},{32,40},{40,32},{48,56},{56,48},{64,72... | collective-permute-start | bytes 786440 | tf_op jit(solution)/shard_map/ppermute | solution.py:368
  61.9 0.0 collective-permute-done.14.beside
  61.9 1.0 %collective-permute-start.10 = (f32[64,1024]{1,0:T(8,128)S(1)}, f32[64,1024]{1,0:T(8,128)S(1)}, u32[]{:S(2)}, u32[]{:S(2)}) collective-permute-start(f32[64,1024]{1,0:T(8,128)S(1)} %get-tuple-element.65), channel_id=1, source_target_pairs={{0,48},{8,56},{16,0},{24,8},{32,16},{40,24},{48,32},{56,40},{64,11... | collective-permute-start | bytes 786440 | tf_op jit(solution)/shard_map/ppermute | solution.py:368
  62.9 2.7 %collective-permute-done.15.edge = f32[8,1280]{1,0:T(8,128)S(1)} collective-permute-done((f32[8,1280]{1,0:T(8,128)S(1)}, f32[8,1280]{1,0:T(8,128)S(1)}, u32[]{:S(2)}, u32[]{:S(2)}) %collective-permute-start.15) | collective-permute-done | bytes 40992 | tf_op jit(solution)/shard_map/ppermute | solution.py:382
  65.6 0.0 collective-permute-start.11
  65.6 0.0 collective-permute-done.17.refs_4_
  65.6 0.3 collective-permute-start.12
  65.9 0.0 collective-permute-done.18.refs_5_
  65.9 2.0 %collective-permute-start.13 = (f32[64,1024]{1,0:T(8,128)S(1)}, f32[64,1024]{1,0:T(8,128)S(1)}, u32[]{:S(2)}, u32[]{:S(2)}) collective-permute-start(f32[64,1024]{1,0:T(8,128)S(1)} %get-tuple-element.68), channel_id=1, source_target_pairs={{0,24},{8,16},{16,40},{24,32},{32,56},{40,48},{48,8},{56,0},{64,88... | collective-permute-start | bytes 786440 | tf_op jit(solution)/shard_map/ppermute | solution.py:368
  68.6 0.0 copy-done.1
  68.6 0.0 copy-done.4
  68.6 0.0 copy-done.5
  68.6 4.6 %side_columns_and_stencil.1 = (f32[8,64,1024]{2,1,0:T(8,128)}, f32[8,64,1024]{2,1,0:T(8,128)S(1)}) custom-call(s32[3]{0:T(128)S(1)} %pad_add_fusion.refs_0_.place, f32[2]{0:T(128)S(1)} %copy-done.1, f32[3]{0:T(128)S(1)} %copy-done.4, f32[3]{0:T(128)S(1)} %copy-done.5, f32[1]{0:T(128)S(6)} %copy.14.cross, f32[8,64,1024]{2,1,0:T(8,128)S(1)} %get-tuple-element.43.refs_1_.value, ...), custom_call_target="tpu_custom_call" | custom-call | tf_op jit(solution)/shard_map/side_columns_and_stencil/pallas_call | solution.py:137
  73.2 0.0 collective-permute-done.16.refs_3_
  73.2 1.9 %finish.2 = (f32[8,64,1024]{2,1,0:T(8,128)}, f32[8,64,1024]{2,1,0:T(8,128)}) custom-call(s32[3]{0:T(128)S(1)} %pad_add_fusion.refs_0_.place, f32[2]{0:T(128)S(1)} %copy-done.1, f32[64,1024]{1,0:T(8,128)S(1)} %get-tuple-element.69.refs_2_, f32[64,1024]{1,0:T(8,128)S(1)} %collective-permute-done.16.refs_3_, f32[64,1024]{1,0:T(8,128)S(1)} %collective-permute-done.17.refs_4_, ...), custom_call_target="tpu_custom_call" | custom-call | tf_op jit(solution)/shard_map/finish/pallas_call | solution.py:346
  75.2 0.0 collective-permute-done.10.refs_2_
  75.2 1.3 %collective-permute-done.11.refs_3_ = f32[64,1024]{1,0:T(8,128)S(1)} collective-permute-done((f32[64,1024]{1,0:T(8,128)S(1)}, f32[64,1024]{1,0:T(8,128)S(1)}, u32[]{:S(2)}, u32[]{:S(2)}) %collective-permute-start.11) | collective-permute-done | bytes 262176 | tf_op jit(solution)/shard_map/ppermute | solution.py:368
  76.5 0.0 collective-permute-done.12.refs_4_
  76.5 4.1 %collective-permute-done.13.refs_5_ = f32[64,1024]{1,0:T(8,128)S(1)} collective-permute-done((f32[64,1024]{1,0:T(8,128)S(1)}, f32[64,1024]{1,0:T(8,128)S(1)}, u32[]{:S(2)}, u32[]{:S(2)}) %collective-permute-start.13) | collective-permute-done | bytes 262176 | tf_op jit(solution)/shard_map/ppermute | solution.py:368
  80.6 1.9 %finish.3 = (f32[8,64,1024]{2,1,0:T(8,128)}, f32[8,64,1024]{2,1,0:T(8,128)}) custom-call(s32[3]{0:T(128)S(1)} %pad_add_fusion.refs_0_.place, f32[2]{0:T(128)S(1)} %copy-done.1, f32[64,1024]{1,0:T(8,128)S(1)} %collective-permute-done.10.refs_2_, f32[64,1024]{1,0:T(8,128)S(1)} %collective-permute-done.11.refs_3_, ...), custom_call_target="tpu_custom_call", output_to_operand_aliasing={{0}: (7, {}), {1}: (8, {})} | custom-call | tf_op jit(solution)/shard_map/finish/pallas_call | solution.py:346
Async XLA Ops:
  0.6 4.9 %collective-permute-start = (f32[8,64,1024]{2,1,0:T(8,128)}, f32[8,64,1024]{2,1,0:T(8,128)}, u32[]{:S(2)}, u32[]{:S(2)}) collective-permute-start(f32[8,64,1024]{2,1,0:T(8,128)} %value.1), channel_id=1, source_target_pairs={{0,8},{8,0},{16,24},{24,16},{32,40},{40,32},{48,56},{56,48},{64,72... | collective-permute-start | bytes 6291464 | tf_op jit(solution)/shard_map/ppermute | solution.py:368
  1.4 1.6 %copy-start = (f32[8,64,1024]{2,1,0:T(8,128)S(1)}, f32[8,64,1024]{2,1,0:T(8,128)}, u32[]{:S(2)}) copy-start(f32[8,64,1024]{2,1,0:T(8,128)} %value.1) | copy-start | bytes 6291460
  5.5 13.6 %copy-start.2 = (f32[511]{0:T(512)S(1)}, f32[511]{0:T(512)}, u32[]{:S(2)}) copy-start(f32[511]{0:T(512)} %param.9) | copy-start | bytes 6136
  7.4 14.2 %copy-start.3 = (f32[511]{0:T(512)S(1)}, f32[511]{0:T(512)}, u32[]{:S(2)}) copy-start(f32[511]{0:T(512)} %param.8) | copy-start | bytes 6136
  7.4 14.6 %collective-permute-start.1 = (f32[128,1024]{1,0:T(8,128)S(1)}, f32[128,1024]{1,0:T(8,128)S(1)}, u32[]{:S(2)}, u32[]{:S(2)}) collective-permute-start(f32[128,1024]{1,0:T(8,128)S(1)} %get-tuple-element.44), channel_id=1, source_target_pairs={{0,16},{8,24},{16,32},{24,40},{32,48},{40,56},{48,0},{56,8},{64,80... | collective-permute-start | bytes 1572872 | tf_op jit(solution)/shard_map/ppermute | solution.py:368
  8.8 13.2 %collective-permute-start.4 = (f32[128,1024]{1,0:T(8,128)S(1)}, f32[128,1024]{1,0:T(8,128)S(1)}, u32[]{:S(2)}, u32[]{:S(2)}) collective-permute-start(f32[128,1024]{1,0:T(8,128)S(1)} %get-tuple-element.53), channel_id=1, source_target_pairs={{0,48},{8,56},{16,0},{24,8},{32,16},{40,24},{48,32},{56,40},{64,11... | collective-permute-start | bytes 1572872 | tf_op jit(solution)/shard_map/ppermute | solution.py:368
  10.3 16.2 %collective-permute-start.3 = (f32[8,64,256]{2,1,0:T(8,128)S(1)}, f32[8,64,256]{2,1,0:T(8,128)S(1)}, u32[]{:S(2)}, u32[]{:S(2)}) collective-permute-start(f32[8,64,256]{2,1,0:T(8,128)S(1)} %get-tuple-element.50), channel_id=1, source_target_pairs={{1,0},{2,1},{3,2},{4,3},{5,4},{6,5},{7,6},{9,8},{10,9},{11,10},{12... | collective-permute-start | bytes 1572872 | tf_op jit(solution)/shard_map/ppermute | solution.py:359
  12.2 15.1 %collective-permute-start.2 = (f32[8,64,256]{2,1,0:T(8,128)S(1)}, f32[8,64,256]{2,1,0:T(8,128)S(1)}, u32[]{:S(2)}, u32[]{:S(2)}) collective-permute-start(f32[8,64,256]{2,1,0:T(8,128)S(1)} %get-tuple-element.48), channel_id=1, source_target_pairs={{0,1},{1,2},{2,3},{3,4},{4,5},{5,6},{6,7},{8,9},{9,10},{10,11},{11... | collective-permute-start | bytes 1572872 | tf_op jit(solution)/shard_map/ppermute | solution.py:359
  17.0 14.1 %collective-permute-start.6 = (f32[128,1024]{1,0:T(8,128)S(1)}, f32[128,1024]{1,0:T(8,128)S(1)}, u32[]{:S(2)}, u32[]{:S(2)}) collective-permute-start(f32[128,1024]{1,0:T(8,128)S(1)} %get-tuple-element.47.p0), channel_id=1, source_target_pairs={{32,96},{40,104},{48,112},{56,120},{64,0},{72,8},{80,16},{88,24},{... | collective-permute-start | bytes 1572872 | tf_op jit(solution)/shard_map/ppermute | solution.py:368
  21.9 14.6 %collective-permute-start.5 = (f32[128,1024]{1,0:T(8,128)S(1)}, f32[128,1024]{1,0:T(8,128)S(1)}, u32[]{:S(2)}, u32[]{:S(2)}) collective-permute-start(f32[128,1024]{1,0:T(8,128)S(1)} %get-tuple-element.61), channel_id=1, source_target_pairs={{0,32},{8,40},{16,48},{24,56},{32,0},{40,8},{48,16},{56,24},{64,96... | collective-permute-start | bytes 1572872 | tf_op jit(solution)/shard_map/ppermute | solution.py:368
  27.3 13.5 %collective-permute-start.7 = (f32[128,1024]{1,0:T(8,128)S(1)}, f32[128,1024]{1,0:T(8,128)S(1)}, u32[]{:S(2)}, u32[]{:S(2)}) collective-permute-start(f32[128,1024]{1,0:T(8,128)S(1)} %collective-permute-done.1.p1), channel_id=1, source_target_pairs={{0,64},{8,72},{48,112},{56,120},{64,128},{72,136},{80,16},{88,24},... | collective-permute-start | bytes 1572872 | tf_op jit(solution)/shard_map/ppermute | solution.py:368
  31.1 13.2 %collective-permute-start.9 = (f32[128,1024]{1,0:T(8,128)S(1)}, f32[128,1024]{1,0:T(8,128)S(1)}, u32[]{:S(2)}, u32[]{:S(2)}) collective-permute-start(f32[128,1024]{1,0:T(8,128)S(1)} %collective-permute-done.4.p3), channel_id=1, source_target_pairs={{16,80},{24,88},{32,96},{40,104},{64,0},{72,8},{80,144},{88,152},{... | collective-permute-start | bytes 1572872 | tf_op jit(solution)/shard_map/ppermute | solution.py:368
  36.6 21.2 %collective-permute-start.8 = (f32[128,1024]{1,0:T(8,128)S(1)}, f32[128,1024]{1,0:T(8,128)S(1)}, u32[]{:S(2)}, u32[]{:S(2)}) collective-permute-start(f32[128,1024]{1,0:T(8,128)S(1)} %collective-permute-done.5.p2), channel_id=1, source_target_pairs={{0,64},{8,72},{16,80},{24,88},{64,128},{72,136},{80,144},{88,152},... | collective-permute-start | bytes 1572872 | tf_op jit(solution)/shard_map/ppermute | solution.py:368
  45.7 19.9 %collective-permute-start.17 = (f32[64,1024]{1,0:T(8,128)S(1)}, f32[64,1024]{1,0:T(8,128)S(1)}, u32[]{:S(2)}, u32[]{:S(2)}) collective-permute-start(f32[64,1024]{1,0:T(8,128)S(1)} %get-tuple-element.76), channel_id=1, source_target_pairs={{0,32},{8,40},{16,48},{24,56},{32,0},{40,8},{48,16},{56,24},{64,96... | collective-permute-start | bytes 786440 | tf_op jit(solution)/shard_map/ppermute | solution.py:368
  47.0 18.9 %collective-permute-start.18 = (f32[64,1024]{1,0:T(8,128)S(1)}, f32[64,1024]{1,0:T(8,128)S(1)}, u32[]{:S(2)}, u32[]{:S(2)}) collective-permute-start(f32[64,1024]{1,0:T(8,128)S(1)} %get-tuple-element.77), channel_id=1, source_target_pairs={{0,40},{8,32},{16,56},{24,48},{32,8},{40,0},{48,24},{56,16},{64,10... | collective-permute-start | bytes 786440 | tf_op jit(solution)/shard_map/ppermute | solution.py:368
  51.9 16.7 %copy-start.1 = (f32[2]{0:T(128)S(1)}, f32[2]{0:T(128)}, u32[]{:S(2)}) copy-start(f32[2]{0:T(128)} %refs_1_.3) | copy-start | bytes 28
  51.9 16.7 %copy-start.4 = (f32[3]{0:T(128)S(1)}, f32[3]{0:T(128)}, u32[]{:S(2)}) copy-start(f32[3]{0:T(128)} %diffusion.1) | copy-start | bytes 40
  51.9 16.7 %copy-start.5 = (f32[3]{0:T(128)S(1)}, f32[3]{0:T(128)}, u32[]{:S(2)}) copy-start(f32[3]{0:T(128)} %drift.1) | copy-start | bytes 40
  51.9 10.0 %collective-permute-start.14 = (f32[8,1280]{1,0:T(8,128)S(1)}, f32[8,1280]{1,0:T(8,128)S(1)}, u32[]{:S(2)}, u32[]{:S(2)}) collective-permute-start(f32[8,1280]{1,0:T(8,128)S(1)} %get-tuple-element.71), channel_id=1, source_target_pairs={{0,8},{8,0},{16,24},{24,16},{32,40},{40,32},{48,56},{56,48},{64,72... | collective-permute-start | bytes 122888 | tf_op jit(solution)/shard_map/ppermute | solution.py:368
  51.9 13.7 %collective-permute-start.15 = (f32[8,1280]{1,0:T(8,128)S(1)}, f32[8,1280]{1,0:T(8,128)S(1)}, u32[]{:S(2)}, u32[]{:S(2)}) collective-permute-start(f32[8,1280]{1,0:T(8,128)S(1)} %get-tuple-element.51), channel_id=1, source_target_pairs={{8,16},{16,8},{24,32},{32,24},{40,48},{48,40},{56,64},{64,56},{72,... | collective-permute-start | bytes 122888 | tf_op jit(solution)/shard_map/ppermute | solution.py:382
  60.6 12.7 %collective-permute-start.16 = (f32[64,1024]{1,0:T(8,128)S(1)}, f32[64,1024]{1,0:T(8,128)S(1)}, u32[]{:S(2)}, u32[]{:S(2)}) collective-permute-start(f32[64,1024]{1,0:T(8,128)S(1)} %get-tuple-element.75), channel_id=1, source_target_pairs={{0,8},{8,0},{16,24},{24,16},{32,40},{40,32},{48,56},{56,48},{64,72... | collective-permute-start | bytes 786440 | tf_op jit(solution)/shard_map/ppermute | solution.py:368
  61.9 13.3 %collective-permute-start.10 = (f32[64,1024]{1,0:T(8,128)S(1)}, f32[64,1024]{1,0:T(8,128)S(1)}, u32[]{:S(2)}, u32[]{:S(2)}) collective-permute-start(f32[64,1024]{1,0:T(8,128)S(1)} %get-tuple-element.65), channel_id=1, source_target_pairs={{0,48},{8,56},{16,0},{24,8},{32,16},{40,24},{48,32},{56,40},{64,11... | collective-permute-start | bytes 786440 | tf_op jit(solution)/shard_map/ppermute | solution.py:368
  65.6 10.9 %collective-permute-start.11 = (f32[64,1024]{1,0:T(8,128)S(1)}, f32[64,1024]{1,0:T(8,128)S(1)}, u32[]{:S(2)}, u32[]{:S(2)}) collective-permute-start(f32[64,1024]{1,0:T(8,128)S(1)} %get-tuple-element.66), channel_id=1, source_target_pairs={{0,56},{8,48},{16,8},{24,0},{32,24},{40,16},{48,40},{56,32},{64,12... | collective-permute-start | bytes 786440 | tf_op jit(solution)/shard_map/ppermute | solution.py:368
  65.6 10.9 %collective-permute-start.12 = (f32[64,1024]{1,0:T(8,128)S(1)}, f32[64,1024]{1,0:T(8,128)S(1)}, u32[]{:S(2)}, u32[]{:S(2)}) collective-permute-start(f32[64,1024]{1,0:T(8,128)S(1)} %get-tuple-element.67), channel_id=1, source_target_pairs={{0,16},{8,24},{16,32},{24,40},{32,48},{40,56},{48,0},{56,8},{64,80... | collective-permute-start | bytes 786440 | tf_op jit(solution)/shard_map/ppermute | solution.py:368
  65.9 14.7 %collective-permute-start.13 = (f32[64,1024]{1,0:T(8,128)S(1)}, f32[64,1024]{1,0:T(8,128)S(1)}, u32[]{:S(2)}, u32[]{:S(2)}) collective-permute-start(f32[64,1024]{1,0:T(8,128)S(1)} %get-tuple-element.68), channel_id=1, source_target_pairs={{0,24},{8,16},{16,40},{24,32},{32,56},{40,48},{48,8},{56,0},{64,88... | collective-permute-start | bytes 786440 | tf_op jit(solution)/shard_map/ppermute | solution.py:368

commit v4 on v3

--- a/solution.py
+++ b/solution.py
@@ -175,7 +175,7 @@
     )(weights)
 
 
-def load_kernel(value, held, high_side, low_side, done):
+def load_kernel(place, value, held, high_side, low_side, done):
     copy = pltpu.make_async_copy(value, held, done)
     copy.start()
     copy.wait()
@@ -184,12 +184,12 @@
     low_side[...] = held[:, :, :BLOCK]
 
 
-def load_part(value):
+def load_part(place, value):
     side = f32(*value.shape[:2], BLOCK)
     return pl.pallas_call(
-        load_kernel, out_shape=[f32(*value.shape), side, side], in_specs=[pl.BlockSpec(memory_space=pl.ANY)],
+        load_kernel, out_shape=[f32(*value.shape), side, side], in_specs=[SMEM, pl.BlockSpec(memory_space=pl.ANY)],
         out_specs=[VMEM] * 3, scratch_shapes=[pltpu.SemaphoreType.DMA], compiler_params=params(4), name="load",
-    )(value)
+    )(place, value)
 
 
 def pieces_kernel(steps, place, value, other, *refs):
@@ -209,10 +209,9 @@
 
 def pieces_part(steps, place, value, other):
     _, rows, cols = value.shape
-    anywhere = pl.BlockSpec(memory_space=pl.ANY)
     return pl.pallas_call(
         lambda *refs: pieces_kernel(steps, *refs),
-        out_shape=[f32(CORES * rows, cols)] * len(steps), in_specs=[SMEM, anywhere, anywhere],
+        out_shape=[f32(CORES * rows, cols)] * len(steps), in_specs=[SMEM, VMEM, VMEM],
         out_specs=[VMEM] * len(steps), scratch_shapes=[pltpu.SemaphoreType.DMA((len(steps), 2))],
         compiler_params=params(4), name="pieces",
     )(place, value, other)
@@ -397,7 +396,7 @@
     place = jnp.stack([lax.div(chip, RING), lax.rem(chip, RING), lax.rem(me, CORES)])
 
     other = to_other_core(value)
-    value, high_side, low_side = load_part(value)
+    value, high_side, low_side = load_part(place, value)
 
     s1, s3, p0, s2 = pieces_part((1, 3, 0, 2), place, value, other)
     p1, p3, x0 = to_ring(s1, 1), to_ring(s3, 3), to_group(p0, 0)
@@ -405,10 +404,10 @@
     within, col_hi, col_lo, _ = within_part(value, after(kernel_cols[None], s2))
     taps = taps_part(after(kernel_rows[None], within))
     p2 = to_ring(after(s2, p1, p3, taps[2]), 2)
-    x1, x3 = to_group(after(p1, low, high), 1), to_group(after(p3, x0), 3)
+    x1, x3 = to_group(p1, 1), to_group(p3, 3)
     outer, inner = lines_part(after(place, p1), value, low, high)
     edge, beside = across_chips(outer), to_other_core(inner)
-    near = near_part(after(place, outer), p0, p1, p3, taps)
+    near = near_part(after(place, outer, x0), p0, p1, p3, taps)
     x2 = to_group(after(p2, near), 2)
     b2, o2 = opposite_part(place, near, p2, x0, x1, x3, taps)
     d2, o2 = to_ring(b2, -2), to_ring(o2, -2, True)

time: 83 us -> 77.1 us (0.929)
  the two profiles are of different devices: /device:TPU:99 before, /device:TPU:2 now
where the time goes in v4:
time: 77.1 us; the launch traced here: 76.7 us
  starting transfers between devices  39.9 us (52%)
  Pallas kernels  20.1 us (26%)
  waiting for transfers between devices  13.3 us (17%)
  between operations  1.7 us (2%)
  local copies, waits for them, and re-layouts  1.61 us (2%)
    ppermute x16, starting transfers between devices, send(): return lax.ppermute(block, 'gx', route)  29.7 us
    ppermute x16, waiting for transfers between devices, send(): return lax.ppermute(block, 'gx', route)  11.3 us
    pallas_call x1, Pallas kernels, local_part(): pl.pallas_call(local_kernel, out_shape=(f32(*value.shape),) * 2, in_specs...  4.73 us
    ppermute x1, starting transfers between devices, neighbours(): lax.ppermute(high_side, axis, forward)  4.58 us
    ppermute x1, starting transfers between devices, across_chips(): return lax.ppermute(line, 'gx', route)  4.32 us
    pallas_call x2, Pallas kernels, finish_part(): pl.pallas_call(lambda *refs: finish_kernel(steps, *refs), out_shape=[f32(...  3.87 us
    pallas_call x1, Pallas kernels, others_part(): pl.pallas_call(others_kernel, out_shape=[f32(rows // RING // CORES, cols)...  2.8 us
    pallas_call x1, Pallas kernels, near_part(): pl.pallas_call(near_kernel, out_shape=f32(RING * size, cols), in_specs=[S...  2.66 us
  transfers between devices with their start and end apart: 19, of which 6 were waited for; matrix products, arithmetic and copies ran while one was open for 0% of the time, Pallas kernels for 23%

profile of v4, /device:TPU:2, one launch (start us, length us, event | category | flops | bytes accessed | tf_op | source)
XLA Modules:
  0.0 76.7 jit_solution(1744235999488410009)
XLA Ops:
  0.6 0.1 collective-permute-start
  0.7 0.1 pad_add_fusion.place.refs_0_
  0.8 0.0 copy-start
  0.8 1.6 %copy-done = f32[8,64,1024]{2,1,0:T(8,128)S(1)} copy-done((f32[8,64,1024]{2,1,0:T(8,128)S(1)}, f32[8,64,1024]{2,1,0:T(8,128)}, u32[]{:S(2)}) %copy-start) | copy-done | bytes 2097176
  2.4 0.8 %load.1 = (f32[8,64,1024]{2,1,0:T(8,128)S(1)}, f32[8,64,256]{2,1,0:T(8,128)S(1)}, f32[8,64,256]{2,1,0:T(8,128)S(1)}) custom-call(s32[3]{0:T(128)S(1)} %pad_add_fusion.place.refs_0_, f32[8,64,1024]{2,1,0:T(8,128)S(1)} %copy-done), custom_call_target="tpu_custom_call" | custom-call | tf_op jit(solution)/shard_map/load/pallas_call | solution.py:189
  3.2 1.9 %collective-permute-done.refs_2_ = f32[8,64,1024]{2,1,0:T(8,128)S(1)} collective-permute-done((f32[8,64,1024]{2,1,0:T(8,128)}, f32[8,64,1024]{2,1,0:T(8,128)S(1)}, u32[]{:S(2)}, u32[]{:S(2)}) %collective-permute-start) | collective-permute-done | bytes 2097184 | tf_op jit(solution)/shard_map/ppermute | solution.py:367
  5.1 0.0 copy-start.2
  5.1 0.8 %pieces.1 = (f32[128,1024]{1,0:T(8,128)S(1)}, f32[128,1024]{1,0:T(8,128)S(1)}, f32[128,1024]{1,0:T(8,128)S(1)}, f32[128,1024]{1,0:T(8,128)S(1)}) custom-call(s32[3]{0:T(128)S(1)} %pad_add_fusion.place.refs_0_, f32[8,64,1024]{2,1,0:T(8,128)S(1)} %get-tuple-element.41.refs_1_.value, f32[8,64,1024]{2,1,0:T(8,128)S(1)} %collective-permute-done.refs_2_), custom_call_target="tpu_custom_call" | custom-call | tf_op jit(solution)/shard_map/pieces/pallas_call | solution.py:212
  5.9 0.0 copy-start.3
  5.9 1.7 %collective-permute-start.1 = (f32[128,1024]{1,0:T(8,128)S(1)}, f32[128,1024]{1,0:T(8,128)S(1)}, u32[]{:S(2)}, u32[]{:S(2)}) collective-permute-start(f32[128,1024]{1,0:T(8,128)S(1)} %get-tuple-element.42), channel_id=1, source_target_pairs={{0,16},{8,24},{16,32},{24,40},{32,48},{40,56},{48,0},{56,8},{64,80... | collective-permute-start | bytes 1572872 | tf_op jit(solution)/shard_map/ppermute | solution.py:367
  7.6 1.7 %collective-permute-start.5 = (f32[128,1024]{1,0:T(8,128)S(1)}, f32[128,1024]{1,0:T(8,128)S(1)}, u32[]{:S(2)}, u32[]{:S(2)}) collective-permute-start(f32[128,1024]{1,0:T(8,128)S(1)} %get-tuple-element.51), channel_id=1, source_target_pairs={{0,48},{8,56},{16,0},{24,8},{32,16},{40,24},{48,32},{56,40},{64,11... | collective-permute-start | bytes 1572872 | tf_op jit(solution)/shard_map/ppermute | solution.py:367
  9.2 1.3 %collective-permute-start.3 = (f32[8,64,256]{2,1,0:T(8,128)S(1)}, f32[8,64,256]{2,1,0:T(8,128)S(1)}, u32[]{:S(2)}, u32[]{:S(2)}) collective-permute-start(f32[8,64,256]{2,1,0:T(8,128)S(1)} %get-tuple-element.48), channel_id=1, source_target_pairs={{1,0},{2,1},{3,2},{4,3},{5,4},{6,5},{7,6},{9,8},{10,9},{11,10},{12... | collective-permute-start | bytes 1572872 | tf_op jit(solution)/shard_map/ppermute | solution.py:358
  10.5 4.2 %collective-permute-start.4 = (f32[128,1024]{1,0:T(8,128)S(1)}, f32[128,1024]{1,0:T(8,128)S(1)}, u32[]{:S(2)}, u32[]{:S(2)}) collective-permute-start(f32[128,1024]{1,0:T(8,128)S(1)} %get-tuple-element.45.p0), channel_id=1, source_target_pairs={{32,96},{40,104},{48,112},{56,120},{64,0},{72,8},{80,16},{88,24},{... | collective-permute-start | bytes 1572872 | tf_op jit(solution)/shard_map/ppermute | solution.py:367
  14.7 0.0 copy-done.2
  14.7 2.4 %own_columns.1 = (f32[8,64,1024]{2,1,0:T(8,128)S(1)}, bf16[256,768]{1,0:T(8,128)(2,1)S(1)}, bf16[256,768]{1,0:T(8,128)(2,1)S(1)}, f32[8,128]{1,0:T(8,128)}) custom-call(f32[8,64,1024]{2,1,0:T(8,128)S(1)} %get-tuple-element.41.refs_1_.value, f32[1,511]{1,0:T(1,128)S(1)} %bitcast.5), custom_call_target="tpu_custom_call" | custom-call | tf_op jit(solution)/shard_map/own_columns/pallas_call | solution.py:76
  17.1 4.6 %collective-permute-start.2 = (f32[8,64,256]{2,1,0:T(8,128)S(1)}, f32[8,64,256]{2,1,0:T(8,128)S(1)}, u32[]{:S(2)}, u32[]{:S(2)}) collective-permute-start(f32[8,64,256]{2,1,0:T(8,128)S(1)} %get-tuple-element.46), channel_id=1, source_target_pairs={{0,1},{1,2},{2,3},{3,4},{4,5},{5,6},{6,7},{8,9},{9,10},{10,11},{11... | collective-permute-start | bytes 1572872 | tf_op jit(solution)/shard_map/ppermute | solution.py:358
  21.7 0.0 copy-done.3
  21.7 0.2 row_taps.1
  21.9 0.0 collective-permute-done.1.p1
  21.9 0.0 collective-permute-done.5.p3
  21.9 2.2 %collective-permute-start.6 = (f32[128,1024]{1,0:T(8,128)S(1)}, f32[128,1024]{1,0:T(8,128)S(1)}, u32[]{:S(2)}, u32[]{:S(2)}) collective-permute-start(f32[128,1024]{1,0:T(8,128)S(1)} %get-tuple-element.59), channel_id=1, source_target_pairs={{0,32},{8,40},{16,48},{24,56},{32,0},{40,8},{48,16},{56,24},{64,96... | collective-permute-start | bytes 1572872 | tf_op jit(solution)/shard_map/ppermute | solution.py:367
  24.1 3.4 %collective-permute-start.7 = (f32[128,1024]{1,0:T(8,128)S(1)}, f32[128,1024]{1,0:T(8,128)S(1)}, u32[]{:S(2)}, u32[]{:S(2)}) collective-permute-start(f32[128,1024]{1,0:T(8,128)S(1)} %collective-permute-done.1.p1), channel_id=1, source_target_pairs={{0,64},{8,72},{48,112},{56,120},{64,128},{72,136},{80,16},{88,24},... | collective-permute-start | bytes 1572872 | tf_op jit(solution)/shard_map/ppermute | solution.py:367
  27.5 0.0 collective-permute-done.3.high
  27.5 2.5 %collective-permute-start.9 = (f32[128,1024]{1,0:T(8,128)S(1)}, f32[128,1024]{1,0:T(8,128)S(1)}, u32[]{:S(2)}, u32[]{:S(2)}) collective-permute-start(f32[128,1024]{1,0:T(8,128)S(1)} %collective-permute-done.5.p3), channel_id=1, source_target_pairs={{16,80},{24,88},{32,96},{40,104},{64,0},{72,8},{80,144},{88,152},{... | collective-permute-start | bytes 1572872 | tf_op jit(solution)/shard_map/ppermute | solution.py:367
  30.0 2.0 %collective-permute-done.2.low = f32[8,64,256]{2,1,0:T(8,128)S(1)} collective-permute-done((f32[8,64,256]{2,1,0:T(8,128)S(1)}, f32[8,64,256]{2,1,0:T(8,128)S(1)}, u32[]{:S(2)}, u32[]{:S(2)}) %collective-permute-start.2) | collective-permute-done | bytes 524320 | tf_op jit(solution)/shard_map/ppermute | solution.py:358
  32.0 0.6 lines.1
  32.6 0.0 collective-permute-done.4.x0
  32.6 2.7 %near_rows.1.near = f32[512,1024]{1,0:T(8,128)S(1)} custom-call(s32[3]{0:T(128)S(1)} %pad_add_fusion.place.refs_0_, f32[128,1024]{1,0:T(8,128)S(1)} %get-tuple-element.45.p0, f32[128,1024]{1,0:T(8,128)S(1)} %collective-permute-done.1.p1, f32[128,1024]{1,0:T(8,128)S(1)} %collective-permute-done.5.p3, bf16[256,768]{1,0:T(8,128)(2,1)S(1)} %get-tuple-element.56.taps_hi, ...), custom_call_target="tpu_custom_call" | custom-call | tf_op jit(solution)/shard_map/near_rows/pallas_call | solution.py:248
  35.3 0.8 %collective-permute-done.6.p2 = f32[128,1024]{1,0:T(8,128)S(1)} collective-permute-done((f32[128,1024]{1,0:T(8,128)S(1)}, f32[128,1024]{1,0:T(8,128)S(1)}, u32[]{:S(2)}, u32[]{:S(2)}) %collective-permute-start.6) | collective-permute-done | bytes 524320 | tf_op jit(solution)/shard_map/ppermute | solution.py:367
  36.1 3.2 %collective-permute-start.8 = (f32[128,1024]{1,0:T(8,128)S(1)}, f32[128,1024]{1,0:T(8,128)S(1)}, u32[]{:S(2)}, u32[]{:S(2)}) collective-permute-start(f32[128,1024]{1,0:T(8,128)S(1)} %collective-permute-done.6.p2), channel_id=1, source_target_pairs={{0,64},{8,72},{16,80},{24,88},{64,128},{72,136},{80,144},{88,152},... | collective-permute-start | bytes 1572872 | tf_op jit(solution)/shard_map/ppermute | solution.py:367
  39.3 0.0 collective-permute-done.7.x1
  39.3 2.4 %collective-permute-done.9.x3 = f32[128,1024]{1,0:T(8,128)S(1)} collective-permute-done((f32[128,1024]{1,0:T(8,128)S(1)}, f32[128,1024]{1,0:T(8,128)S(1)}, u32[]{:S(2)}, u32[]{:S(2)}) %collective-permute-start.9) | collective-permute-done | bytes 524320 | tf_op jit(solution)/shard_map/ppermute | solution.py:367
  41.7 1.3 %opposite_rows.1 = (f32[64,1024]{1,0:T(8,128)S(1)}, f32[64,1024]{1,0:T(8,128)S(1)}) custom-call(s32[3]{0:T(128)S(1)} %pad_add_fusion.place.refs_0_, f32[512,1024]{1,0:T(8,128)S(1)} %near_rows.1.near, f32[128,1024]{1,0:T(8,128)S(1)} %collective-permute-done.6.p2, f32[128,1024]{1,0:T(8,128)S(1)} %collective-permute-done.4.x0, ...), custom_call_target="tpu_custom_call" | custom-call | tf_op jit(solution)/shard_map/opposite_rows/pallas_call | solution.py:283
  43.0 1.7 %collective-permute-start.17 = (f32[64,1024]{1,0:T(8,128)S(1)}, f32[64,1024]{1,0:T(8,128)S(1)}, u32[]{:S(2)}, u32[]{:S(2)}) collective-permute-start(f32[64,1024]{1,0:T(8,128)S(1)} %get-tuple-element.72), channel_id=1, source_target_pairs={{0,32},{8,40},{16,48},{24,56},{32,0},{40,8},{48,16},{56,24},{64,96... | collective-permute-start | bytes 786440 | tf_op jit(solution)/shard_map/ppermute | solution.py:367
  44.8 0.0 collective-permute-start.18
  44.8 0.0 copy-start.1
  44.8 0.0 copy-start.4
  44.8 0.0 copy-start.5
  44.8 2.0 %collective-permute-start.14 = (f32[8,1280]{1,0:T(8,128)S(1)}, f32[8,1280]{1,0:T(8,128)S(1)}, u32[]{:S(2)}, u32[]{:S(2)}) collective-permute-start(f32[8,1280]{1,0:T(8,128)S(1)} %get-tuple-element.67), channel_id=1, source_target_pairs={{0,8},{8,0},{16,24},{24,16},{32,40},{40,32},{48,56},{56,48},{64,72... | collective-permute-start | bytes 122888 | tf_op jit(solution)/shard_map/ppermute | solution.py:367
  46.8 4.3 %collective-permute-start.15 = (f32[8,1280]{1,0:T(8,128)S(1)}, f32[8,1280]{1,0:T(8,128)S(1)}, u32[]{:S(2)}, u32[]{:S(2)}) collective-permute-start(f32[8,1280]{1,0:T(8,128)S(1)} %get-tuple-element.49), channel_id=1, source_target_pairs={{8,16},{16,8},{24,32},{32,24},{40,48},{48,40},{56,64},{64,56},{72,... | collective-permute-start | bytes 122888 | tf_op jit(solution)/shard_map/ppermute | solution.py:381
  51.1 0.0 collective-permute-done.8.x2
  51.1 2.8 %other_rows.1 = (f32[64,1024]{1,0:T(8,128)S(1)}, f32[64,1024]{1,0:T(8,128)S(1)}, f32[64,1024]{1,0:T(8,128)S(1)}, f32[64,1024]{1,0:T(8,128)S(1)}, f32[64,1024]{1,0:T(8,128)S(1)}, /*index=5*/f32[64,1024]{1,0:T(8,128)S(1)}) custom-call(s32[3]{0:T(128)S(1)} %pad_add_fusion.place.refs_0_, f32[512,1024]{1,0:T(8,128)S(1)} %near_rows.1.near, ...), custom_call_target="tpu_custom_call" | custom-call | tf_op jit(solution)/shard_map/other_rows/pallas_call | solution.py:317
  53.9 2.2 %collective-permute-start.16 = (f32[64,1024]{1,0:T(8,128)S(1)}, f32[64,1024]{1,0:T(8,128)S(1)}, u32[]{:S(2)}, u32[]{:S(2)}) collective-permute-start(f32[64,1024]{1,0:T(8,128)S(1)} %get-tuple-element.71), channel_id=1, source_target_pairs={{0,8},{8,0},{16,24},{24,16},{32,40},{40,32},{48,56},{56,48},{64,72... | collective-permute-start | bytes 786440 | tf_op jit(solution)/shard_map/ppermute | solution.py:367
  56.1 0.0 collective-permute-done.14.beside
  56.1 1.4 %collective-permute-start.10 = (f32[64,1024]{1,0:T(8,128)S(1)}, f32[64,1024]{1,0:T(8,128)S(1)}, u32[]{:S(2)}, u32[]{:S(2)}) collective-permute-start(f32[64,1024]{1,0:T(8,128)S(1)} %get-tuple-element.61), channel_id=1, source_target_pairs={{0,48},{8,56},{16,0},{24,8},{32,16},{40,24},{48,32},{56,40},{64,11... | collective-permute-start | bytes 786440 | tf_op jit(solution)/shard_map/ppermute | solution.py:367
  57.4 0.0 collective-permute-done.15.edge
  57.5 0.7 collective-permute-start.11
  58.2 0.0 collective-permute-done.17.refs_4_
  58.2 1.4 %collective-permute-start.12 = (f32[64,1024]{1,0:T(8,128)S(1)}, f32[64,1024]{1,0:T(8,128)S(1)}, u32[]{:S(2)}, u32[]{:S(2)}) collective-permute-start(f32[64,1024]{1,0:T(8,128)S(1)} %get-tuple-element.63), channel_id=1, source_target_pairs={{0,16},{8,24},{16,32},{24,40},{32,48},{40,56},{48,0},{56,8},{64,80... | collective-permute-start | bytes 786440 | tf_op jit(solution)/shard_map/ppermute | solution.py:367
  59.6 0.0 collective-permute-done.18.refs_5_
  59.6 1.4 %collective-permute-start.13 = (f32[64,1024]{1,0:T(8,128)S(1)}, f32[64,1024]{1,0:T(8,128)S(1)}, u32[]{:S(2)}, u32[]{:S(2)}) collective-permute-start(f32[64,1024]{1,0:T(8,128)S(1)} %get-tuple-element.64), channel_id=1, source_target_pairs={{0,24},{8,16},{16,40},{24,32},{32,56},{40,48},{48,8},{56,0},{64,88... | collective-permute-start | bytes 786440 | tf_op jit(solution)/shard_map/ppermute | solution.py:367
  61.6 0.0 copy-done.1
  61.7 0.0 copy-done.4
  61.7 0.0 copy-done.5
  61.7 4.7 %side_columns_and_stencil.1 = (f32[8,64,1024]{2,1,0:T(8,128)}, f32[8,64,1024]{2,1,0:T(8,128)S(1)}) custom-call(s32[3]{0:T(128)S(1)} %pad_add_fusion.place.refs_0_, f32[2]{0:T(128)S(1)} %copy-done.1, f32[3]{0:T(128)S(1)} %copy-done.4, f32[3]{0:T(128)S(1)} %copy-done.5, f32[1]{0:T(128)S(6)} %copy.14.cross, f32[8,64,1024]{2,1,0:T(8,128)S(1)} %get-tuple-element.41.refs_1_.value, ...), custom_call_target="tpu_custom_call" | custom-call | tf_op jit(solution)/shard_map/side_columns_and_stencil/pallas_call | solution.py:137
  66.4 0.0 collective-permute-done.16.refs_3_
  66.4 1.9 %finish.2 = (f32[8,64,1024]{2,1,0:T(8,128)}, f32[8,64,1024]{2,1,0:T(8,128)}) custom-call(s32[3]{0:T(128)S(1)} %pad_add_fusion.place.refs_0_, f32[2]{0:T(128)S(1)} %copy-done.1, f32[64,1024]{1,0:T(8,128)S(1)} %get-tuple-element.65.refs_2_, f32[64,1024]{1,0:T(8,128)S(1)} %collective-permute-done.16.refs_3_, f32[64,1024]{1,0:T(8,128)S(1)} %collective-permute-done.17.refs_4_, ...), custom_call_target="tpu_custom_call" | custom-call | tf_op jit(solution)/shard_map/finish/pallas_call | solution.py:345
  68.4 0.0 collective-permute-done.10.refs_2_
  68.4 1.2 %collective-permute-done.11.refs_3_ = f32[64,1024]{1,0:T(8,128)S(1)} collective-permute-done((f32[64,1024]{1,0:T(8,128)S(1)}, f32[64,1024]{1,0:T(8,128)S(1)}, u32[]{:S(2)}, u32[]{:S(2)}) %collective-permute-start.11) | collective-permute-done | bytes 262176 | tf_op jit(solution)/shard_map/ppermute | solution.py:367
  69.6 0.0 collective-permute-done.12.refs_4_
  69.6 5.1 %collective-permute-done.13.refs_5_ = f32[64,1024]{1,0:T(8,128)S(1)} collective-permute-done((f32[64,1024]{1,0:T(8,128)S(1)}, f32[64,1024]{1,0:T(8,128)S(1)}, u32[]{:S(2)}, u32[]{:S(2)}) %collective-permute-start.13) | collective-permute-done | bytes 262176 | tf_op jit(solution)/shard_map/ppermute | solution.py:367
  74.6 1.9 %finish.3 = (f32[8,64,1024]{2,1,0:T(8,128)}, f32[8,64,1024]{2,1,0:T(8,128)}) custom-call(s32[3]{0:T(128)S(1)} %pad_add_fusion.place.refs_0_, f32[2]{0:T(128)S(1)} %copy-done.1, f32[64,1024]{1,0:T(8,128)S(1)} %collective-permute-done.10.refs_2_, f32[64,1024]{1,0:T(8,128)S(1)} %collective-permute-done.11.refs_3_, ...), custom_call_target="tpu_custom_call", output_to_operand_aliasing={{0}: (7, {}), {1}: (8, {})} | custom-call | tf_op jit(solution)/shard_map/finish/pallas_call | solution.py:345
Async XLA Ops:
  0.6 4.5 %collective-permute-start = (f32[8,64,1024]{2,1,0:T(8,128)}, f32[8,64,1024]{2,1,0:T(8,128)S(1)}, u32[]{:S(2)}, u32[]{:S(2)}) collective-permute-start(f32[8,64,1024]{2,1,0:T(8,128)} %value.1), channel_id=1, source_target_pairs={{0,8},{8,0},{16,24},{24,16},{32,40},{40,32},{48,56},{56,48},{64,72... | collective-permute-start | bytes 6291464 | tf_op jit(solution)/shard_map/ppermute | solution.py:367
  0.8 1.6 %copy-start = (f32[8,64,1024]{2,1,0:T(8,128)S(1)}, f32[8,64,1024]{2,1,0:T(8,128)}, u32[]{:S(2)}) copy-start(f32[8,64,1024]{2,1,0:T(8,128)} %value.1) | copy-start | bytes 6291460
  5.1 9.6 %copy-start.2 = (f32[511]{0:T(512)S(1)}, f32[511]{0:T(512)}, u32[]{:S(2)}) copy-start(f32[511]{0:T(512)} %param.9) | copy-start | bytes 6136
  5.9 15.8 %copy-start.3 = (f32[511]{0:T(512)S(1)}, f32[511]{0:T(512)}, u32[]{:S(2)}) copy-start(f32[511]{0:T(512)} %param.8) | copy-start | bytes 6136
  5.9 16.0 %collective-permute-start.1 = (f32[128,1024]{1,0:T(8,128)S(1)}, f32[128,1024]{1,0:T(8,128)S(1)}, u32[]{:S(2)}, u32[]{:S(2)}) collective-permute-start(f32[128,1024]{1,0:T(8,128)S(1)} %get-tuple-element.42), channel_id=1, source_target_pairs={{0,16},{8,24},{16,32},{24,40},{32,48},{40,56},{48,0},{56,8},{64,80... | collective-permute-start | bytes 1572872 | tf_op jit(solution)/shard_map/ppermute | solution.py:367
  7.6 14.4 %collective-permute-start.5 = (f32[128,1024]{1,0:T(8,128)S(1)}, f32[128,1024]{1,0:T(8,128)S(1)}, u32[]{:S(2)}, u32[]{:S(2)}) collective-permute-start(f32[128,1024]{1,0:T(8,128)S(1)} %get-tuple-element.51), channel_id=1, source_target_pairs={{0,48},{8,56},{16,0},{24,8},{32,16},{40,24},{48,32},{56,40},{64,11... | collective-permute-start | bytes 1572872 | tf_op jit(solution)/shard_map/ppermute | solution.py:367
  9.2 18.3 %collective-permute-start.3 = (f32[8,64,256]{2,1,0:T(8,128)S(1)}, f32[8,64,256]{2,1,0:T(8,128)S(1)}, u32[]{:S(2)}, u32[]{:S(2)}) collective-permute-start(f32[8,64,256]{2,1,0:T(8,128)S(1)} %get-tuple-element.48), channel_id=1, source_target_pairs={{1,0},{2,1},{3,2},{4,3},{5,4},{6,5},{7,6},{9,8},{10,9},{11,10},{12... | collective-permute-start | bytes 1572872 | tf_op jit(solution)/shard_map/ppermute | solution.py:358
  10.5 22.1 %collective-permute-start.4 = (f32[128,1024]{1,0:T(8,128)S(1)}, f32[128,1024]{1,0:T(8,128)S(1)}, u32[]{:S(2)}, u32[]{:S(2)}) collective-permute-start(f32[128,1024]{1,0:T(8,128)S(1)} %get-tuple-element.45.p0), channel_id=1, source_target_pairs={{32,96},{40,104},{48,112},{56,120},{64,0},{72,8},{80,16},{88,24},{... | collective-permute-start | bytes 1572872 | tf_op jit(solution)/shard_map/ppermute | solution.py:367
  17.1 14.9 %collective-permute-start.2 = (f32[8,64,256]{2,1,0:T(8,128)S(1)}, f32[8,64,256]{2,1,0:T(8,128)S(1)}, u32[]{:S(2)}, u32[]{:S(2)}) collective-permute-start(f32[8,64,256]{2,1,0:T(8,128)S(1)} %get-tuple-element.46), channel_id=1, source_target_pairs={{0,1},{1,2},{2,3},{3,4},{4,5},{5,6},{6,7},{8,9},{9,10},{10,11},{11... | collective-permute-start | bytes 1572872 | tf_op jit(solution)/shard_map/ppermute | solution.py:358
  21.9 14.2 %collective-permute-start.6 = (f32[128,1024]{1,0:T(8,128)S(1)}, f32[128,1024]{1,0:T(8,128)S(1)}, u32[]{:S(2)}, u32[]{:S(2)}) collective-permute-start(f32[128,1024]{1,0:T(8,128)S(1)} %get-tuple-element.59), channel_id=1, source_target_pairs={{0,32},{8,40},{16,48},{24,56},{32,0},{40,8},{48,16},{56,24},{64,96... | collective-permute-start | bytes 1572872 | tf_op jit(solution)/shard_map/ppermute | solution.py:367
  24.1 15.2 %collective-permute-start.7 = (f32[128,1024]{1,0:T(8,128)S(1)}, f32[128,1024]{1,0:T(8,128)S(1)}, u32[]{:S(2)}, u32[]{:S(2)}) collective-permute-start(f32[128,1024]{1,0:T(8,128)S(1)} %collective-permute-done.1.p1), channel_id=1, source_target_pairs={{0,64},{8,72},{48,112},{56,120},{64,128},{72,136},{80,16},{88,24},... | collective-permute-start | bytes 1572872 | tf_op jit(solution)/shard_map/ppermute | solution.py:367
  27.5 14.1 %collective-permute-start.9 = (f32[128,1024]{1,0:T(8,128)S(1)}, f32[128,1024]{1,0:T(8,128)S(1)}, u32[]{:S(2)}, u32[]{:S(2)}) collective-permute-start(f32[128,1024]{1,0:T(8,128)S(1)} %collective-permute-done.5.p3), channel_id=1, source_target_pairs={{16,80},{24,88},{32,96},{40,104},{64,0},{72,8},{80,144},{88,152},{... | collective-permute-start | bytes 1572872 | tf_op jit(solution)/shard_map/ppermute | solution.py:367
  36.1 15.0 %collective-permute-start.8 = (f32[128,1024]{1,0:T(8,128)S(1)}, f32[128,1024]{1,0:T(8,128)S(1)}, u32[]{:S(2)}, u32[]{:S(2)}) collective-permute-start(f32[128,1024]{1,0:T(8,128)S(1)} %collective-permute-done.6.p2), channel_id=1, source_target_pairs={{0,64},{8,72},{16,80},{24,88},{64,128},{72,136},{80,144},{88,152},... | collective-permute-start | bytes 1572872 | tf_op jit(solution)/shard_map/ppermute | solution.py:367
  43.0 15.2 %collective-permute-start.17 = (f32[64,1024]{1,0:T(8,128)S(1)}, f32[64,1024]{1,0:T(8,128)S(1)}, u32[]{:S(2)}, u32[]{:S(2)}) collective-permute-start(f32[64,1024]{1,0:T(8,128)S(1)} %get-tuple-element.72), channel_id=1, source_target_pairs={{0,32},{8,40},{16,48},{24,56},{32,0},{40,8},{48,16},{56,24},{64,96... | collective-permute-start | bytes 786440 | tf_op jit(solution)/shard_map/ppermute | solution.py:367
  44.8 14.8 %collective-permute-start.18 = (f32[64,1024]{1,0:T(8,128)S(1)}, f32[64,1024]{1,0:T(8,128)S(1)}, u32[]{:S(2)}, u32[]{:S(2)}) collective-permute-start(f32[64,1024]{1,0:T(8,128)S(1)} %get-tuple-element.73), channel_id=1, source_target_pairs={{0,40},{8,32},{16,56},{24,48},{32,8},{40,0},{48,24},{56,16},{64,10... | collective-permute-start | bytes 786440 | tf_op jit(solution)/shard_map/ppermute | solution.py:367
  44.8 16.9 %copy-start.1 = (f32[2]{0:T(128)S(1)}, f32[2]{0:T(128)}, u32[]{:S(2)}) copy-start(f32[2]{0:T(128)} %refs_1_.3) | copy-start | bytes 28
  44.8 16.9 %copy-start.4 = (f32[3]{0:T(128)S(1)}, f32[3]{0:T(128)}, u32[]{:S(2)}) copy-start(f32[3]{0:T(128)} %diffusion.1) | copy-start | bytes 40
  44.8 16.9 %copy-start.5 = (f32[3]{0:T(128)S(1)}, f32[3]{0:T(128)}, u32[]{:S(2)}) copy-start(f32[3]{0:T(128)} %drift.1) | copy-start | bytes 40
  44.8 11.3 %collective-permute-start.14 = (f32[8,1280]{1,0:T(8,128)S(1)}, f32[8,1280]{1,0:T(8,128)S(1)}, u32[]{:S(2)}, u32[]{:S(2)}) collective-permute-start(f32[8,1280]{1,0:T(8,128)S(1)} %get-tuple-element.67), channel_id=1, source_target_pairs={{0,8},{8,0},{16,24},{24,16},{32,40},{40,32},{48,56},{56,48},{64,72... | collective-permute-start | bytes 122888 | tf_op jit(solution)/shard_map/ppermute | solution.py:367
  46.8 10.7 %collective-permute-start.15 = (f32[8,1280]{1,0:T(8,128)S(1)}, f32[8,1280]{1,0:T(8,128)S(1)}, u32[]{:S(2)}, u32[]{:S(2)}) collective-permute-start(f32[8,1280]{1,0:T(8,128)S(1)} %get-tuple-element.49), channel_id=1, source_target_pairs={{8,16},{16,8},{24,32},{32,24},{40,48},{48,40},{56,64},{64,56},{72,... | collective-permute-start | bytes 122888 | tf_op jit(solution)/shard_map/ppermute | solution.py:381
  53.9 12.5 %collective-permute-start.16 = (f32[64,1024]{1,0:T(8,128)S(1)}, f32[64,1024]{1,0:T(8,128)S(1)}, u32[]{:S(2)}, u32[]{:S(2)}) collective-permute-start(f32[64,1024]{1,0:T(8,128)S(1)} %get-tuple-element.71), channel_id=1, source_target_pairs={{0,8},{8,0},{16,24},{24,16},{32,40},{40,32},{48,56},{56,48},{64,72... | collective-permute-start | bytes 786440 | tf_op jit(solution)/shard_map/ppermute | solution.py:367
  56.1 12.3 %collective-permute-start.10 = (f32[64,1024]{1,0:T(8,128)S(1)}, f32[64,1024]{1,0:T(8,128)S(1)}, u32[]{:S(2)}, u32[]{:S(2)}) collective-permute-start(f32[64,1024]{1,0:T(8,128)S(1)} %get-tuple-element.61), channel_id=1, source_target_pairs={{0,48},{8,56},{16,0},{24,8},{32,16},{40,24},{48,32},{56,40},{64,11... | collective-permute-start | bytes 786440 | tf_op jit(solution)/shard_map/ppermute | solution.py:367
  57.5 12.1 %collective-permute-start.11 = (f32[64,1024]{1,0:T(8,128)S(1)}, f32[64,1024]{1,0:T(8,128)S(1)}, u32[]{:S(2)}, u32[]{:S(2)}) collective-permute-start(f32[64,1024]{1,0:T(8,128)S(1)} %get-tuple-element.62), channel_id=1, source_target_pairs={{0,56},{8,48},{16,8},{24,0},{32,24},{40,16},{48,40},{56,32},{64,12... | collective-permute-start | bytes 786440 | tf_op jit(solution)/shard_map/ppermute | solution.py:367
  58.2 11.4 %collective-permute-start.12 = (f32[64,1024]{1,0:T(8,128)S(1)}, f32[64,1024]{1,0:T(8,128)S(1)}, u32[]{:S(2)}, u32[]{:S(2)}) collective-permute-start(f32[64,1024]{1,0:T(8,128)S(1)} %get-tuple-element.63), channel_id=1, source_target_pairs={{0,16},{8,24},{16,32},{24,40},{32,48},{40,56},{48,0},{56,8},{64,80... | collective-permute-start | bytes 786440 | tf_op jit(solution)/shard_map/ppermute | solution.py:367
  59.6 15.1 %collective-permute-start.13 = (f32[64,1024]{1,0:T(8,128)S(1)}, f32[64,1024]{1,0:T(8,128)S(1)}, u32[]{:S(2)}, u32[]{:S(2)}) collective-permute-start(f32[64,1024]{1,0:T(8,128)S(1)} %get-tuple-element.64), channel_id=1, source_target_pairs={{0,24},{8,16},{16,40},{24,32},{32,56},{40,48},{48,8},{56,0},{64,88... | collective-permute-start | bytes 786440 | tf_op jit(solution)/shard_map/ppermute | solution.py:367

commit v5 on v4

--- a/solution.py
+++ b/solution.py
@@ -320,33 +320,35 @@
     )(place, near, p2, x0, x1, x2, x3, *taps[:2])
 
 
-def finish_kernel(steps, place, intensity, same1, other1, same2, other2, part, *refs):
+def finish_kernel(steps, place, intensity, *refs):
+    count = len(steps)
+    blocks, part = refs[:count], refs[count]
     updated, jump, new_updated, new_jump, done = refs[-5:]
     y, core = place[1], place[2]
     copies = []
-    for i, (step, blocks) in enumerate(zip(steps, ((same1, other1), (same2, other2)))):
-        for j, block in enumerate(blocks):
-            at = CORES * i + j
-            plane = CORES * ring(y, step) + (1 - core if j else core)
-            new_jump[at] = block[...]
-            new_updated[at] = part[plane] + intensity[0] * block[...]
-            for k, (new, out) in enumerate(((new_jump, jump), (new_updated, updated))):
-                copy = pltpu.make_async_copy(new.at[at], out.at[plane], done.at[at, k])
-                copy.start()
-                copies.append(copy)
+    for at, ((step, flip), block) in enumerate(zip(steps, blocks)):
+        plane = CORES * ring(y, step) + (1 - core if flip else core)
+        new_jump[at] = block[...]
+        new_updated[at] = part[plane] + intensity[0] * block[...]
+        for k, (new, out) in enumerate(((new_jump, jump), (new_updated, updated))):
+            copy = pltpu.make_async_copy(new.at[at], out.at[plane], done.at[at, k])
+            copy.start()
+            copies.append(copy)
     for copy in copies:
         copy.wait()
 
 
 def finish_part(steps, place, intensity, blocks, part, results):
     planes, rows, cols = part.shape
+    count = len(steps)
     anywhere = pl.BlockSpec(memory_space=pl.ANY)
-    scratch = pltpu.VMEM((2 * CORES, rows, cols), jnp.float32)
+    scratch = pltpu.VMEM((count, rows, cols), jnp.float32)
     return pl.pallas_call(
         lambda *refs: finish_kernel(steps, *refs),
-        out_shape=[f32(*part.shape)] * 2, in_specs=[SMEM, SMEM] + [VMEM] * 5 + [anywhere] * len(results),
-        out_specs=[anywhere] * 2, scratch_shapes=[scratch, scratch, pltpu.SemaphoreType.DMA((2 * CORES, 2))],
-        input_output_aliases={7: 0, 8: 1} if results else {},
+        out_shape=[f32(*part.shape)] * 2,
+        in_specs=[SMEM, SMEM] + [VMEM] * (count + 1) + [anywhere] * len(results),
+        out_specs=[anywhere] * 2, scratch_shapes=[scratch, scratch, pltpu.SemaphoreType.DMA((count, 2))],
+        input_output_aliases={count + 3: 0, count + 4: 1} if results else {},
         compiler_params=params(8), name="finish",
     )(place, intensity, *blocks, part, *results)
 
@@ -398,7 +400,8 @@
     other = to_other_core(value)
     value, high_side, low_side = load_part(place, value)
 
-    s1, s3, p0, s2 = pieces_part((1, 3, 0, 2), place, value, other)
+    s1, s3 = pieces_part((1, 3), place, value, other)
+    p0, s2 = pieces_part((0, 2), after(place, s1), value, other)
     p1, p3, x0 = to_ring(s1, 1), to_ring(s3, 3), to_group(p0, 0)
     low, high = neighbours(after(low_side, p0), after(high_side, p0), "gy")
     within, col_hi, col_lo, _ = within_part(value, after(kernel_cols[None], s2))
@@ -418,8 +421,9 @@
     jump_cols, part = local_part(
         place, after(intensity, b0), diffusion, drift, cross, value, low, high, beside, edge, within, (col_hi, col_lo)
     )
-    results = finish_part((0, 2), place, intensity, (b0, o0, d2, o2), part, ())
-    updated, jump_rows = finish_part((1, 3), place, intensity, (d1, o1, d3, o3), part, results)
+    results = finish_part(((0, 0), (0, 1), (2, 0), (2, 1)), place, intensity, (b0, o0, d2, o2), part, ())
+    results = finish_part(((1, 0), (3, 0)), place, intensity, (d1, d3), part, results)
+    updated, jump_rows = finish_part(((1, 1), (3, 1)), place, intensity, (o1, o3), part, results)
     return updated, jump_rows, jump_cols
 
 

time: 77.1 us -> 75.7 us (0.982)
  the two profiles are of different devices: /device:TPU:2 before, /device:TPU:99 now
where the time goes in v5:
time: 75.7 us; the launch traced here: 74.2 us
  starting transfers between devices  41.2 us (54%)
  Pallas kernels  21.8 us (29%)
  waiting for transfers between devices  7.78 us (10%)
  between operations  1.72 us (2%)
  local copies, waits for them, and re-layouts  1.61 us (2%)
    ppermute x16, starting transfers between devices, send(): return lax.ppermute(block, 'gx', route)  29.9 us
    ppermute x16, waiting for transfers between devices, send(): return lax.ppermute(block, 'gx', route)  5.86 us
    pallas_call x3, Pallas kernels, finish_part(): pl.pallas_call(lambda *refs: finish_kernel(steps, *refs), out_shape=[f32(...  5.06 us
    ppermute x1, starting transfers between devices, neighbours(): lax.ppermute(high_side, axis, forward)  4.76 us
    pallas_call x1, Pallas kernels, local_part(): pl.pallas_call(local_kernel, out_shape=(f32(*value.shape),) * 2, in_specs...  4.74 us
    ppermute x1, starting transfers between devices, across_chips(): return lax.ppermute(line, 'gx', route)  4.63 us
    pallas_call x1, Pallas kernels, others_part(): pl.pallas_call(others_kernel, out_shape=[f32(rows // RING // CORES, cols)...  2.8 us
    pallas_call x1, Pallas kernels, near_part(): pl.pallas_call(near_kernel, out_shape=f32(RING * size, cols), in_specs=[S...  2.66 us
  transfers between devices with their start and end apart: 19, of which 5 were waited for; matrix products, arithmetic and copies ran while one was open for 0% of the time, Pallas kernels for 26%

profile of v5, /device:TPU:99, one launch (start us, length us, event | category | flops | bytes accessed | tf_op | source)
XLA Modules:
  0.0 74.2 jit_solution(6153933516519650762)
XLA Ops:
  0.6 0.8 %collective-permute-start = (f32[8,64,1024]{2,1,0:T(8,128)}, f32[8,64,1024]{2,1,0:T(8,128)S(1)}, u32[]{:S(2)}, u32[]{:S(2)}) collective-permute-start(f32[8,64,1024]{2,1,0:T(8,128)} %value.1), channel_id=1, source_target_pairs={{0,8},{8,0},{16,24},{24,16},{32,40},{40,32},{48,56},{56,48},{64,72... | collective-permute-start | bytes 6291464 | tf_op jit(solution)/shard_map/ppermute | solution.py:369
  1.4 0.1 pad_add_fusion.place.refs_0_
  1.5 0.0 copy-start
  1.5 1.6 %copy-done = f32[8,64,1024]{2,1,0:T(8,128)S(1)} copy-done((f32[8,64,1024]{2,1,0:T(8,128)S(1)}, f32[8,64,1024]{2,1,0:T(8,128)}, u32[]{:S(2)}) %copy-start) | copy-done | bytes 2097176
  3.1 0.8 %load.1 = (f32[8,64,1024]{2,1,0:T(8,128)S(1)}, f32[8,64,256]{2,1,0:T(8,128)S(1)}, f32[8,64,256]{2,1,0:T(8,128)S(1)}) custom-call(s32[3]{0:T(128)S(1)} %pad_add_fusion.place.refs_0_, f32[8,64,1024]{2,1,0:T(8,128)S(1)} %copy-done), custom_call_target="tpu_custom_call" | custom-call | tf_op jit(solution)/shard_map/load/pallas_call | solution.py:189
  3.8 1.5 %collective-permute-done.refs_2_ = f32[8,64,1024]{2,1,0:T(8,128)S(1)} collective-permute-done((f32[8,64,1024]{2,1,0:T(8,128)}, f32[8,64,1024]{2,1,0:T(8,128)S(1)}, u32[]{:S(2)}, u32[]{:S(2)}) %collective-permute-start) | collective-permute-done | bytes 2097184 | tf_op jit(solution)/shard_map/ppermute | solution.py:369
  5.4 0.7 pieces.2
  6.1 1.4 %collective-permute-start.1 = (f32[128,1024]{1,0:T(8,128)S(1)}, f32[128,1024]{1,0:T(8,128)S(1)}, u32[]{:S(2)}, u32[]{:S(2)}) collective-permute-start(f32[128,1024]{1,0:T(8,128)S(1)} %get-tuple-element.45), channel_id=1, source_target_pairs={{0,16},{8,24},{16,32},{24,40},{32,48},{40,56},{48,0},{56,8},{64,80... | collective-permute-start | bytes 1572872 | tf_op jit(solution)/shard_map/ppermute | solution.py:369
  7.4 0.0 copy-start.2
  7.4 1.5 %collective-permute-start.5 = (f32[128,1024]{1,0:T(8,128)S(1)}, f32[128,1024]{1,0:T(8,128)S(1)}, u32[]{:S(2)}, u32[]{:S(2)}) collective-permute-start(f32[128,1024]{1,0:T(8,128)S(1)} %get-tuple-element.55), channel_id=1, source_target_pairs={{0,48},{8,56},{16,0},{24,8},{32,16},{40,24},{48,32},{56,40},{64,11... | collective-permute-start | bytes 1572872 | tf_op jit(solution)/shard_map/ppermute | solution.py:369
  9.0 0.7 pieces.3
  9.7 0.0 copy-start.3
  9.7 1.9 %collective-permute-start.3 = (f32[8,64,256]{2,1,0:T(8,128)S(1)}, f32[8,64,256]{2,1,0:T(8,128)S(1)}, u32[]{:S(2)}, u32[]{:S(2)}) collective-permute-start(f32[8,64,256]{2,1,0:T(8,128)S(1)} %get-tuple-element.52), channel_id=1, source_target_pairs={{1,0},{2,1},{3,2},{4,3},{5,4},{6,5},{7,6},{9,8},{10,9},{11,10},{12... | collective-permute-start | bytes 1572872 | tf_op jit(solution)/shard_map/ppermute | solution.py:360
  11.6 2.2 %collective-permute-start.4 = (f32[128,1024]{1,0:T(8,128)S(1)}, f32[128,1024]{1,0:T(8,128)S(1)}, u32[]{:S(2)}, u32[]{:S(2)}) collective-permute-start(f32[128,1024]{1,0:T(8,128)S(1)} %get-tuple-element.49.p0), channel_id=1, source_target_pairs={{32,96},{40,104},{48,112},{56,120},{64,0},{72,8},{80,16},{88,24},{... | collective-permute-start | bytes 1572872 | tf_op jit(solution)/shard_map/ppermute | solution.py:369
  13.8 0.0 copy-done.2
  13.8 2.4 %own_columns.1 = (f32[8,64,1024]{2,1,0:T(8,128)S(1)}, bf16[256,768]{1,0:T(8,128)(2,1)S(1)}, bf16[256,768]{1,0:T(8,128)(2,1)S(1)}, f32[8,128]{1,0:T(8,128)}) custom-call(f32[8,64,1024]{2,1,0:T(8,128)S(1)} %get-tuple-element.44.refs_1_.value, f32[1,511]{1,0:T(1,128)S(1)} %bitcast.5), custom_call_target="tpu_custom_call" | custom-call | tf_op jit(solution)/shard_map/own_columns/pallas_call | solution.py:76
  16.2 4.8 %collective-permute-start.2 = (f32[8,64,256]{2,1,0:T(8,128)S(1)}, f32[8,64,256]{2,1,0:T(8,128)S(1)}, u32[]{:S(2)}, u32[]{:S(2)}) collective-permute-start(f32[8,64,256]{2,1,0:T(8,128)S(1)} %get-tuple-element.50), channel_id=1, source_target_pairs={{0,1},{1,2},{2,3},{3,4},{4,5},{5,6},{6,7},{8,9},{9,10},{10,11},{11... | collective-permute-start | bytes 1572872 | tf_op jit(solution)/shard_map/ppermute | solution.py:360
  20.9 0.0 copy-done.3
  21.0 0.2 row_taps.1
  21.2 0.0 collective-permute-done.1.p1
  21.2 0.0 collective-permute-done.5.p3
  21.2 2.6 %collective-permute-start.6 = (f32[128,1024]{1,0:T(8,128)S(1)}, f32[128,1024]{1,0:T(8,128)S(1)}, u32[]{:S(2)}, u32[]{:S(2)}) collective-permute-start(f32[128,1024]{1,0:T(8,128)S(1)} %get-tuple-element.63), channel_id=1, source_target_pairs={{0,32},{8,40},{16,48},{24,56},{32,0},{40,8},{48,16},{56,24},{64,96... | collective-permute-start | bytes 1572872 | tf_op jit(solution)/shard_map/ppermute | solution.py:369
  23.8 2.8 %collective-permute-start.7 = (f32[128,1024]{1,0:T(8,128)S(1)}, f32[128,1024]{1,0:T(8,128)S(1)}, u32[]{:S(2)}, u32[]{:S(2)}) collective-permute-start(f32[128,1024]{1,0:T(8,128)S(1)} %collective-permute-done.1.p1), channel_id=1, source_target_pairs={{0,64},{8,72},{48,112},{56,120},{64,128},{72,136},{80,16},{88,24},... | collective-permute-start | bytes 1572872 | tf_op jit(solution)/shard_map/ppermute | solution.py:369
  26.6 0.0 collective-permute-done.3.high
  26.6 2.5 %collective-permute-start.9 = (f32[128,1024]{1,0:T(8,128)S(1)}, f32[128,1024]{1,0:T(8,128)S(1)}, u32[]{:S(2)}, u32[]{:S(2)}) collective-permute-start(f32[128,1024]{1,0:T(8,128)S(1)} %collective-permute-done.5.p3), channel_id=1, source_target_pairs={{16,80},{24,88},{32,96},{40,104},{64,0},{72,8},{80,144},{88,152},{... | collective-permute-start | bytes 1572872 | tf_op jit(solution)/shard_map/ppermute | solution.py:369
  29.1 1.9 %collective-permute-done.2.low = f32[8,64,256]{2,1,0:T(8,128)S(1)} collective-permute-done((f32[8,64,256]{2,1,0:T(8,128)S(1)}, f32[8,64,256]{2,1,0:T(8,128)S(1)}, u32[]{:S(2)}, u32[]{:S(2)}) %collective-permute-start.2) | collective-permute-done | bytes 524320 | tf_op jit(solution)/shard_map/ppermute | solution.py:360
  31.0 0.6 lines.1
  31.6 0.0 collective-permute-done.4.x0
  31.6 2.7 %near_rows.1.near = f32[512,1024]{1,0:T(8,128)S(1)} custom-call(s32[3]{0:T(128)S(1)} %pad_add_fusion.place.refs_0_, f32[128,1024]{1,0:T(8,128)S(1)} %get-tuple-element.49.p0, f32[128,1024]{1,0:T(8,128)S(1)} %collective-permute-done.1.p1, f32[128,1024]{1,0:T(8,128)S(1)} %collective-permute-done.5.p3, bf16[256,768]{1,0:T(8,128)(2,1)S(1)} %get-tuple-element.60.taps_hi, ...), custom_call_target="tpu_custom_call" | custom-call | tf_op jit(solution)/shard_map/near_rows/pallas_call | solution.py:248
  34.3 0.5 collective-permute-done.6.p2
  34.7 3.1 %collective-permute-start.8 = (f32[128,1024]{1,0:T(8,128)S(1)}, f32[128,1024]{1,0:T(8,128)S(1)}, u32[]{:S(2)}, u32[]{:S(2)}) collective-permute-start(f32[128,1024]{1,0:T(8,128)S(1)} %collective-permute-done.6.p2), channel_id=1, source_target_pairs={{0,64},{8,72},{16,80},{24,88},{64,128},{72,136},{80,144},{88,152},... | collective-permute-start | bytes 1572872 | tf_op jit(solution)/shard_map/ppermute | solution.py:369
  37.9 0.0 collective-permute-done.7.x1
  37.9 1.9 %collective-permute-done.9.x3 = f32[128,1024]{1,0:T(8,128)S(1)} collective-permute-done((f32[128,1024]{1,0:T(8,128)S(1)}, f32[128,1024]{1,0:T(8,128)S(1)}, u32[]{:S(2)}, u32[]{:S(2)}) %collective-permute-start.9) | collective-permute-done | bytes 524320 | tf_op jit(solution)/shard_map/ppermute | solution.py:369
  39.8 1.3 %opposite_rows.1 = (f32[64,1024]{1,0:T(8,128)S(1)}, f32[64,1024]{1,0:T(8,128)S(1)}) custom-call(s32[3]{0:T(128)S(1)} %pad_add_fusion.place.refs_0_, f32[512,1024]{1,0:T(8,128)S(1)} %near_rows.1.near, f32[128,1024]{1,0:T(8,128)S(1)} %collective-permute-done.6.p2, f32[128,1024]{1,0:T(8,128)S(1)} %collective-permute-done.4.x0, ...), custom_call_target="tpu_custom_call" | custom-call | tf_op jit(solution)/shard_map/opposite_rows/pallas_call | solution.py:283
  41.1 1.2 %collective-permute-start.17 = (f32[64,1024]{1,0:T(8,128)S(1)}, f32[64,1024]{1,0:T(8,128)S(1)}, u32[]{:S(2)}, u32[]{:S(2)}) collective-permute-start(f32[64,1024]{1,0:T(8,128)S(1)} %get-tuple-element.76), channel_id=1, source_target_pairs={{0,32},{8,40},{16,48},{24,56},{32,0},{40,8},{48,16},{56,24},{64,96... | collective-permute-start | bytes 786440 | tf_op jit(solution)/shard_map/ppermute | solution.py:369
  42.3 5.1 %collective-permute-start.18 = (f32[64,1024]{1,0:T(8,128)S(1)}, f32[64,1024]{1,0:T(8,128)S(1)}, u32[]{:S(2)}, u32[]{:S(2)}) collective-permute-start(f32[64,1024]{1,0:T(8,128)S(1)} %get-tuple-element.77), channel_id=1, source_target_pairs={{0,40},{8,32},{16,56},{24,48},{32,8},{40,0},{48,24},{56,16},{64,10... | collective-permute-start | bytes 786440 | tf_op jit(solution)/shard_map/ppermute | solution.py:369
  47.4 0.0 copy-start.1
  47.4 0.0 copy-start.4
  47.4 0.0 copy-start.5
  47.4 0.0 collective-permute-start.12
  47.4 4.6 %collective-permute-start.13 = (f32[8,1280]{1,0:T(8,128)S(1)}, f32[8,1280]{1,0:T(8,128)S(1)}, u32[]{:S(2)}, u32[]{:S(2)}) collective-permute-start(f32[8,1280]{1,0:T(8,128)S(1)} %get-tuple-element.53), channel_id=1, source_target_pairs={{8,16},{16,8},{24,32},{32,24},{40,48},{48,40},{56,64},{64,56},{72,... | collective-permute-start | bytes 122888 | tf_op jit(solution)/shard_map/ppermute | solution.py:383
  52.0 0.0 collective-permute-done.8.x2
  52.0 2.8 %other_rows.1 = (f32[64,1024]{1,0:T(8,128)S(1)}, f32[64,1024]{1,0:T(8,128)S(1)}, f32[64,1024]{1,0:T(8,128)S(1)}, f32[64,1024]{1,0:T(8,128)S(1)}, f32[64,1024]{1,0:T(8,128)S(1)}, /*index=5*/f32[64,1024]{1,0:T(8,128)S(1)}) custom-call(s32[3]{0:T(128)S(1)} %pad_add_fusion.place.refs_0_, f32[512,1024]{1,0:T(8,128)S(1)} %near_rows.1.near, ...), custom_call_target="tpu_custom_call" | custom-call | tf_op jit(solution)/shard_map/other_rows/pallas_call | solution.py:317
  54.8 0.3 collective-permute-start.16
  55.1 0.0 collective-permute-done.12.beside
  55.1 2.5 %collective-permute-start.14 = (f32[64,1024]{1,0:T(8,128)S(1)}, f32[64,1024]{1,0:T(8,128)S(1)}, u32[]{:S(2)}, u32[]{:S(2)}) collective-permute-start(f32[64,1024]{1,0:T(8,128)S(1)} %get-tuple-element.73), channel_id=1, source_target_pairs={{0,48},{8,56},{16,0},{24,8},{32,16},{40,24},{48,32},{56,40},{64,11... | collective-permute-start | bytes 786440 | tf_op jit(solution)/shard_map/ppermute | solution.py:369
  57.6 0.0 collective-permute-done.13.edge
  57.6 2.2 %collective-permute-start.15 = (f32[64,1024]{1,0:T(8,128)S(1)}, f32[64,1024]{1,0:T(8,128)S(1)}, u32[]{:S(2)}, u32[]{:S(2)}) collective-permute-start(f32[64,1024]{1,0:T(8,128)S(1)} %get-tuple-element.74), channel_id=1, source_target_pairs={{0,16},{8,24},{16,32},{24,40},{32,48},{40,56},{48,0},{56,8},{64,80... | collective-permute-start | bytes 786440 | tf_op jit(solution)/shard_map/ppermute | solution.py:369
  59.8 0.0 collective-permute-done.17.refs_4_
  59.8 1.0 %collective-permute-start.10 = (f32[64,1024]{1,0:T(8,128)S(1)}, f32[64,1024]{1,0:T(8,128)S(1)}, u32[]{:S(2)}, u32[]{:S(2)}) collective-permute-start(f32[64,1024]{1,0:T(8,128)S(1)} %get-tuple-element.65), channel_id=1, source_target_pairs={{0,56},{8,48},{16,8},{24,0},{32,24},{40,16},{48,40},{56,32},{64,12... | collective-permute-start | bytes 786440 | tf_op jit(solution)/shard_map/ppermute | solution.py:369
  60.8 0.0 collective-permute-done.18.refs_5_
  60.8 0.8 %collective-permute-start.11 = (f32[64,1024]{1,0:T(8,128)S(1)}, f32[64,1024]{1,0:T(8,128)S(1)}, u32[]{:S(2)}, u32[]{:S(2)}) collective-permute-start(f32[64,1024]{1,0:T(8,128)S(1)} %get-tuple-element.66), channel_id=1, source_target_pairs={{0,24},{8,16},{16,40},{24,32},{32,56},{40,48},{48,8},{56,0},{64,88... | collective-permute-start | bytes 786440 | tf_op jit(solution)/shard_map/ppermute | solution.py:369
  62.2 0.0 copy-done.1
  62.3 0.0 copy-done.4
  62.3 0.0 copy-done.5
  62.3 4.7 %side_columns_and_stencil.1 = (f32[8,64,1024]{2,1,0:T(8,128)}, f32[8,64,1024]{2,1,0:T(8,128)S(1)}) custom-call(s32[3]{0:T(128)S(1)} %pad_add_fusion.place.refs_0_, f32[2]{0:T(128)S(1)} %copy-done.1, f32[3]{0:T(128)S(1)} %copy-done.4, f32[3]{0:T(128)S(1)} %copy-done.5, f32[1]{0:T(128)S(6)} %copy.18.cross, f32[8,64,1024]{2,1,0:T(8,128)S(1)} %get-tuple-element.44.refs_1_.value, ...), custom_call_target="tpu_custom_call" | custom-call | tf_op jit(solution)/shard_map/side_columns_and_stencil/pallas_call | solution.py:137
  67.0 0.0 collective-permute-done.16.refs_3_
  67.0 1.9 %finish.3 = (f32[8,64,1024]{2,1,0:T(8,128)}, f32[8,64,1024]{2,1,0:T(8,128)}) custom-call(s32[3]{0:T(128)S(1)} %pad_add_fusion.place.refs_0_, f32[2]{0:T(128)S(1)} %copy-done.1, f32[64,1024]{1,0:T(8,128)S(1)} %get-tuple-element.67.refs_2_, f32[64,1024]{1,0:T(8,128)S(1)} %collective-permute-done.16.refs_3_, f32[64,1024]{1,0:T(8,128)S(1)} %collective-permute-done.17.refs_4_, ...), custom_call_target="tpu_custom_call" | custom-call | tf_op jit(solution)/shard_map/finish/pallas_call | solution.py:346
  69.0 0.0 collective-permute-done.14.refs_2_
  69.0 0.0 collective-permute-done.15.refs_3_
  69.0 1.6 %finish.4 = (f32[8,64,1024]{2,1,0:T(8,128)}, f32[8,64,1024]{2,1,0:T(8,128)}) custom-call(s32[3]{0:T(128)S(1)} %pad_add_fusion.place.refs_0_, f32[2]{0:T(128)S(1)} %copy-done.1, f32[64,1024]{1,0:T(8,128)S(1)} %collective-permute-done.14.refs_2_, f32[64,1024]{1,0:T(8,128)S(1)} %collective-permute-done.15.refs_3_, ...), custom_call_target="tpu_custom_call", output_to_operand_aliasing={{0}: (5, {}), {1}: (6, {})} | custom-call | tf_op jit(solution)/shard_map/finish/pallas_call | solution.py:346
  70.6 0.0 collective-permute-done.10.refs_2_
  70.6 1.9 %collective-permute-done.11.refs_3_ = f32[64,1024]{1,0:T(8,128)S(1)} collective-permute-done((f32[64,1024]{1,0:T(8,128)S(1)}, f32[64,1024]{1,0:T(8,128)S(1)}, u32[]{:S(2)}, u32[]{:S(2)}) %collective-permute-start.11) | collective-permute-done | bytes 262176 | tf_op jit(solution)/shard_map/ppermute | solution.py:369
  72.5 1.6 %finish.5 = (f32[8,64,1024]{2,1,0:T(8,128)}, f32[8,64,1024]{2,1,0:T(8,128)}) custom-call(s32[3]{0:T(128)S(1)} %pad_add_fusion.place.refs_0_, f32[2]{0:T(128)S(1)} %copy-done.1, f32[64,1024]{1,0:T(8,128)S(1)} %collective-permute-done.10.refs_2_, f32[64,1024]{1,0:T(8,128)S(1)} %collective-permute-done.11.refs_3_, ...), custom_call_target="tpu_custom_call", output_to_operand_aliasing={{0}: (5, {}), {1}: (6, {})} | custom-call | tf_op jit(solution)/shard_map/finish/pallas_call | solution.py:346
Async XLA Ops:
  0.6 4.8 %collective-permute-start = (f32[8,64,1024]{2,1,0:T(8,128)}, f32[8,64,1024]{2,1,0:T(8,128)S(1)}, u32[]{:S(2)}, u32[]{:S(2)}) collective-permute-start(f32[8,64,1024]{2,1,0:T(8,128)} %value.1), channel_id=1, source_target_pairs={{0,8},{8,0},{16,24},{24,16},{32,40},{40,32},{48,56},{56,48},{64,72... | collective-permute-start | bytes 6291464 | tf_op jit(solution)/shard_map/ppermute | solution.py:369
  1.5 1.6 %copy-start = (f32[8,64,1024]{2,1,0:T(8,128)S(1)}, f32[8,64,1024]{2,1,0:T(8,128)}, u32[]{:S(2)}) copy-start(f32[8,64,1024]{2,1,0:T(8,128)} %value.1) | copy-start | bytes 6291460
  6.1 15.1 %collective-permute-start.1 = (f32[128,1024]{1,0:T(8,128)S(1)}, f32[128,1024]{1,0:T(8,128)S(1)}, u32[]{:S(2)}, u32[]{:S(2)}) collective-permute-start(f32[128,1024]{1,0:T(8,128)S(1)} %get-tuple-element.45), channel_id=1, source_target_pairs={{0,16},{8,24},{16,32},{24,40},{32,48},{40,56},{48,0},{56,8},{64,80... | collective-permute-start | bytes 1572872 | tf_op jit(solution)/shard_map/ppermute | solution.py:369
  7.4 6.3 %copy-start.2 = (f32[511]{0:T(512)S(1)}, f32[511]{0:T(512)}, u32[]{:S(2)}) copy-start(f32[511]{0:T(512)} %param.9) | copy-start | bytes 6136
  7.4 13.7 %collective-permute-start.5 = (f32[128,1024]{1,0:T(8,128)S(1)}, f32[128,1024]{1,0:T(8,128)S(1)}, u32[]{:S(2)}, u32[]{:S(2)}) collective-permute-start(f32[128,1024]{1,0:T(8,128)S(1)} %get-tuple-element.55), channel_id=1, source_target_pairs={{0,48},{8,56},{16,0},{24,8},{32,16},{40,24},{48,32},{56,40},{64,11... | collective-permute-start | bytes 1572872 | tf_op jit(solution)/shard_map/ppermute | solution.py:369
  9.7 11.3 %copy-start.3 = (f32[511]{0:T(512)S(1)}, f32[511]{0:T(512)}, u32[]{:S(2)}) copy-start(f32[511]{0:T(512)} %param.8) | copy-start | bytes 6136
  9.7 16.9 %collective-permute-start.3 = (f32[8,64,256]{2,1,0:T(8,128)S(1)}, f32[8,64,256]{2,1,0:T(8,128)S(1)}, u32[]{:S(2)}, u32[]{:S(2)}) collective-permute-start(f32[8,64,256]{2,1,0:T(8,128)S(1)} %get-tuple-element.52), channel_id=1, source_target_pairs={{1,0},{2,1},{3,2},{4,3},{5,4},{6,5},{7,6},{9,8},{10,9},{11,10},{12... | collective-permute-start | bytes 1572872 | tf_op jit(solution)/shard_map/ppermute | solution.py:360
  11.6 20.0 %collective-permute-start.4 = (f32[128,1024]{1,0:T(8,128)S(1)}, f32[128,1024]{1,0:T(8,128)S(1)}, u32[]{:S(2)}, u32[]{:S(2)}) collective-permute-start(f32[128,1024]{1,0:T(8,128)S(1)} %get-tuple-element.49.p0), channel_id=1, source_target_pairs={{32,96},{40,104},{48,112},{56,120},{64,0},{72,8},{80,16},{88,24},{... | collective-permute-start | bytes 1572872 | tf_op jit(solution)/shard_map/ppermute | solution.py:369
  16.2 14.8 %collective-permute-start.2 = (f32[8,64,256]{2,1,0:T(8,128)S(1)}, f32[8,64,256]{2,1,0:T(8,128)S(1)}, u32[]{:S(2)}, u32[]{:S(2)}) collective-permute-start(f32[8,64,256]{2,1,0:T(8,128)S(1)} %get-tuple-element.50), channel_id=1, source_target_pairs={{0,1},{1,2},{2,3},{3,4},{4,5},{5,6},{6,7},{8,9},{9,10},{10,11},{11... | collective-permute-start | bytes 1572872 | tf_op jit(solution)/shard_map/ppermute | solution.py:360
  21.2 13.6 %collective-permute-start.6 = (f32[128,1024]{1,0:T(8,128)S(1)}, f32[128,1024]{1,0:T(8,128)S(1)}, u32[]{:S(2)}, u32[]{:S(2)}) collective-permute-start(f32[128,1024]{1,0:T(8,128)S(1)} %get-tuple-element.63), channel_id=1, source_target_pairs={{0,32},{8,40},{16,48},{24,56},{32,0},{40,8},{48,16},{56,24},{64,96... | collective-permute-start | bytes 1572872 | tf_op jit(solution)/shard_map/ppermute | solution.py:369
  23.8 14.1 %collective-permute-start.7 = (f32[128,1024]{1,0:T(8,128)S(1)}, f32[128,1024]{1,0:T(8,128)S(1)}, u32[]{:S(2)}, u32[]{:S(2)}) collective-permute-start(f32[128,1024]{1,0:T(8,128)S(1)} %collective-permute-done.1.p1), channel_id=1, source_target_pairs={{0,64},{8,72},{48,112},{56,120},{64,128},{72,136},{80,16},{88,24},... | collective-permute-start | bytes 1572872 | tf_op jit(solution)/shard_map/ppermute | solution.py:369
  26.6 13.2 %collective-permute-start.9 = (f32[128,1024]{1,0:T(8,128)S(1)}, f32[128,1024]{1,0:T(8,128)S(1)}, u32[]{:S(2)}, u32[]{:S(2)}) collective-permute-start(f32[128,1024]{1,0:T(8,128)S(1)} %collective-permute-done.5.p3), channel_id=1, source_target_pairs={{16,80},{24,88},{32,96},{40,104},{64,0},{72,8},{80,144},{88,152},{... | collective-permute-start | bytes 1572872 | tf_op jit(solution)/shard_map/ppermute | solution.py:369
  34.7 17.3 %collective-permute-start.8 = (f32[128,1024]{1,0:T(8,128)S(1)}, f32[128,1024]{1,0:T(8,128)S(1)}, u32[]{:S(2)}, u32[]{:S(2)}) collective-permute-start(f32[128,1024]{1,0:T(8,128)S(1)} %collective-permute-done.6.p2), channel_id=1, source_target_pairs={{0,64},{8,72},{16,80},{24,88},{64,128},{72,136},{80,144},{88,152},... | collective-permute-start | bytes 1572872 | tf_op jit(solution)/shard_map/ppermute | solution.py:369
  41.1 18.8 %collective-permute-start.17 = (f32[64,1024]{1,0:T(8,128)S(1)}, f32[64,1024]{1,0:T(8,128)S(1)}, u32[]{:S(2)}, u32[]{:S(2)}) collective-permute-start(f32[64,1024]{1,0:T(8,128)S(1)} %get-tuple-element.76), channel_id=1, source_target_pairs={{0,32},{8,40},{16,48},{24,56},{32,0},{40,8},{48,16},{56,24},{64,96... | collective-permute-start | bytes 786440 | tf_op jit(solution)/shard_map/ppermute | solution.py:369
  42.3 18.5 %collective-permute-start.18 = (f32[64,1024]{1,0:T(8,128)S(1)}, f32[64,1024]{1,0:T(8,128)S(1)}, u32[]{:S(2)}, u32[]{:S(2)}) collective-permute-start(f32[64,1024]{1,0:T(8,128)S(1)} %get-tuple-element.77), channel_id=1, source_target_pairs={{0,40},{8,32},{16,56},{24,48},{32,8},{40,0},{48,24},{56,16},{64,10... | collective-permute-start | bytes 786440 | tf_op jit(solution)/shard_map/ppermute | solution.py:369
  47.4 14.9 %copy-start.1 = (f32[2]{0:T(128)S(1)}, f32[2]{0:T(128)}, u32[]{:S(2)}) copy-start(f32[2]{0:T(128)} %refs_1_.5) | copy-start | bytes 28
  47.4 14.9 %copy-start.4 = (f32[3]{0:T(128)S(1)}, f32[3]{0:T(128)}, u32[]{:S(2)}) copy-start(f32[3]{0:T(128)} %diffusion.1) | copy-start | bytes 40
  47.4 14.9 %copy-start.5 = (f32[3]{0:T(128)S(1)}, f32[3]{0:T(128)}, u32[]{:S(2)}) copy-start(f32[3]{0:T(128)} %drift.1) | copy-start | bytes 40
  47.4 7.7 %collective-permute-start.12 = (f32[8,1280]{1,0:T(8,128)S(1)}, f32[8,1280]{1,0:T(8,128)S(1)}, u32[]{:S(2)}, u32[]{:S(2)}) collective-permute-start(f32[8,1280]{1,0:T(8,128)S(1)} %get-tuple-element.69), channel_id=1, source_target_pairs={{0,8},{8,0},{16,24},{24,16},{32,40},{40,32},{48,56},{56,48},{64,72... | collective-permute-start | bytes 122888 | tf_op jit(solution)/shard_map/ppermute | solution.py:369
  47.4 10.2 %collective-permute-start.13 = (f32[8,1280]{1,0:T(8,128)S(1)}, f32[8,1280]{1,0:T(8,128)S(1)}, u32[]{:S(2)}, u32[]{:S(2)}) collective-permute-start(f32[8,1280]{1,0:T(8,128)S(1)} %get-tuple-element.53), channel_id=1, source_target_pairs={{8,16},{16,8},{24,32},{32,24},{40,48},{48,40},{56,64},{64,56},{72,... | collective-permute-start | bytes 122888 | tf_op jit(solution)/shard_map/ppermute | solution.py:383
  54.8 12.2 %collective-permute-start.16 = (f32[64,1024]{1,0:T(8,128)S(1)}, f32[64,1024]{1,0:T(8,128)S(1)}, u32[]{:S(2)}, u32[]{:S(2)}) collective-permute-start(f32[64,1024]{1,0:T(8,128)S(1)} %get-tuple-element.75), channel_id=1, source_target_pairs={{0,8},{8,0},{16,24},{24,16},{32,40},{40,32},{48,56},{56,48},{64,72... | collective-permute-start | bytes 786440 | tf_op jit(solution)/shard_map/ppermute | solution.py:369
  55.1 13.8 %collective-permute-start.14 = (f32[64,1024]{1,0:T(8,128)S(1)}, f32[64,1024]{1,0:T(8,128)S(1)}, u32[]{:S(2)}, u32[]{:S(2)}) collective-permute-start(f32[64,1024]{1,0:T(8,128)S(1)} %get-tuple-element.73), channel_id=1, source_target_pairs={{0,48},{8,56},{16,0},{24,8},{32,16},{40,24},{48,32},{56,40},{64,11... | collective-permute-start | bytes 786440 | tf_op jit(solution)/shard_map/ppermute | solution.py:369
  57.6 11.3 %collective-permute-start.15 = (f32[64,1024]{1,0:T(8,128)S(1)}, f32[64,1024]{1,0:T(8,128)S(1)}, u32[]{:S(2)}, u32[]{:S(2)}) collective-permute-start(f32[64,1024]{1,0:T(8,128)S(1)} %get-tuple-element.74), channel_id=1, source_target_pairs={{0,16},{8,24},{16,32},{24,40},{32,48},{40,56},{48,0},{56,8},{64,80... | collective-permute-start | bytes 786440 | tf_op jit(solution)/shard_map/ppermute | solution.py:369
  59.8 10.7 %collective-permute-start.10 = (f32[64,1024]{1,0:T(8,128)S(1)}, f32[64,1024]{1,0:T(8,128)S(1)}, u32[]{:S(2)}, u32[]{:S(2)}) collective-permute-start(f32[64,1024]{1,0:T(8,128)S(1)} %get-tuple-element.65), channel_id=1, source_target_pairs={{0,56},{8,48},{16,8},{24,0},{32,24},{40,16},{48,40},{56,32},{64,12... | collective-permute-start | bytes 786440 | tf_op jit(solution)/shard_map/ppermute | solution.py:369
  60.8 11.6 %collective-permute-start.11 = (f32[64,1024]{1,0:T(8,128)S(1)}, f32[64,1024]{1,0:T(8,128)S(1)}, u32[]{:S(2)}, u32[]{:S(2)}) collective-permute-start(f32[64,1024]{1,0:T(8,128)S(1)} %get-tuple-element.66), channel_id=1, source_target_pairs={{0,24},{8,16},{16,40},{24,32},{32,56},{40,48},{48,8},{56,0},{64,88... | collective-permute-start | bytes 786440 | tf_op jit(solution)/shard_map/ppermute | solution.py:369
